TPU v7x, 32 devices: a whole 2x2x4 slice. The times are simulated.
32 devices in a mesh: groups: 2 (over x), node: 16 (over z, y, core).
Axes of the slice: x: 2, y: 2, z: 4, core: 2. Of those that a mesh axis runs over, the one named last changes fastest.
Arguments:
- tokens: bfloat16 [2048, 4096], P(('groups', 'node')), parts along dimension 0, may hold values from -6 to 6
- routes: int32 [2048, 8], P(('groups', 'node')), parts along dimension 0, may hold values from 0 to 15, all different within a row; in each aligned block of 64 rows (0 to 63, 64 to 127, ...) at most 48 rows name the same one
- gate_codes: int32 [2048, 8], P(('groups', 'node')), parts along dimension 0, may hold values from 1 to 255
- w_gate: bfloat16 [16, 4096, 768], P('node'), may hold values from -0.09375 to 0.09375
- w_up: bfloat16 [16, 4096, 768], P('node'), may hold values from -0.09375 to 0.09375
- w_down: bfloat16 [16, 768, 4096], P('node'), may hold values from -0.21875 to 0.21875
Outputs:
- mixed: bfloat16 [2048, 4096], P(('groups', 'node')), parts along dimension 0
There are 2 independent parts, one for each index of `groups`. A program takes and returns all parts, laid end to end along the dimension named above; an argument that names none is the same for every part. Nothing has to cross between parts.
Inputs may be any that keep to these rules, and one draw needn't show every extreme that they name: `routes`: each row names 8 different experts; among the rows of one device no expert is named by more than 48 rows, a bound that some block reaches.
All inputs are finite; a program needn't handle non-finite values.
Results may differ from a plain program's by a relative error of at most 0.015.
Values may be sent and summed in bfloat16 or wider, within the bound.
No kernel may reach another device: no remote copies, remote signals or barrier semaphores. Data moves between devices by JAX's collectives and lax.ppermute only.
A program may use at most 128 MiB of HBM per device.

v0:
```python
import jax
import jax.numpy as jnp
from jax import lax
from jax.sharding import PartitionSpec as P


def quantize(tokens):
    blocks = tokens.astype(jnp.float32).reshape(tokens.shape[0], -1, 128)
    largest = jnp.max(jnp.abs(blocks), axis=-1)
    row_scales = ((largest + 1e-06) / 448.0).astype(jnp.bfloat16)
    coded_rows = (blocks / row_scales.astype(jnp.float32)[..., None]).astype(jnp.bfloat16)
    return (coded_rows.reshape(tokens.shape[0], -1), row_scales)


def dequantize(coded_rows, row_scales):
    blocks = coded_rows.astype(jnp.float32).reshape(coded_rows.shape[0], -1, 128)
    joined = blocks * row_scales.astype(jnp.float32)[..., None]
    return joined.astype(jnp.bfloat16).reshape(coded_rows.shape[0], -1)


def expert_forward(inputs, gate_w, up_w, down_w):
    gate = jnp.dot(inputs, gate_w, preferred_element_type=jnp.float32)
    up = jnp.dot(inputs, up_w, preferred_element_type=jnp.float32)
    hidden = (jax.nn.silu(gate) * up).astype(jnp.bfloat16)
    return jnp.dot(hidden, down_w, preferred_element_type=jnp.float32).astype(jnp.bfloat16)


def local(tokens, routes, gate_codes, w_gate, w_up, w_down):
    tok_rows, model_width = tokens.shape
    top_k = routes.shape[1]
    node_count = lax.axis_size("node")
    mean_load = tok_rows * top_k // node_count
    slot_most = mean_load + mean_load // 2
    slot_total = node_count * slot_most
    scale_cols = model_width // 128
    coded_rows, row_scales = quantize(tokens)
    flat_routes = routes.reshape(-1)
    onehot = (flat_routes[:, None] == jnp.arange(node_count, dtype=jnp.int32)[None, :]).astype(
        jnp.int32
    )
    slot_rank = jnp.sum((jnp.cumsum(onehot, axis=0) - 1) * onehot, axis=1)
    dest_slot = flat_routes * slot_most + slot_rank
    owner_row = jnp.arange(tok_rows * top_k, dtype=jnp.int32) // top_k
    send_coded = (
        jnp.zeros((slot_total, model_width), jnp.bfloat16).at[dest_slot].set(coded_rows[owner_row])
    )
    send_scales = (
        jnp.zeros((slot_total, scale_cols), jnp.bfloat16).at[dest_slot].set(row_scales[owner_row])
    )
    recv_coded, recv_scales = (
        lax.all_to_all(
            send_coded.reshape(node_count, slot_most, model_width),
            "node",
            split_axis=0,
            concat_axis=0,
            tiled=True,
        ),
        lax.all_to_all(
            send_scales.reshape(node_count, slot_most, scale_cols),
            "node",
            split_axis=0,
            concat_axis=0,
            tiled=True,
        ),
    )
    recv_coded = recv_coded.reshape(slot_total, model_width)
    recv_scales = recv_scales.reshape(slot_total, scale_cols)
    dequant_rows = dequantize(recv_coded, recv_scales)
    gate_w = w_gate[0]
    up_w = w_up[0]
    down_w = w_down[0]
    expert_rows = expert_forward(dequant_rows, gate_w, up_w, down_w)
    returned = lax.all_to_all(
        expert_rows.reshape(node_count, slot_most, model_width),
        "node",
        split_axis=0,
        concat_axis=0,
        tiled=True,
    )
    returned = returned.reshape(slot_total, model_width)
    picked = returned[dest_slot].reshape(tok_rows, top_k, model_width).astype(jnp.float32)
    codes = gate_codes.astype(jnp.float32)
    weights = codes / jnp.sum(codes, axis=1, keepdims=True)
    return jnp.sum(picked * weights[:, :, None], axis=1).astype(jnp.bfloat16)


def solution(mesh):
    return jax.shard_map(
        local,
        mesh=mesh,
        in_specs=(
            P(("groups", "node"), None),
            P(("groups", "node"), None),
            P(("groups", "node"), None),
            P("node", None, None),
            P("node", None, None),
            P("node", None, None),
        ),
        out_specs=P(("groups", "node"), None),
        check_vma=False,
    )
```

profile of v0, /device:TPU:15, one launch (start us, length us, event | category | flops | bytes accessed | tf_op | source)
XLA Modules:
  0.0 372.6 jit_solution(11731331083964271727)
XLA Ops:
  0.0 0.0 copy-start
  0.0 0.8 copy.27
  0.8 0.1 eq.29
  0.9 0.1 eq.25
  1.0 0.7 broadcast_multiply_fusion
  1.7 1.2 reduce-window.6
  2.9 0.2 slice_reduce_fusion
  3.1 0.1 copy.26
  3.2 0.1 mul.56
  3.3 1.1 fusion.18
  4.5 0.2 copy.40
  4.7 0.3 reduce_max.9
  5.0 0.1 fusion.24
  5.1 3.0 scatter_custom_fusion.1
  8.2 0.1 copy.31
  8.3 0.8 reshape.217
  9.1 7.0 %all-to-all-start.1 = ((bf16[16,2,768]{2,1,0:T(2,128)(2,1)}), bf16[16,2,768]{2,1,0:T(2,128)(2,1)S(1)}, u32[]{:S(2)}, u32[]{:S(2)}) async-start(bf16[16,2,768]{2,1,0:T(2,128)(2,1)} %reshape.217), calls=%async_computation.1 | async-start | bytes 98304 | tf_op jit(solution)/shard_map/all_to_all | solution.py:58
  16.1 0.3 div.41
  16.5 0.0 copy-done
  16.5 0.7 fusion.19
  17.2 22.1 %scatter_custom_fusion = bf16[768,4096]{1,0:T(8,128)(2,1)} fusion(s32[512]{0:T(512)S(1)} %bitcast.72, bf16[64,4096]{1,0:T(8,128)(2,1)S(1)} %fusion.19, s32[1024]{0:T(1024)S(1)} %pad_clamp_fusion.1, bf16[]{:T(256)} %constant.19.clone.1), kind=kCustom, calls=%fused_computation.19 | custom fusion | bytes 6291458 | tf_op jit(solution)/shard_map/scatter | solution.py:45
  39.4 0.0 all-to-all-done.1
  39.4 6.4 %all-to-all-start = ((bf16[16,48,4096]{2,1,0:T(8,128)(2,1)}), bf16[16,48,4096]{2,1,0:T(8,128)(2,1)}, u32[]{:S(2)}, u32[]{:S(2)}) async-start(bf16[16,48,4096]{2,1,0:T(8,128)(2,1)} %bitcast.61), calls=%async_computation | async-start | bytes 12582912 | tf_op jit(solution)/shard_map/all_to_all | solution.py:51
  45.7 0.2 reshape.218
  45.9 0.1 copy.37
  46.0 137.0 %all-to-all-done = bf16[16,48,4096]{2,1,0:T(8,128)(2,1)} async-done(((bf16[16,48,4096]{2,1,0:T(8,128)(2,1)}), bf16[16,48,4096]{2,1,0:T(8,128)(2,1)}, u32[]{:S(2)}, u32[]{:S(2)}) %all-to-all-start) | async-done | bytes 6291488 | tf_op jit(solution)/shard_map/all_to_all | solution.py:51
  183.0 0.0 slice-start
  183.0 5.0 %copy.42 = f32[96,8,32,128]{3,2,1,0:T(8,128)S(1)} copy(bf16[96,8,32,128]{3,1,2,0:T(8,128)(2,1)} %bitcast.56) | data formatting | bytes 18874368
  188.0 0.0 slice-start.1
  188.0 0.0 slice-start.2
  188.1 4.1 %fusion = bf16[768,32,128]{2,1,0:T(8,128)(2,1)S(1)} fusion(f32[96,8,32,128]{3,2,1,0:T(8,128)S(1)} %copy.42, f32[768,32]{1,0:T(8,128)S(1)} %bitcast.67), kind=kLoop, calls=%fused_computation.6 | loop fusion | flops 6291456 | bytes 18972672 | tf_op jit(solution)/shard_map/convert_element_type | solution.py:18
  192.2 0.0 slice-done
  192.2 0.0 slice-done.1
  192.2 0.0 slice-start.3
  192.2 0.0 slice-start.4
  192.2 5.6 %fusion.4 = f32[768,768]{1,0:T(8,128)S(1)} fusion(bf16[1,4096,768]{2,1,0:T(8,128)(2,1)S(1)} %bitcast.77, bf16[96,8,32,128]{3,2,1,0:T(8,128)(2,1)S(1)} %bitcast.63), kind=kOutput, calls=%fused_computation.12 | convolution fusion | flops 4831838208 | bytes 14942208 | tf_op jit(solution)/shard_map/dot_general | solution.py:22
  197.9 0.0 slice-done.2
  197.9 0.0 slice-done.3
  197.9 0.0 slice-start.5
  197.9 5.8 %multiply_convert_fusion = bf16[768,768]{1,0:T(8,128)(2,1)S(1)} fusion(f32[768,768]{1,0:T(8,128)S(1)} %fusion.4, bf16[1,4096,768]{2,1,0:T(8,128)(2,1)S(1)} %bitcast.79, bf16[96,8,32,128]{3,2,1,0:T(8,128)(2,1)S(1)} %bitcast.64), kind=kOutput, calls=%fused_computation.22 | convolution fusion | flops 4835377152 | bytes 16121856 | tf_op jit(solution)/shard_map/dot_general | solution.py:23
  203.7 0.0 slice-done.4
  203.7 0.0 slice-done.5
  203.7 7.3 %convolution_convert_fusion = bf16[768,4096]{1,0:T(8,128)(2,1)} fusion(bf16[768,768]{1,0:T(8,128)(2,1)S(1)} %multiply_convert_fusion, bf16[1,768,4096]{2,1,0:T(8,128)(2,1)S(1)} %bitcast.81), kind=kOutput, calls=%fused_computation.9 | convolution fusion | flops 4834983936 | bytes 13762560 | tf_op jit(solution)/shard_map/dot_general | solution.py:25
  211.0 0.0 copy-start.1
  211.0 5.0 %all-to-all-start.2 = ((bf16[16,48,4096]{2,1,0:T(8,128)(2,1)}), bf16[16,48,4096]{2,1,0:T(8,128)(2,1)}, u32[]{:S(2)}, u32[]{:S(2)}) async-start(bf16[16,48,4096]{2,1,0:T(8,128)(2,1)} %bitcast.62), calls=%async_computation.2 | async-start | bytes 12582912 | tf_op jit(solution)/shard_map/all_to_all | solution.py:73
  216.0 0.0 copy-done.1
  216.1 0.1 copy.34
  216.2 137.3 %all-to-all-done.2 = bf16[16,48,4096]{2,1,0:T(8,128)(2,1)} async-done(((bf16[16,48,4096]{2,1,0:T(8,128)(2,1)}), bf16[16,48,4096]{2,1,0:T(8,128)(2,1)}, u32[]{:S(2)}, u32[]{:S(2)}) %all-to-all-start.2) | async-done | bytes 6291488 | tf_op jit(solution)/shard_map/all_to_all | solution.py:73
  353.4 12.3 %gather_fusion = bf16[512,4096]{1,0:T(8,128)(2,1)} fusion(bf16[768,4096]{1,0:T(8,128)(2,1)} %bitcast.11, s32[1024]{0:T(1024)S(1)} %pad_clamp_fusion), kind=kCustom, calls=%fused_computation.2 | custom fusion | bytes 8390656 | tf_op jit(solution)/shard_map/gather | solution.py:81
  365.7 6.5 %fusion.1 = bf16[64,4096]{1,0:T(8,128)(2,1)} fusion(bf16[512,4096]{1,0:T(8,128)(2,1)} %gather_fusion, f32[64,8]{1,0:T(8,128)S(1)} %copy.34), kind=kLoop, calls=%fused_computation.8 | loop fusion | flops 6029312 | bytes 4720640 | tf_op jit(solution)/shard_map/reduce_sum | solution.py:84
  (13 shorter events, 0.1 us)
Async XLA Ops:
  0.0 16.5 %copy-start = (bf16[64,4096]{1,0:T(8,128)(2,1)S(1)}, bf16[64,4096]{1,0:T(8,128)(2,1)}, u32[]{:S(2)}) copy-start(bf16[64,4096]{1,0:T(8,128)(2,1)} %param.6) | copy-start | bytes 1572868
  9.1 30.2 %all-to-all-start.1 = ((bf16[16,2,768]{2,1,0:T(2,128)(2,1)}), bf16[16,2,768]{2,1,0:T(2,128)(2,1)S(1)}, u32[]{:S(2)}, u32[]{:S(2)}) async-start(bf16[16,2,768]{2,1,0:T(2,128)(2,1)} %reshape.217), calls=%async_computation.1 | async-start | bytes 98304 | tf_op jit(solution)/shard_map/all_to_all | solution.py:58
  39.4 143.6 %all-to-all-start = ((bf16[16,48,4096]{2,1,0:T(8,128)(2,1)}), bf16[16,48,4096]{2,1,0:T(8,128)(2,1)}, u32[]{:S(2)}, u32[]{:S(2)}) async-start(bf16[16,48,4096]{2,1,0:T(8,128)(2,1)} %bitcast.61), calls=%async_computation | async-start | bytes 12582912 | tf_op jit(solution)/shard_map/all_to_all | solution.py:51
  183.0 9.2 %slice-start = ((s8[6291456]{0:T(1024)(128)(4,1)}), s8[4194304]{0:T(1024)(128)(4,1)S(1)}, s32[]{:S(2)}) async-start(s8[6291456]{0:T(1024)(128)(4,1)} %bitcast.76), calls=%async_computation.3 | async-start | bytes 8388608
  188.0 4.2 %slice-start.1 = ((s8[6291456]{0:T(1024)(128)(4,1)}), s8[2097152]{0:T(1024)(128)(4,1)S(1)}, s32[]{:S(2)}) async-start(s8[6291456]{0:T(1024)(128)(4,1)} %bitcast.76), calls=%async_computation.4 | async-start | bytes 4194304
  188.0 9.8 %slice-start.2 = ((s8[6291456]{0:T(1024)(128)(4,1)}), s8[4194304]{0:T(1024)(128)(4,1)S(1)}, s32[]{:S(2)}) async-start(s8[6291456]{0:T(1024)(128)(4,1)} %bitcast.78), calls=%async_computation.5 | async-start | bytes 8388608
  192.2 5.7 %slice-start.3 = ((s8[6291456]{0:T(1024)(128)(4,1)}), s8[2097152]{0:T(1024)(128)(4,1)S(1)}, s32[]{:S(2)}) async-start(s8[6291456]{0:T(1024)(128)(4,1)} %bitcast.78), calls=%async_computation.6 | async-start | bytes 4194304
  192.2 11.5 %slice-start.4 = ((s8[6291456]{0:T(1024)(128)(4,1)}), s8[4194304]{0:T(1024)(128)(4,1)S(1)}, s32[]{:S(2)}) async-start(s8[6291456]{0:T(1024)(128)(4,1)} %bitcast.80), calls=%async_computation.7 | async-start | bytes 8388608
  197.9 5.8 %slice-start.5 = ((s8[6291456]{0:T(1024)(128)(4,1)}), s8[2097152]{0:T(1024)(128)(4,1)S(1)}, s32[]{:S(2)}) async-start(s8[6291456]{0:T(1024)(128)(4,1)} %bitcast.80), calls=%async_computation.8 | async-start | bytes 4194304
  211.0 5.0 %copy-start.1 = (s32[64,8]{0,1:T(8,128)S(1)}, s32[64,8]{0,1:T(8,128)}, u32[]{:S(2)}) copy-start(s32[64,8]{0,1:T(8,128)} %param.8) | copy-start | bytes 6148
  211.0 142.4 %all-to-all-start.2 = ((bf16[16,48,4096]{2,1,0:T(8,128)(2,1)}), bf16[16,48,4096]{2,1,0:T(8,128)(2,1)}, u32[]{:S(2)}, u32[]{:S(2)}) async-start(bf16[16,48,4096]{2,1,0:T(8,128)(2,1)} %bitcast.62), calls=%async_computation.2 | async-start | bytes 12582912 | tf_op jit(solution)/shard_map/all_to_all | solution.py:73
where the time goes:
time: 376 us; the launch traced here: 373 us
  waiting for transfers between devices  274 us (73%)
  local copies, waits for them, and re-layouts  45.7 us (12%)
  matrix products  18.7 us (5%)
  starting transfers between devices  18.4 us (5%)
  other arithmetic  14.8 us (4%)
    all_to_all x1, waiting for transfers between devices, local(): lax.all_to_all(expert_rows.reshape(node_count, slot_most, model_width), '...  137 us
    all_to_all x1, waiting for transfers between devices, local(): lax.all_to_all(send_coded.reshape(node_count, slot_most, model_width), 'n...  137 us
    scatter x1, local copies, waits for them, and re-layouts, local(): jnp.zeros((slot_total, model_width), jnp.bfloat16).at[dest_slot]  22.1 us
    gather x1, local copies, waits for them, and re-layouts, local(): returned[dest_slot].reshape(tok_rows, top_k, model_width)  12.3 us
  transfers between devices with their start and end apart: 3, of which 2 were waited for; matrix products, arithmetic and copies ran while one was open for 6% of the time, Pallas kernels for 0%

commit v1 on v0

v1 whole, which is shorter than its diff:
```python
import functools

import jax
import jax.numpy as jnp
from jax import lax
from jax.experimental import pallas as pl
from jax.experimental.pallas import tpu as pltpu
from jax.sharding import PartitionSpec as P

LANES = 128
FF_TILE = 256
OUT_TILE = 1024


def encode_kernel(tokens_ref, routes_ref, codes_ref, first_ref, second_ref):
    rows, width = tokens_ref.shape
    half = rows // 2
    for b in range(width // LANES):
        cols = slice(b * LANES, (b + 1) * LANES)
        block = tokens_ref[:, cols].astype(jnp.float32)
        largest = jnp.max(jnp.abs(block), axis=1, keepdims=True)
        scale = ((largest + 1e-6) / 448.0).astype(jnp.bfloat16).astype(jnp.float32)
        coded = (block / scale).astype(jnp.bfloat16).astype(jnp.float32)
        value = (coded * scale).astype(jnp.bfloat16)
        first_ref[:, cols] = value[:half]
        second_ref[:, cols] = value[half:]
    lane = lax.broadcasted_iota(jnp.int32, (rows, LANES), 1)
    table = jnp.zeros((rows, LANES), jnp.float32)
    for k in range(routes_ref.shape[1]):
        code = codes_ref[:, k : k + 1].astype(jnp.float32)
        table = table + jnp.where(lane == routes_ref[:, k : k + 1], code, 0.0)
    first_ref[:, width:] = table[:half].astype(jnp.bfloat16)
    second_ref[:, width:] = table[half:].astype(jnp.bfloat16)


def encode(tokens, routes, gate_codes):
    rows, width = tokens.shape
    out = jax.ShapeDtypeStruct((rows // 2, width + LANES), jnp.bfloat16)
    return pl.pallas_call(
        encode_kernel,
        out_shape=(out, out),
        compiler_params=pltpu.CompilerParams(vmem_limit_bytes=8 << 20),
    )(tokens, routes, gate_codes)


def expert_kernel(count, me_ref, *refs):
    x_refs = refs[:count]
    gate_hbm, up_hbm, down_hbm = refs[count : count + 3]
    out_refs = refs[count + 3 : 2 * count + 3]
    gate_w, up_w, down_w, x, hidden, scale, gate_sem, up_sem, down_sem = refs[2 * count + 3 :]
    width, ff = gate_w.shape
    ff_tiles, out_tiles = ff // FF_TILE, width // OUT_TILE

    def gate_copy(t):
        cols = pl.ds(pl.multiple_of(t * FF_TILE, FF_TILE), FF_TILE)
        return (
            pltpu.make_async_copy(gate_hbm.at[:, cols], gate_w.at[:, cols], gate_sem.at[t]),
            pltpu.make_async_copy(up_hbm.at[:, cols], up_w.at[:, cols], up_sem.at[t]),
        )

    def down_copy(t):
        cols = pl.ds(pl.multiple_of(t * OUT_TILE, OUT_TILE), OUT_TILE)
        return pltpu.make_async_copy(down_hbm.at[:, cols], down_w.at[:, cols], down_sem.at[t])

    for t in range(ff_tiles):
        for copy in gate_copy(t):
            copy.start()
    for t in range(out_tiles):
        down_copy(t).start()

    lane = lax.broadcasted_iota(jnp.int32, (x_refs[0].shape[0], LANES), 1)
    for i, ref in enumerate(x_refs):
        rows = ref.shape[0]
        span = slice(i * rows, (i + 1) * rows)
        x[span, :] = ref[:, :width]
        codes = ref[:, width:].astype(jnp.float32)
        total = jnp.sum(codes, axis=1, keepdims=True)
        mine = jnp.sum(jnp.where(lane == me_ref[0], codes, 0.0), axis=1, keepdims=True)
        scale[span, :] = jnp.broadcast_to(mine / total, (rows, LANES))

    @pl.loop(0, ff_tiles)
    def _(t):
        for copy in gate_copy(t):
            copy.wait()
        cols = pl.ds(pl.multiple_of(t * FF_TILE, FF_TILE), FF_TILE)
        gate = jnp.dot(x[...], gate_w[:, cols], preferred_element_type=jnp.float32)
        up = jnp.dot(x[...], up_w[:, cols], preferred_element_type=jnp.float32)
        hidden[:, cols] = (gate / (1.0 + jnp.exp(-gate)) * up).astype(jnp.bfloat16)

    @pl.loop(0, out_tiles)
    def _(t):
        down_copy(t).wait()
        cols = pl.ds(pl.multiple_of(t * OUT_TILE, OUT_TILE), OUT_TILE)
        result = jnp.dot(hidden[...], down_w[:, cols], preferred_element_type=jnp.float32)
        for i, ref in enumerate(out_refs):
            rows = ref.shape[0]
            span = slice(i * rows, (i + 1) * rows)
            ref[:, cols] = (result[span, :] * scale[span, 0:1]).astype(jnp.bfloat16)


def expert(me, blocks, w_gate, w_up, w_down):
    count = len(blocks)
    rows = blocks[0].shape[0]
    width, ff = w_gate.shape
    total = rows * count
    out = jax.ShapeDtypeStruct((rows, width), jnp.bfloat16)
    vmem = pl.BlockSpec(memory_space=pltpu.VMEM)
    return pl.pallas_call(
        functools.partial(expert_kernel, count),
        in_specs=[pl.BlockSpec(memory_space=pltpu.SMEM)] + [vmem] * count + [pl.BlockSpec(memory_space=pl.ANY)] * 3,
        out_specs=[vmem] * count,
        out_shape=[out] * count,
        scratch_shapes=[
            pltpu.VMEM((width, ff), jnp.bfloat16),
            pltpu.VMEM((width, ff), jnp.bfloat16),
            pltpu.VMEM((ff, width), jnp.bfloat16),
            pltpu.VMEM((total, width), jnp.bfloat16),
            pltpu.VMEM((total, ff), jnp.bfloat16),
            pltpu.VMEM((total, LANES), jnp.float32),
            pltpu.SemaphoreType.DMA((ff // FF_TILE,)),
            pltpu.SemaphoreType.DMA((ff // FF_TILE,)),
            pltpu.SemaphoreType.DMA((width // OUT_TILE,)),
        ],
        cost_estimate=pl.CostEstimate(
            flops=6 * total * width * ff,
            bytes_accessed=6 * width * ff + 4 * total * width,
            transcendentals=total * ff,
        ),
        compiler_params=pltpu.CompilerParams(vmem_limit_bytes=40 << 20),
    )(me, *blocks, w_gate, w_up, w_down)


def ring_order(nodes, groups):
    chips = nodes // 2
    if groups == 2:
        return list(range(0, chips, 2)) + list(range(1, chips, 2))[::-1]
    return list(range(chips))


def local(nodes, groups, tokens, routes, gate_codes, w_gate, w_up, w_down):
    order = ring_order(nodes, groups)
    chips = len(order)
    far = chips // 2
    me = lax.axis_index("node").astype(jnp.int32).reshape(1)
    gate_w, up_w, down_w = w_gate[0], w_up[0], w_down[0]

    def hop(value, step):
        pairs = [
            (2 * order[i] + core, 2 * order[(i + step) % chips] + core) for i in range(chips) for core in (0, 1)
        ]
        return lax.ppermute(value, "node", pairs)

    def swap(value):
        return lax.ppermute(value, "node", [(i, i ^ 1) for i in range(nodes)])

    def total(*terms):
        return functools.reduce(lambda a, b: a + b, [t.astype(jnp.float32) for t in terms]).astype(jnp.bfloat16)

    held = {}
    held[0, 0], held[1, 0] = encode(tokens, routes, gate_codes)
    slots = [[(0, 0), (1, 0)]]
    for k in range(1, 2 * far):
        s = (k + 1) // 2
        ahead, behind = (0, 1) if k % 2 else (1, 0)
        held[ahead, s] = hop(held[ahead, s - 1], 1)
        held[behind, -s] = hop(held[behind, 1 - s], -1)
        slots.append([(ahead, s), (behind, -s)])
    other = {key: swap(held[key]) for slot in slots for key in slot}

    groups_of = []
    pending = []
    for k, slot in enumerate(slots):
        pending += slot
        if k % 2 or k >= 2 * far - 2:
            groups_of.append(pending)
            pending = []
    mine, theirs = {}, {}
    for keys in groups_of:
        outs = expert(me, [held[key] for key in keys] + [other[key] for key in keys], gate_w, up_w, down_w)
        for i, key in enumerate(keys):
            mine[key] = outs[i]
            theirs[key] = swap(outs[len(keys) + i])

    carried = {}
    for half in (0, 1):
        for sign in (1, -1):
            last = far if (half == 0) == (sign == 1) else far - 1
            message = None
            for s in range(last, 0, -1):
                key = (half, sign * s)
                terms = [mine[key], theirs[key]] + ([] if message is None else [message])
                message = hop(total(*terms), -sign)
            carried[half, sign] = message
    final = [
        total(mine[half, 0], theirs[half, 0], carried[half, 1], carried[half, -1]) for half in (0, 1)
    ]
    return jnp.concatenate(final, axis=0)


def solution(mesh):
    return jax.shard_map(
        functools.partial(local, mesh.shape["node"], mesh.shape["groups"]),
        mesh=mesh,
        in_specs=(
            P(("groups", "node"), None),
            P(("groups", "node"), None),
            P(("groups", "node"), None),
            P("node", None, None),
            P("node", None, None),
            P("node", None, None),
        ),
        out_specs=P(("groups", "node"), None),
        check_vma=False,
    )
```

time: 376 us -> 177 us (0.47)
  the two profiles are of different devices: /device:TPU:15 before, /device:TPU:0 now
where the time goes in v1:
time: 177 us; the launch traced here: 176 us
  waiting for transfers between devices  86.2 us (49%)
  Pallas kernels  41.3 us (23%)
  starting transfers between devices  37.4 us (21%)
  local copies, waits for them, and re-layouts  8.69 us (5%)
  other arithmetic  2.34 us (1%)
    ppermute x28, waiting for transfers between devices, hop(): return lax.ppermute(value, 'node', pairs)  81.9 us
    pallas_call x5, Pallas kernels, expert(): pl.pallas_call(functools.partial(expert_kernel, count), in_specs=[pl.Bloc...  40.7 us
    ppermute x28, starting transfers between devices, hop(): return lax.ppermute(value, 'node', pairs)  32.7 us
    unnamed x16, local copies, waits for them, and re-layouts  8.69 us
    ppermute x32, starting transfers between devices, swap(): return lax.ppermute(value, 'node', [(i, i ^ 1) for i in range(nodes)])  4.77 us
    ppermute x32, waiting for transfers between devices, swap(): return lax.ppermute(value, 'node', [(i, i ^ 1) for i in range(nodes)])  4.27 us
  transfers between devices with their start and end apart: 60, of which 24 were waited for; matrix products, arithmetic and copies ran while one was open for 1% of the time, Pallas kernels for 23%

profile of v1, /device:TPU:0, one launch (start us, length us, event | category | flops | bytes accessed | tf_op | source)
XLA Modules:
  0.0 176.3 jit_solution(7068629929108703847)
XLA Ops:
  0.0 0.8 copy.7.routes_ref
  0.8 0.8 copy.8.codes_ref
  1.5 1.0 copy-done.2
  2.6 0.6 shard_map.64
  3.2 3.1 %collective-permute-start = (bf16[32,4224]{1,0:T(8,128)(2,1)S(1)}, bf16[32,4224]{1,0:T(8,128)(2,1)S(1)}, u32[]{:S(2)}, u32[]{:S(2)}) collective-permute-start(bf16[32,4224]{1,0:T(8,128)(2,1)S(1)} %get-tuple-element.39.refs_0_), channel_id=1, source_target_pairs={{0,4},{1,5},{4,8},{5,9},{8,12},{9,13},{12,14},{13,15},{14,10},{15,... | collective-permute-start | bytes 811016 | tf_op jit(solution)/shard_map/ppermute | solution.py:151
  6.3 2.0 %collective-permute-start.8 = (bf16[32,4224]{1,0:T(8,128)(2,1)S(1)}, bf16[32,4224]{1,0:T(8,128)(2,1)S(1)}, u32[]{:S(2)}, u32[]{:S(2)}) collective-permute-start(bf16[32,4224]{1,0:T(8,128)(2,1)S(1)} %get-tuple-element.40.refs_1_), channel_id=1, source_target_pairs={{0,4},{1,5},{4,8},{5,9},{8,12},{9,13},{12,14},{13,15},{14,10},{15,... | collective-permute-start | bytes 811016 | tf_op jit(solution)/shard_map/ppermute | solution.py:151
  8.3 5.2 %collective-permute-done.refs_2_ = bf16[32,4224]{1,0:T(8,128)(2,1)S(1)} collective-permute-done((bf16[32,4224]{1,0:T(8,128)(2,1)S(1)}, bf16[32,4224]{1,0:T(8,128)(2,1)S(1)}, u32[]{:S(2)}, u32[]{:S(2)}) %collective-permute-start) | collective-permute-done | bytes 270368 | tf_op jit(solution)/shard_map/ppermute | solution.py:151
  13.5 2.1 %collective-permute-done.1.refs_3_ = bf16[32,4224]{1,0:T(8,128)(2,1)S(1)} collective-permute-done((bf16[32,4224]{1,0:T(8,128)(2,1)S(1)}, bf16[32,4224]{1,0:T(8,128)(2,1)S(1)}, u32[]{:S(2)}, u32[]{:S(2)}) %collective-permute-start.1) | collective-permute-done | bytes 270368 | tf_op jit(solution)/shard_map/ppermute | solution.py:151
  15.7 1.6 collective-permute-start.10
  17.3 2.1 %collective-permute-done.8.refs_0_ = bf16[32,4224]{1,0:T(8,128)(2,1)S(1)} collective-permute-done((bf16[32,4224]{1,0:T(8,128)(2,1)S(1)}, bf16[32,4224]{1,0:T(8,128)(2,1)S(1)}, u32[]{:S(2)}, u32[]{:S(2)}) %collective-permute-start.8) | collective-permute-done | bytes 270368 | tf_op jit(solution)/shard_map/ppermute | solution.py:151
  19.3 2.1 %collective-permute-start.11 = (bf16[32,4224]{1,0:T(8,128)(2,1)S(1)}, bf16[32,4224]{1,0:T(8,128)(2,1)S(1)}, u32[]{:S(2)}, u32[]{:S(2)}) collective-permute-start(bf16[32,4224]{1,0:T(8,128)(2,1)S(1)} %collective-permute-done.1.refs_3_), channel_id=1, source_target_pairs={{0,2},{1,3},{4,0},{5,1},{8,4},{9,5},{12,8},{13,9},{14,12},{15,13},... | collective-permute-start | bytes 811016 | tf_op jit(solution)/shard_map/ppermute | solution.py:151
  21.6 0.7 copy-done.3
  22.3 1.8 %collective-permute-start.18 = (bf16[32,4224]{1,0:T(8,128)(2,1)S(1)}, bf16[32,4224]{1,0:T(8,128)(2,1)S(1)}, u32[]{:S(2)}, u32[]{:S(2)}) collective-permute-start(bf16[32,4224]{1,0:T(8,128)(2,1)S(1)} %collective-permute-done.9.refs_1_), channel_id=1, source_target_pairs={{0,2},{1,3},{4,0},{5,1},{8,4},{9,5},{12,8},{13,9},{14,12},{15,13},... | collective-permute-start | bytes 811016 | tf_op jit(solution)/shard_map/ppermute | solution.py:151
  24.1 0.7 copy-done.5
  25.4 3.5 %collective-permute-done.11.refs_3_ = bf16[32,4224]{1,0:T(8,128)(2,1)S(1)} collective-permute-done((bf16[32,4224]{1,0:T(8,128)(2,1)S(1)}, bf16[32,4224]{1,0:T(8,128)(2,1)S(1)}, u32[]{:S(2)}, u32[]{:S(2)}) %collective-permute-start.11) | collective-permute-done | bytes 270368 | tf_op jit(solution)/shard_map/ppermute | solution.py:151
  28.8 1.2 collective-permute-done.17.refs_0_
  30.1 1.9 %collective-permute-done.18.refs_1_ = bf16[32,4224]{1,0:T(8,128)(2,1)S(1)} collective-permute-done((bf16[32,4224]{1,0:T(8,128)(2,1)S(1)}, bf16[32,4224]{1,0:T(8,128)(2,1)S(1)}, u32[]{:S(2)}, u32[]{:S(2)}) %collective-permute-start.18) | collective-permute-done | bytes 270368 | tf_op jit(solution)/shard_map/ppermute | solution.py:151
  32.0 1.6 collective-permute-start.19
  33.5 1.5 collective-permute-start.37
  35.1 0.6 collective-permute-start.20
  35.8 5.6 %collective-permute-done.19.refs_2_ = bf16[32,4224]{1,0:T(8,128)(2,1)S(1)} collective-permute-done((bf16[32,4224]{1,0:T(8,128)(2,1)S(1)}, bf16[32,4224]{1,0:T(8,128)(2,1)S(1)}, u32[]{:S(2)}, u32[]{:S(2)}) %collective-permute-start.19) | collective-permute-done | bytes 270368 | tf_op jit(solution)/shard_map/ppermute | solution.py:151
  41.4 1.4 collective-permute-start.38
  42.8 2.1 %collective-permute-done.37.refs_0_ = bf16[32,4224]{1,0:T(8,128)(2,1)} collective-permute-done((bf16[32,4224]{1,0:T(8,128)(2,1)S(1)}, bf16[32,4224]{1,0:T(8,128)(2,1)}, u32[]{:S(2)}, u32[]{:S(2)}) %collective-permute-start.37) | collective-permute-done | bytes 270368 | tf_op jit(solution)/shard_map/ppermute | solution.py:151
  44.9 2.8 %copy-done = bf16[1,4096,768]{2,1,0:T(8,128)(2,1)S(1)} copy-done((bf16[1,4096,768]{2,1,0:T(8,128)(2,1)S(1)}, bf16[1,4096,768]{2,1,0:T(8,128)(2,1)}, u32[]{:S(2)}) %copy-start) | copy-done | bytes 6291480
  47.7 1.0 copy-done.4
  48.6 1.0 copy-done.6
  49.6 9.6 %shard_map.65 = (bf16[32,4096]{1,0:T(8,128)(2,1)S(1)}, bf16[32,4096]{1,0:T(8,128)(2,1)S(1)}, bf16[32,4096]{1,0:T(8,128)(2,1)S(1)}, bf16[32,4096]{1,0:T(8,128)(2,...) custom-call(s32[1]{0:T(128)} %bitcast.me_ref, ...), custom_call_target="tpu_custom_call" | custom-call | flops 4831838208 | bytes 23068672 | tf_op jit(solution)/shard_map/pallas_call | solution.py:108
  59.2 0.6 collective-permute-start.21
  59.8 0.4 collective-permute-start.23
  60.4 0.4 collective-permute-start.40
  60.8 8.2 %shard_map.66 = (bf16[32,4096]{1,0:T(8,128)(2,1)S(1)}, bf16[32,4096]{1,0:T(8,128)(2,1)S(1)}, bf16[32,4096]{1,0:T(8,128)(2,1)S(1)}, bf16[32,4096]{1,0:T(8,128)(2,...) custom-call(s32[1]{0:T(128)} %bitcast.me_ref, ...), custom_call_target="tpu_custom_call" | custom-call | flops 4831838208 | bytes 23068672 | tf_op jit(solution)/shard_map/pallas_call | solution.py:108
  69.2 7.8 %shard_map.69 = (bf16[32,4096]{1,0:T(8,128)(2,1)S(1)}, bf16[32,4096]{1,0:T(8,128)(2,1)S(1)}, bf16[32,4096]{1,0:T(8,128)(2,1)S(1)}, bf16[32,4096]{1,0:T(8,128)(2,1)S(1)}) custom-call(s32[1]{0:T(128)} %bitcast.me_ref, bf16[32,4224]{1,0:T(8,128)(2,1)} %collective-permute-done.37.refs_0_, bf16[32,4224]{1,0:T(8,128)(2,1)S(1)} %collective-permute-done.38.refs_1_, ...), custom_call_target="tpu_custom_call" | custom-call | flops 2415919104 | bytes 20971520 | tf_op jit(solution)/shard_map/pallas_call | solution.py:108
  77.0 1.8 %collective-permute-start.26 = (bf16[32,4224]{1,0:T(8,128)(2,1)S(1)}, bf16[32,4224]{1,0:T(8,128)(2,1)S(1)}, u32[]{:S(2)}, u32[]{:S(2)}) collective-permute-start(bf16[32,4224]{1,0:T(8,128)(2,1)S(1)} %collective-permute-done.19.refs_2_), channel_id=1, source_target_pairs={{0,4},{1,5},{4,8},{5,9},{8,12},{9,13},{12,14},{13,15},{14,10},{15,... | collective-permute-start | bytes 811016 | tf_op jit(solution)/shard_map/ppermute | solution.py:151
  79.1 8.2 %shard_map.67 = (bf16[32,4096]{1,0:T(8,128)(2,1)S(1)}, bf16[32,4096]{1,0:T(8,128)(2,1)S(1)}, bf16[32,4096]{1,0:T(8,128)(2,1)S(1)}, bf16[32,4096]{1,0:T(8,128)(2,...) custom-call(s32[1]{0:T(128)} %bitcast.me_ref, ...), custom_call_target="tpu_custom_call" | custom-call | flops 4831838208 | bytes 23068672 | tf_op jit(solution)/shard_map/pallas_call | solution.py:108
  87.3 0.6 collective-permute-start.36
  88.0 0.4 collective-permute-start.28
  88.6 0.9 collective-permute-done.48
  89.4 1.8 %collective-permute-start.42 = (bf16[32,4096]{1,0:T(8,128)(2,1)S(1)}, bf16[32,4096]{1,0:T(8,128)(2,1)S(1)}, u32[]{:S(2)}, u32[]{:S(2)}) collective-permute-start(bf16[32,4096]{1,0:T(8,128)(2,1)S(1)} %add_convert_fusion.11), channel_id=1, source_target_pairs={{0,4},{1,5},{4,8},{5,9},{8,12},{9,13},{12,14},{13,15},{14,10},{15,... | collective-permute-start | bytes 786440 | tf_op jit(solution)/shard_map/ppermute | solution.py:151
  91.5 0.4 collective-permute-start.52
  91.9 6.9 %shard_map.68 = (bf16[32,4096]{1,0:T(8,128)(2,1)S(1)}, bf16[32,4096]{1,0:T(8,128)(2,1)S(1)}, bf16[32,4096]{1,0:T(8,128)(2,1)S(1)}, bf16[32,4096]{1,0:T(8,128)(2,1)S(1)}) custom-call(s32[1]{0:T(128)} %bitcast.me_ref, bf16[32,4224]{1,0:T(8,128)(2,1)S(1)} %collective-permute-done.26.refs_0_, bf16[32,4224]{1,0:T(8,128)(2,1)S(1)} %collective-permute-done.27.refs_1_, ...), custom_call_target="tpu_custom_call" | custom-call | flops 2415919104 | bytes 20971520 | tf_op jit(solution)/shard_map/pallas_call | solution.py:108
  99.0 0.8 collective-permute-start.49
  99.8 0.6 collective-permute-done.47
  100.5 7.1 %collective-permute-done.49 = bf16[32,4096]{1,0:T(8,128)(2,1)S(1)} collective-permute-done((bf16[32,4096]{1,0:T(8,128)(2,1)S(1)}, bf16[32,4096]{1,0:T(8,128)(2,1)S(1)}, u32[]{:S(2)}, u32[]{:S(2)}) %collective-permute-start.49) | collective-permute-done | bytes 262176 | tf_op jit(solution)/shard_map/ppermute | solution.py:151
  107.7 1.4 collective-permute-done.30
  109.4 1.3 collective-permute-done.55
  110.7 1.6 collective-permute-start.43
  112.4 6.6 %collective-permute-done.43 = bf16[32,4096]{1,0:T(8,128)(2,1)S(1)} collective-permute-done((bf16[32,4096]{1,0:T(8,128)(2,1)S(1)}, bf16[32,4096]{1,0:T(8,128)(2,1)S(1)}, u32[]{:S(2)}, u32[]{:S(2)}) %collective-permute-start.43) | collective-permute-done | bytes 262176 | tf_op jit(solution)/shard_map/ppermute | solution.py:151
  119.0 0.4 collective-permute-start.50
  119.6 6.9 %collective-permute-done.50 = bf16[32,4096]{1,0:T(8,128)(2,1)S(1)} collective-permute-done((bf16[32,4096]{1,0:T(8,128)(2,1)S(1)}, bf16[32,4096]{1,0:T(8,128)(2,1)S(1)}, u32[]{:S(2)}, u32[]{:S(2)}) %collective-permute-start.50) | collective-permute-done | bytes 262176 | tf_op jit(solution)/shard_map/ppermute | solution.py:151
  126.6 0.4 collective-permute-start.31
  127.1 6.0 %collective-permute-done.31 = bf16[32,4096]{1,0:T(8,128)(2,1)S(1)} collective-permute-done((bf16[32,4096]{1,0:T(8,128)(2,1)S(1)}, bf16[32,4096]{1,0:T(8,128)(2,1)S(1)}, u32[]{:S(2)}, u32[]{:S(2)}) %collective-permute-start.31) | collective-permute-done | bytes 262176 | tf_op jit(solution)/shard_map/ppermute | solution.py:151
  133.2 1.6 collective-permute-start.56
  134.9 4.6 %collective-permute-done.56 = bf16[32,4096]{1,0:T(8,128)(2,1)S(1)} collective-permute-done((bf16[32,4096]{1,0:T(8,128)(2,1)S(1)}, bf16[32,4096]{1,0:T(8,128)(2,1)S(1)}, u32[]{:S(2)}, u32[]{:S(2)}) %collective-permute-start.56) | collective-permute-done | bytes 262176 | tf_op jit(solution)/shard_map/ppermute | solution.py:151
  140.1 5.8 %collective-permute-done.32 = bf16[32,4096]{1,0:T(8,128)(2,1)S(1)} collective-permute-done((bf16[32,4096]{1,0:T(8,128)(2,1)S(1)}, bf16[32,4096]{1,0:T(8,128)(2,1)S(1)}, u32[]{:S(2)}, u32[]{:S(2)}) %collective-permute-start.32) | collective-permute-done | bytes 262176 | tf_op jit(solution)/shard_map/ppermute | solution.py:151
  145.9 1.6 collective-permute-start.57
  147.7 5.7 %collective-permute-done.57 = bf16[32,4096]{1,0:T(8,128)(2,1)S(1)} collective-permute-done((bf16[32,4096]{1,0:T(8,128)(2,1)S(1)}, bf16[32,4096]{1,0:T(8,128)(2,1)S(1)}, u32[]{:S(2)}, u32[]{:S(2)}) %collective-permute-start.57) | collective-permute-done | bytes 262176 | tf_op jit(solution)/shard_map/ppermute | solution.py:151
  153.9 1.7 collective-permute-start.44
  155.6 6.4 %collective-permute-done.33 = bf16[32,4096]{1,0:T(8,128)(2,1)S(1)} collective-permute-done((bf16[32,4096]{1,0:T(8,128)(2,1)S(1)}, bf16[32,4096]{1,0:T(8,128)(2,1)S(1)}, u32[]{:S(2)}, u32[]{:S(2)}) %collective-permute-start.33) | collective-permute-done | bytes 262176 | tf_op jit(solution)/shard_map/ppermute | solution.py:151
  162.0 1.6 collective-permute-start.58
  163.7 0.5 collective-permute-start.51
  164.2 4.5 %collective-permute-done.58 = bf16[32,4096]{1,0:T(8,128)(2,1)S(1)} collective-permute-done((bf16[32,4096]{1,0:T(8,128)(2,1)S(1)}, bf16[32,4096]{1,0:T(8,128)(2,1)S(1)}, u32[]{:S(2)}, u32[]{:S(2)}) %collective-permute-start.58) | collective-permute-done | bytes 262176 | tf_op jit(solution)/shard_map/ppermute | solution.py:151
  168.9 2.0 %collective-permute-start.59 = (bf16[32,4096]{1,0:T(8,128)(2,1)S(1)}, bf16[32,4096]{1,0:T(8,128)(2,1)S(1)}, u32[]{:S(2)}, u32[]{:S(2)}) collective-permute-start(bf16[32,4096]{1,0:T(8,128)(2,1)S(1)} %add_convert_fusion.1), channel_id=1, source_target_pairs={{0,4},{1,5},{4,8},{5,9},{8,12},{9,13},{12,14},{13,15},{14,10},{15,... | collective-permute-start | bytes 786440 | tf_op jit(solution)/shard_map/ppermute | solution.py:151
  170.9 4.2 %collective-permute-done.34 = bf16[32,4096]{1,0:T(8,128)(2,1)S(1)} collective-permute-done((bf16[32,4096]{1,0:T(8,128)(2,1)S(1)}, bf16[32,4096]{1,0:T(8,128)(2,1)S(1)}, u32[]{:S(2)}, u32[]{:S(2)}) %collective-permute-start.34) | collective-permute-done | bytes 262176 | tf_op jit(solution)/shard_map/ppermute | solution.py:151
  175.5 0.8 pad_maximum_fusion
  (95 shorter events, 5.2 us)
Async XLA Ops:
  1.5 1.0 copy-start.2
  3.2 10.3 %collective-permute-start = (bf16[32,4224]{1,0:T(8,128)(2,1)S(1)}, bf16[32,4224]{1,0:T(8,128)(2,1)S(1)}, u32[]{:S(2)}, u32[]{:S(2)}) collective-permute-start(bf16[32,4224]{1,0:T(8,128)(2,1)S(1)} %get-tuple-element.39.refs_0_), channel_id=1, source_target_pairs={{0,4},{1,5},{4,8},{5,9},{8,12},{9,13},{12,14},{13,15},{14,10},{15,... | collective-permute-start | bytes 811016 | tf_op jit(solution)/shard_map/ppermute | solution.py:151
  6.3 9.4 %collective-permute-start.1 = (bf16[32,4224]{1,0:T(8,128)(2,1)S(1)}, bf16[32,4224]{1,0:T(8,128)(2,1)S(1)}, u32[]{:S(2)}, u32[]{:S(2)}) collective-permute-start(bf16[32,4224]{1,0:T(8,128)(2,1)S(1)} %get-tuple-element.40.refs_1_), channel_id=1, source_target_pairs={{0,2},{1,3},{4,0},{5,1},{8,4},{9,5},{12,8},{13,9},{14,12},{15,13},... | collective-permute-start | bytes 811016 | tf_op jit(solution)/shard_map/ppermute | solution.py:151
  6.3 13.0 %collective-permute-start.8 = (bf16[32,4224]{1,0:T(8,128)(2,1)S(1)}, bf16[32,4224]{1,0:T(8,128)(2,1)S(1)}, u32[]{:S(2)}, u32[]{:S(2)}) collective-permute-start(bf16[32,4224]{1,0:T(8,128)(2,1)S(1)} %get-tuple-element.40.refs_1_), channel_id=1, source_target_pairs={{0,4},{1,5},{4,8},{5,9},{8,12},{9,13},{12,14},{13,15},{14,10},{15,... | collective-permute-start | bytes 811016 | tf_op jit(solution)/shard_map/ppermute | solution.py:151
  8.3 13.1 %collective-permute-start.9 = (bf16[32,4224]{1,0:T(8,128)(2,1)S(1)}, bf16[32,4224]{1,0:T(8,128)(2,1)S(1)}, u32[]{:S(2)}, u32[]{:S(2)}) collective-permute-start(bf16[32,4224]{1,0:T(8,128)(2,1)S(1)} %get-tuple-element.39.refs_0_), channel_id=1, source_target_pairs={{0,2},{1,3},{4,0},{5,1},{8,4},{9,5},{12,8},{13,9},{14,12},{15,13},... | collective-permute-start | bytes 811016 | tf_op jit(solution)/shard_map/ppermute | solution.py:151
  8.3 13.3 %collective-permute-start.2 = (bf16[32,4224]{1,0:T(8,128)(2,1)S(1)}, bf16[32,4224]{1,0:T(8,128)(2,1)S(1)}, u32[]{:S(2)}, u32[]{:S(2)}) collective-permute-start(bf16[32,4224]{1,0:T(8,128)(2,1)S(1)} %get-tuple-element.39.refs_0_), channel_id=1, source_target_pairs={{0,1},{1,0},{2,3},{3,2},{4,5},{5,4},{6,7},{7,6},{8,9},{9,8},{10,11... | collective-permute-start | bytes 811016 | tf_op jit(solution)/shard_map/ppermute | solution.py:154
  13.5 10.6 %collective-permute-start.3 = (bf16[32,4224]{1,0:T(8,128)(2,1)S(1)}, bf16[32,4224]{1,0:T(8,128)(2,1)S(1)}, u32[]{:S(2)}, u32[]{:S(2)}) collective-permute-start(bf16[32,4224]{1,0:T(8,128)(2,1)S(1)} %get-tuple-element.40.refs_1_), channel_id=1, source_target_pairs={{0,1},{1,0},{2,3},{3,2},{4,5},{5,4},{6,7},{7,6},{8,9},{9,8},{10,11... | collective-permute-start | bytes 811016 | tf_op jit(solution)/shard_map/ppermute | solution.py:154
  15.7 9.4 %collective-permute-start.10 = (bf16[32,4224]{1,0:T(8,128)(2,1)S(1)}, bf16[32,4224]{1,0:T(8,128)(2,1)S(1)}, u32[]{:S(2)}, u32[]{:S(2)}) collective-permute-start(bf16[32,4224]{1,0:T(8,128)(2,1)S(1)} %collective-permute-done.refs_2_), channel_id=1, source_target_pairs={{0,4},{1,5},{4,8},{5,9},{8,12},{9,13},{12,14},{13,15},{14,10},{15,... | collective-permute-start | bytes 811016 | tf_op jit(solution)/shard_map/ppermute | solution.py:151
  19.3 9.5 %collective-permute-start.11 = (bf16[32,4224]{1,0:T(8,128)(2,1)S(1)}, bf16[32,4224]{1,0:T(8,128)(2,1)S(1)}, u32[]{:S(2)}, u32[]{:S(2)}) collective-permute-start(bf16[32,4224]{1,0:T(8,128)(2,1)S(1)} %collective-permute-done.1.refs_3_), channel_id=1, source_target_pairs={{0,2},{1,3},{4,0},{5,1},{8,4},{9,5},{12,8},{13,9},{14,12},{15,13},... | collective-permute-start | bytes 811016 | tf_op jit(solution)/shard_map/ppermute | solution.py:151
  21.4 8.7 %collective-permute-start.17 = (bf16[32,4224]{1,0:T(8,128)(2,1)S(1)}, bf16[32,4224]{1,0:T(8,128)(2,1)S(1)}, u32[]{:S(2)}, u32[]{:S(2)}) collective-permute-start(bf16[32,4224]{1,0:T(8,128)(2,1)S(1)} %collective-permute-done.8.refs_0_), channel_id=1, source_target_pairs={{0,4},{1,5},{4,8},{5,9},{8,12},{9,13},{12,14},{13,15},{14,10},{15,... | collective-permute-start | bytes 811016 | tf_op jit(solution)/shard_map/ppermute | solution.py:151
  22.3 9.7 %collective-permute-start.18 = (bf16[32,4224]{1,0:T(8,128)(2,1)S(1)}, bf16[32,4224]{1,0:T(8,128)(2,1)S(1)}, u32[]{:S(2)}, u32[]{:S(2)}) collective-permute-start(bf16[32,4224]{1,0:T(8,128)(2,1)S(1)} %collective-permute-done.9.refs_1_), channel_id=1, source_target_pairs={{0,2},{1,3},{4,0},{5,1},{8,4},{9,5},{12,8},{13,9},{14,12},{15,13},... | collective-permute-start | bytes 811016 | tf_op jit(solution)/shard_map/ppermute | solution.py:151
  24.8 8.7 %collective-permute-start.12 = (bf16[32,4224]{1,0:T(8,128)(2,1)S(1)}, bf16[32,4224]{1,0:T(8,128)(2,1)S(1)}, u32[]{:S(2)}, u32[]{:S(2)}) collective-permute-start(bf16[32,4224]{1,0:T(8,128)(2,1)S(1)} %collective-permute-done.8.refs_0_), channel_id=1, source_target_pairs={{0,1},{1,0},{2,3},{3,2},{4,5},{5,4},{6,7},{7,6},{8,9},{9,8},{10,11... | collective-permute-start | bytes 811016 | tf_op jit(solution)/shard_map/ppermute | solution.py:154
  25.1 9.9 %collective-permute-start.13 = (bf16[32,4224]{1,0:T(8,128)(2,1)S(1)}, bf16[32,4224]{1,0:T(8,128)(2,1)S(1)}, u32[]{:S(2)}, u32[]{:S(2)}) collective-permute-start(bf16[32,4224]{1,0:T(8,128)(2,1)S(1)} %collective-permute-done.9.refs_1_), channel_id=1, source_target_pairs={{0,1},{1,0},{2,3},{3,2},{4,5},{5,4},{6,7},{7,6},{8,9},{9,8},{10,11... | collective-permute-start | bytes 811016 | tf_op jit(solution)/shard_map/ppermute | solution.py:154
  28.8 6.2 %collective-permute-start.4 = (bf16[32,4224]{1,0:T(8,128)(2,1)S(1)}, bf16[32,4224]{1,0:T(8,128)(2,1)}, u32[]{:S(2)}, u32[]{:S(2)}) collective-permute-start(bf16[32,4224]{1,0:T(8,128)(2,1)S(1)} %collective-permute-done.refs_2_), channel_id=1, source_target_pairs={{0,1},{1,0},{2,3},{3,2},{4,5},{5,4},{6,7},{7,6},{8,9},{9,8},{10,11... | collective-permute-start | bytes 811016 | tf_op jit(solution)/shard_map/ppermute | solution.py:154
  30.1 5.5 %collective-permute-start.5 = (bf16[32,4224]{1,0:T(8,128)(2,1)S(1)}, bf16[32,4224]{1,0:T(8,128)(2,1)}, u32[]{:S(2)}, u32[]{:S(2)}) collective-permute-start(bf16[32,4224]{1,0:T(8,128)(2,1)S(1)} %collective-permute-done.1.refs_3_), channel_id=1, source_target_pairs={{0,1},{1,0},{2,3},{3,2},{4,5},{5,4},{6,7},{7,6},{8,9},{9,8},{10,11... | collective-permute-start | bytes 811016 | tf_op jit(solution)/shard_map/ppermute | solution.py:154
  32.0 9.4 %collective-permute-start.19 = (bf16[32,4224]{1,0:T(8,128)(2,1)S(1)}, bf16[32,4224]{1,0:T(8,128)(2,1)S(1)}, u32[]{:S(2)}, u32[]{:S(2)}) collective-permute-start(bf16[32,4224]{1,0:T(8,128)(2,1)S(1)} %collective-permute-done.10.refs_2_), channel_id=1, source_target_pairs={{0,4},{1,5},{4,8},{5,9},{8,12},{9,13},{12,14},{13,15},{14,10},{15,... | collective-permute-start | bytes 811016 | tf_op jit(solution)/shard_map/ppermute | solution.py:151
  33.5 11.4 %collective-permute-start.37 = (bf16[32,4224]{1,0:T(8,128)(2,1)S(1)}, bf16[32,4224]{1,0:T(8,128)(2,1)}, u32[]{:S(2)}, u32[]{:S(2)}) collective-permute-start(bf16[32,4224]{1,0:T(8,128)(2,1)S(1)} %collective-permute-done.17.refs_0_), channel_id=1, source_target_pairs={{0,4},{1,5},{4,8},{5,9},{8,12},{9,13},{12,14},{13,15},{14,10},{15,... | collective-permute-start | bytes 811016 | tf_op jit(solution)/shard_map/ppermute | solution.py:151
  35.0 24.7 %collective-permute-start.14 = (bf16[32,4224]{1,0:T(8,128)(2,1)S(1)}, bf16[32,4224]{1,0:T(8,128)(2,1)S(1)}, u32[]{:S(2)}, u32[]{:S(2)}) collective-permute-start(bf16[32,4224]{1,0:T(8,128)(2,1)S(1)} %collective-permute-done.10.refs_2_), channel_id=1, source_target_pairs={{0,1},{1,0},{2,3},{3,2},{4,5},{5,4},{6,7},{7,6},{8,9},{9,8},{10,11... | collective-permute-start | bytes 811016 | tf_op jit(solution)/shard_map/ppermute | solution.py:154
  35.1 24.1 %collective-permute-start.20 = (bf16[32,4224]{1,0:T(8,128)(2,1)S(1)}, bf16[32,4224]{1,0:T(8,128)(2,1)S(1)}, u32[]{:S(2)}, u32[]{:S(2)}) collective-permute-start(bf16[32,4224]{1,0:T(8,128)(2,1)S(1)} %collective-permute-done.11.refs_3_), channel_id=1, source_target_pairs={{0,2},{1,3},{4,0},{5,1},{8,4},{9,5},{12,8},{13,9},{14,12},{15,13},... | collective-permute-start | bytes 811016 | tf_op jit(solution)/shard_map/ppermute | solution.py:151
  35.6 24.2 %collective-permute-start.15 = (bf16[32,4224]{1,0:T(8,128)(2,1)S(1)}, bf16[32,4224]{1,0:T(8,128)(2,1)S(1)}, u32[]{:S(2)}, u32[]{:S(2)}) collective-permute-start(bf16[32,4224]{1,0:T(8,128)(2,1)S(1)} %collective-permute-done.11.refs_3_), channel_id=1, source_target_pairs={{0,1},{1,0},{2,3},{3,2},{4,5},{5,4},{6,7},{7,6},{8,9},{9,8},{10,11... | collective-permute-start | bytes 811016 | tf_op jit(solution)/shard_map/ppermute | solution.py:154
  41.4 18.9 %collective-permute-start.38 = (bf16[32,4224]{1,0:T(8,128)(2,1)S(1)}, bf16[32,4224]{1,0:T(8,128)(2,1)S(1)}, u32[]{:S(2)}, u32[]{:S(2)}) collective-permute-start(bf16[32,4224]{1,0:T(8,128)(2,1)S(1)} %collective-permute-done.18.refs_1_), channel_id=1, source_target_pairs={{0,2},{1,3},{4,0},{5,1},{8,4},{9,5},{12,8},{13,9},{14,12},{15,13},... | collective-permute-start | bytes 811016 | tf_op jit(solution)/shard_map/ppermute | solution.py:151
  44.9 15.5 %collective-permute-start.39 = (bf16[32,4224]{1,0:T(8,128)(2,1)}, bf16[32,4224]{1,0:T(8,128)(2,1)S(1)}, u32[]{:S(2)}, u32[]{:S(2)}) collective-permute-start(bf16[32,4224]{1,0:T(8,128)(2,1)} %collective-permute-done.37.refs_0_), channel_id=1, source_target_pairs={{0,1},{1,0},{2,3},{3,2},{4,5},{5,4},{6,7},{7,6},{8,9},{9,8},{10,11... | collective-permute-start | bytes 811016 | tf_op jit(solution)/shard_map/ppermute | solution.py:154
  44.9 2.8 %copy-start = (bf16[1,4096,768]{2,1,0:T(8,128)(2,1)S(1)}, bf16[1,4096,768]{2,1,0:T(8,128)(2,1)}, u32[]{:S(2)}) copy-start(bf16[1,4096,768]{2,1,0:T(8,128)(2,1)} %param.9) | copy-start | bytes 18874372
  48.6 1.0 copy-start.6
  49.6 11.2 %copy-start.1 = (bf16[1,4096,768]{2,1,0:T(8,128)(2,1)S(1)}, bf16[1,4096,768]{2,1,0:T(8,128)(2,1)}, u32[]{:S(2)}) copy-start(bf16[1,4096,768]{2,1,0:T(8,128)(2,1)} %param.9) | copy-start | bytes 18874372
  59.2 17.8 %collective-permute-start.21 = (bf16[32,4224]{1,0:T(8,128)(2,1)S(1)}, bf16[32,4224]{1,0:T(8,128)(2,1)S(1)}, u32[]{:S(2)}, u32[]{:S(2)}) collective-permute-start(bf16[32,4224]{1,0:T(8,128)(2,1)S(1)} %collective-permute-done.17.refs_0_), channel_id=1, source_target_pairs={{0,1},{1,0},{2,3},{3,2},{4,5},{5,4},{6,7},{7,6},{8,9},{9,8},{10,11... | collective-permute-start | bytes 811016 | tf_op jit(solution)/shard_map/ppermute | solution.py:154
  59.8 19.1 %collective-permute-start.22 = (bf16[32,4224]{1,0:T(8,128)(2,1)S(1)}, bf16[32,4224]{1,0:T(8,128)(2,1)S(1)}, u32[]{:S(2)}, u32[]{:S(2)}) collective-permute-start(bf16[32,4224]{1,0:T(8,128)(2,1)S(1)} %collective-permute-done.18.refs_1_), channel_id=1, source_target_pairs={{0,1},{1,0},{2,3},{3,2},{4,5},{5,4},{6,7},{7,6},{8,9},{9,8},{10,11... | collective-permute-start | bytes 811016 | tf_op jit(solution)/shard_map/ppermute | solution.py:154
  59.8 19.3 %collective-permute-start.23 = (bf16[32,4224]{1,0:T(8,128)(2,1)S(1)}, bf16[32,4224]{1,0:T(8,128)(2,1)S(1)}, u32[]{:S(2)}, u32[]{:S(2)}) collective-permute-start(bf16[32,4224]{1,0:T(8,128)(2,1)S(1)} %collective-permute-done.19.refs_2_), channel_id=1, source_target_pairs={{0,1},{1,0},{2,3},{3,2},{4,5},{5,4},{6,7},{7,6},{8,9},{9,8},{10,11... | collective-permute-start | bytes 811016 | tf_op jit(solution)/shard_map/ppermute | solution.py:154
  60.3 18.8 %collective-permute-start.24 = (bf16[32,4224]{1,0:T(8,128)(2,1)S(1)}, bf16[32,4224]{1,0:T(8,128)(2,1)S(1)}, u32[]{:S(2)}, u32[]{:S(2)}) collective-permute-start(bf16[32,4224]{1,0:T(8,128)(2,1)S(1)} %collective-permute-done.20.refs_3_), channel_id=1, source_target_pairs={{0,1},{1,0},{2,3},{3,2},{4,5},{5,4},{6,7},{7,6},{8,9},{9,8},{10,11... | collective-permute-start | bytes 811016 | tf_op jit(solution)/shard_map/ppermute | solution.py:154
  60.4 8.6 %collective-permute-start.40 = (bf16[32,4224]{1,0:T(8,128)(2,1)S(1)}, bf16[32,4224]{1,0:T(8,128)(2,1)S(1)}, u32[]{:S(2)}, u32[]{:S(2)}) collective-permute-start(bf16[32,4224]{1,0:T(8,128)(2,1)S(1)} %collective-permute-done.38.refs_1_), channel_id=1, source_target_pairs={{0,1},{1,0},{2,3},{3,2},{4,5},{5,4},{6,7},{7,6},{8,9},{9,8},{10,11... | collective-permute-start | bytes 811016 | tf_op jit(solution)/shard_map/ppermute | solution.py:154
  69.0 84.9 %collective-permute-start.7 = (bf16[32,4096]{1,0:T(8,128)(2,1)S(1)}, bf16[32,4096]{1,0:T(8,128)(2,1)S(1)}, u32[]{:S(2)}, u32[]{:S(2)}) collective-permute-start(bf16[32,4096]{1,0:T(8,128)(2,1)S(1)} %get-tuple-element.44), channel_id=1, source_target_pairs={{0,1},{1,0},{2,3},{3,2},{4,5},{5,4},{6,7},{7,6},{8,9},{9,8},{10,11... | collective-permute-start | bytes 786440 | tf_op jit(solution)/shard_map/ppermute | solution.py:154
  77.0 10.9 %collective-permute-start.26 = (bf16[32,4224]{1,0:T(8,128)(2,1)S(1)}, bf16[32,4224]{1,0:T(8,128)(2,1)S(1)}, u32[]{:S(2)}, u32[]{:S(2)}) collective-permute-start(bf16[32,4224]{1,0:T(8,128)(2,1)S(1)} %collective-permute-done.19.refs_2_), channel_id=1, source_target_pairs={{0,4},{1,5},{4,8},{5,9},{8,12},{9,13},{12,14},{13,15},{14,10},{15,... | collective-permute-start | bytes 811016 | tf_op jit(solution)/shard_map/ppermute | solution.py:151
  78.9 9.1 %collective-permute-start.27 = (bf16[32,4224]{1,0:T(8,128)(2,1)S(1)}, bf16[32,4224]{1,0:T(8,128)(2,1)S(1)}, u32[]{:S(2)}, u32[]{:S(2)}) collective-permute-start(bf16[32,4224]{1,0:T(8,128)(2,1)S(1)} %collective-permute-done.20.refs_3_), channel_id=1, source_target_pairs={{0,2},{1,3},{4,0},{5,1},{8,4},{9,5},{12,8},{13,9},{14,12},{15,13},... | collective-permute-start | bytes 811016 | tf_op jit(solution)/shard_map/ppermute | solution.py:151
  79.1 9.3 %collective-permute-start.41 = (bf16[32,4096]{1,0:T(8,128)(2,1)S(1)}, bf16[32,4096]{1,0:T(8,128)(2,1)S(1)}, u32[]{:S(2)}, u32[]{:S(2)}) collective-permute-start(bf16[32,4096]{1,0:T(8,128)(2,1)S(1)} %get-tuple-element.56), channel_id=1, source_target_pairs={{0,1},{1,0},{2,3},{3,2},{4,5},{5,4},{6,7},{7,6},{8,9},{9,8},{10,11... | collective-permute-start | bytes 786440 | tf_op jit(solution)/shard_map/ppermute | solution.py:154
  87.3 11.5 %collective-permute-start.36 = (bf16[32,4096]{1,0:T(8,128)(2,1)S(1)}, bf16[32,4096]{1,0:T(8,128)(2,1)S(1)}, u32[]{:S(2)}, u32[]{:S(2)}) collective-permute-start(bf16[32,4096]{1,0:T(8,128)(2,1)S(1)} %get-tuple-element.54), channel_id=1, source_target_pairs={{0,1},{1,0},{2,3},{3,2},{4,5},{5,4},{6,7},{7,6},{8,9},{9,8},{10,11... | collective-permute-start | bytes 786440 | tf_op jit(solution)/shard_map/ppermute | solution.py:154
  87.9 1.5 collective-permute-start.48
  88.0 3.3 %collective-permute-start.28 = (bf16[32,4224]{1,0:T(8,128)(2,1)S(1)}, bf16[32,4224]{1,0:T(8,128)(2,1)S(1)}, u32[]{:S(2)}, u32[]{:S(2)}) collective-permute-start(bf16[32,4224]{1,0:T(8,128)(2,1)S(1)} %collective-permute-done.26.refs_0_), channel_id=1, source_target_pairs={{0,1},{1,0},{2,3},{3,2},{4,5},{5,4},{6,7},{7,6},{8,9},{9,8},{10,11... | collective-permute-start | bytes 811016 | tf_op jit(solution)/shard_map/ppermute | solution.py:154
  88.4 3.1 %collective-permute-start.29 = (bf16[32,4224]{1,0:T(8,128)(2,1)S(1)}, bf16[32,4224]{1,0:T(8,128)(2,1)S(1)}, u32[]{:S(2)}, u32[]{:S(2)}) collective-permute-start(bf16[32,4224]{1,0:T(8,128)(2,1)S(1)} %collective-permute-done.27.refs_1_), channel_id=1, source_target_pairs={{0,1},{1,0},{2,3},{3,2},{4,5},{5,4},{6,7},{7,6},{8,9},{9,8},{10,11... | collective-permute-start | bytes 811016 | tf_op jit(solution)/shard_map/ppermute | solution.py:154
  89.4 9.5 %collective-permute-start.42 = (bf16[32,4096]{1,0:T(8,128)(2,1)S(1)}, bf16[32,4096]{1,0:T(8,128)(2,1)S(1)}, u32[]{:S(2)}, u32[]{:S(2)}) collective-permute-start(bf16[32,4096]{1,0:T(8,128)(2,1)S(1)} %add_convert_fusion.11), channel_id=1, source_target_pairs={{0,4},{1,5},{4,8},{5,9},{8,12},{9,13},{12,14},{13,15},{14,10},{15,... | collective-permute-start | bytes 786440 | tf_op jit(solution)/shard_map/ppermute | solution.py:151
  91.3 77.6 %collective-permute-start.6 = (bf16[32,4096]{1,0:T(8,128)(2,1)S(1)}, bf16[32,4096]{1,0:T(8,128)(2,1)S(1)}, u32[]{:S(2)}, u32[]{:S(2)}) collective-permute-start(bf16[32,4096]{1,0:T(8,128)(2,1)S(1)} %get-tuple-element.42), channel_id=1, source_target_pairs={{0,1},{1,0},{2,3},{3,2},{4,5},{5,4},{6,7},{7,6},{8,9},{9,8},{10,11... | collective-permute-start | bytes 786440 | tf_op jit(solution)/shard_map/ppermute | solution.py:154
  91.5 72.2 %collective-permute-start.52 = (bf16[32,4096]{1,0:T(8,128)(2,1)S(1)}, bf16[32,4096]{1,0:T(8,128)(2,1)S(1)}, u32[]{:S(2)}, u32[]{:S(2)}) collective-permute-start(bf16[32,4096]{1,0:T(8,128)(2,1)S(1)} %get-tuple-element.66), channel_id=1, source_target_pairs={{0,1},{1,0},{2,3},{3,2},{4,5},{5,4},{6,7},{7,6},{8,9},{9,8},{10,11... | collective-permute-start | bytes 786440 | tf_op jit(solution)/shard_map/ppermute | solution.py:154
  98.8 1.6 collective-permute-start.47
  99.0 8.6 %collective-permute-start.49 = (bf16[32,4096]{1,0:T(8,128)(2,1)S(1)}, bf16[32,4096]{1,0:T(8,128)(2,1)S(1)}, u32[]{:S(2)}, u32[]{:S(2)}) collective-permute-start(bf16[32,4096]{1,0:T(8,128)(2,1)S(1)} %add_convert_fusion.7), channel_id=1, source_target_pairs={{0,2},{1,3},{4,0},{5,1},{8,4},{9,5},{12,8},{13,9},{14,12},{15,13},... | collective-permute-start | bytes 786440 | tf_op jit(solution)/shard_map/ppermute | solution.py:151
  100.4 11.9 %collective-permute-start.35 = (bf16[32,4096]{1,0:T(8,128)(2,1)S(1)}, bf16[32,4096]{1,0:T(8,128)(2,1)S(1)}, u32[]{:S(2)}, u32[]{:S(2)}) collective-permute-start(bf16[32,4096]{1,0:T(8,128)(2,1)S(1)} %get-tuple-element.52), channel_id=1, source_target_pairs={{0,1},{1,0},{2,3},{3,2},{4,5},{5,4},{6,7},{7,6},{8,9},{9,8},{10,11... | collective-permute-start | bytes 786440 | tf_op jit(solution)/shard_map/ppermute | solution.py:154
  107.6 1.5 collective-permute-start.30
  109.2 1.5 collective-permute-start.55
  110.7 8.3 %collective-permute-start.43 = (bf16[32,4096]{1,0:T(8,128)(2,1)S(1)}, bf16[32,4096]{1,0:T(8,128)(2,1)S(1)}, u32[]{:S(2)}, u32[]{:S(2)}) collective-permute-start(bf16[32,4096]{1,0:T(8,128)(2,1)S(1)} %add_convert_fusion.10), channel_id=1, source_target_pairs={{0,4},{1,5},{4,8},{5,9},{8,12},{9,13},{12,14},{13,15},{14,10},{15,... | collective-permute-start | bytes 786440 | tf_op jit(solution)/shard_map/ppermute | solution.py:151
  112.3 7.2 %collective-permute-start.46 = (bf16[32,4096]{1,0:T(8,128)(2,1)S(1)}, bf16[32,4096]{1,0:T(8,128)(2,1)S(1)}, u32[]{:S(2)}, u32[]{:S(2)}) collective-permute-start(bf16[32,4096]{1,0:T(8,128)(2,1)S(1)} %get-tuple-element.60), channel_id=1, source_target_pairs={{0,1},{1,0},{2,3},{3,2},{4,5},{5,4},{6,7},{7,6},{8,9},{9,8},{10,11... | collective-permute-start | bytes 786440 | tf_op jit(solution)/shard_map/ppermute | solution.py:154
  119.0 7.5 %collective-permute-start.50 = (bf16[32,4096]{1,0:T(8,128)(2,1)S(1)}, bf16[32,4096]{1,0:T(8,128)(2,1)S(1)}, u32[]{:S(2)}, u32[]{:S(2)}) collective-permute-start(bf16[32,4096]{1,0:T(8,128)(2,1)S(1)} %add_convert_fusion.6), channel_id=1, source_target_pairs={{0,2},{1,3},{4,0},{5,1},{8,4},{9,5},{12,8},{13,9},{14,12},{15,13},... | collective-permute-start | bytes 786440 | tf_op jit(solution)/shard_map/ppermute | solution.py:151
  119.5 7.5 %collective-permute-start.25 = (bf16[32,4096]{1,0:T(8,128)(2,1)S(1)}, bf16[32,4096]{1,0:T(8,128)(2,1)S(1)}, u32[]{:S(2)}, u32[]{:S(2)}) collective-permute-start(bf16[32,4096]{1,0:T(8,128)(2,1)S(1)} %get-tuple-element.48), channel_id=1, source_target_pairs={{0,1},{1,0},{2,3},{3,2},{4,5},{5,4},{6,7},{7,6},{8,9},{9,8},{10,11... | collective-permute-start | bytes 786440 | tf_op jit(solution)/shard_map/ppermute | solution.py:154
  126.6 6.6 %collective-permute-start.31 = (bf16[32,4096]{1,0:T(8,128)(2,1)S(1)}, bf16[32,4096]{1,0:T(8,128)(2,1)S(1)}, u32[]{:S(2)}, u32[]{:S(2)}) collective-permute-start(bf16[32,4096]{1,0:T(8,128)(2,1)S(1)} %add_convert_fusion.15), channel_id=1, source_target_pairs={{0,2},{1,3},{4,0},{5,1},{8,4},{9,5},{12,8},{13,9},{14,12},{15,13},... | collective-permute-start | bytes 786440 | tf_op jit(solution)/shard_map/ppermute | solution.py:151
  127.1 7.8 %collective-permute-start.54 = (bf16[32,4096]{1,0:T(8,128)(2,1)S(1)}, bf16[32,4096]{1,0:T(8,128)(2,1)S(1)}, u32[]{:S(2)}, u32[]{:S(2)}) collective-permute-start(bf16[32,4096]{1,0:T(8,128)(2,1)S(1)} %get-tuple-element.70), channel_id=1, source_target_pairs={{0,1},{1,0},{2,3},{3,2},{4,5},{5,4},{6,7},{7,6},{8,9},{9,8},{10,11... | collective-permute-start | bytes 786440 | tf_op jit(solution)/shard_map/ppermute | solution.py:154
  133.2 6.4 %collective-permute-start.56 = (bf16[32,4096]{1,0:T(8,128)(2,1)S(1)}, bf16[32,4096]{1,0:T(8,128)(2,1)S(1)}, u32[]{:S(2)}, u32[]{:S(2)}) collective-permute-start(bf16[32,4096]{1,0:T(8,128)(2,1)S(1)} %add_convert_fusion.4), channel_id=1, source_target_pairs={{0,4},{1,5},{4,8},{5,9},{8,12},{9,13},{12,14},{13,15},{14,10},{15,... | collective-permute-start | bytes 786440 | tf_op jit(solution)/shard_map/ppermute | solution.py:151
  134.8 5.2 %collective-permute-start.16 = (bf16[32,4096]{1,0:T(8,128)(2,1)S(1)}, bf16[32,4096]{1,0:T(8,128)(2,1)S(1)}, u32[]{:S(2)}, u32[]{:S(2)}) collective-permute-start(bf16[32,4096]{1,0:T(8,128)(2,1)S(1)} %get-tuple-element.46), channel_id=1, source_target_pairs={{0,1},{1,0},{2,3},{3,2},{4,5},{5,4},{6,7},{7,6},{8,9},{9,8},{10,11... | collective-permute-start | bytes 786440 | tf_op jit(solution)/shard_map/ppermute | solution.py:154
  139.5 6.4 %collective-permute-start.32 = (bf16[32,4096]{1,0:T(8,128)(2,1)S(1)}, bf16[32,4096]{1,0:T(8,128)(2,1)S(1)}, u32[]{:S(2)}, u32[]{:S(2)}) collective-permute-start(bf16[32,4096]{1,0:T(8,128)(2,1)S(1)} %add_convert_fusion.14), channel_id=1, source_target_pairs={{0,2},{1,3},{4,0},{5,1},{8,4},{9,5},{12,8},{13,9},{14,12},{15,13},... | collective-permute-start | bytes 786440 | tf_op jit(solution)/shard_map/ppermute | solution.py:151
  140.0 7.5 %collective-permute-start.53 = (bf16[32,4096]{1,0:T(8,128)(2,1)S(1)}, bf16[32,4096]{1,0:T(8,128)(2,1)S(1)}, u32[]{:S(2)}, u32[]{:S(2)}) collective-permute-start(bf16[32,4096]{1,0:T(8,128)(2,1)S(1)} %get-tuple-element.68), channel_id=1, source_target_pairs={{0,1},{1,0},{2,3},{3,2},{4,5},{5,4},{6,7},{7,6},{8,9},{9,8},{10,11... | collective-permute-start | bytes 786440 | tf_op jit(solution)/shard_map/ppermute | solution.py:154
  145.9 7.5 %collective-permute-start.57 = (bf16[32,4096]{1,0:T(8,128)(2,1)S(1)}, bf16[32,4096]{1,0:T(8,128)(2,1)S(1)}, u32[]{:S(2)}, u32[]{:S(2)}) collective-permute-start(bf16[32,4096]{1,0:T(8,128)(2,1)S(1)} %add_convert_fusion.3), channel_id=1, source_target_pairs={{0,4},{1,5},{4,8},{5,9},{8,12},{9,13},{12,14},{13,15},{14,10},{15,... | collective-permute-start | bytes 786440 | tf_op jit(solution)/shard_map/ppermute | solution.py:151
  147.6 27.7 %collective-permute-start.45 = (bf16[32,4096]{1,0:T(8,128)(2,1)S(1)}, bf16[32,4096]{1,0:T(8,128)(2,1)S(1)}, u32[]{:S(2)}, u32[]{:S(2)}) collective-permute-start(bf16[32,4096]{1,0:T(8,128)(2,1)S(1)} %get-tuple-element.58), channel_id=1, source_target_pairs={{0,1},{1,0},{2,3},{3,2},{4,5},{5,4},{6,7},{7,6},{8,9},{9,8},{10,11... | collective-permute-start | bytes 786440 | tf_op jit(solution)/shard_map/ppermute | solution.py:154
  153.4 8.6 %collective-permute-start.33 = (bf16[32,4096]{1,0:T(8,128)(2,1)S(1)}, bf16[32,4096]{1,0:T(8,128)(2,1)S(1)}, u32[]{:S(2)}, u32[]{:S(2)}) collective-permute-start(bf16[32,4096]{1,0:T(8,128)(2,1)S(1)} %add_convert_fusion.13), channel_id=1, source_target_pairs={{0,2},{1,3},{4,0},{5,1},{8,4},{9,5},{12,8},{13,9},{14,12},{15,13},... | collective-permute-start | bytes 786440 | tf_op jit(solution)/shard_map/ppermute | solution.py:151
  153.9 17.1 %collective-permute-start.44 = (bf16[32,4096]{1,0:T(8,128)(2,1)S(1)}, bf16[32,4096]{1,0:T(8,128)(2,1)S(1)}, u32[]{:S(2)}, u32[]{:S(2)}) collective-permute-start(bf16[32,4096]{1,0:T(8,128)(2,1)S(1)} %add_convert_fusion.9), channel_id=1, source_target_pairs={{0,4},{1,5},{4,8},{5,9},{8,12},{9,13},{12,14},{13,15},{14,10},{15,... | collective-permute-start | bytes 786440 | tf_op jit(solution)/shard_map/ppermute | solution.py:151
  162.0 6.7 %collective-permute-start.58 = (bf16[32,4096]{1,0:T(8,128)(2,1)S(1)}, bf16[32,4096]{1,0:T(8,128)(2,1)S(1)}, u32[]{:S(2)}, u32[]{:S(2)}) collective-permute-start(bf16[32,4096]{1,0:T(8,128)(2,1)S(1)} %add_convert_fusion.2), channel_id=1, source_target_pairs={{0,4},{1,5},{4,8},{5,9},{8,12},{9,13},{12,14},{13,15},{14,10},{15,... | collective-permute-start | bytes 786440 | tf_op jit(solution)/shard_map/ppermute | solution.py:151
  163.7 11.6 %collective-permute-start.51 = (bf16[32,4096]{1,0:T(8,128)(2,1)S(1)}, bf16[32,4096]{1,0:T(8,128)(2,1)S(1)}, u32[]{:S(2)}, u32[]{:S(2)}) collective-permute-start(bf16[32,4096]{1,0:T(8,128)(2,1)S(1)} %add_convert_fusion.5), channel_id=1, source_target_pairs={{0,2},{1,3},{4,0},{5,1},{8,4},{9,5},{12,8},{13,9},{14,12},{15,13},... | collective-permute-start | bytes 786440 | tf_op jit(solution)/shard_map/ppermute | solution.py:151
  168.7 6.4 %collective-permute-start.34 = (bf16[32,4096]{1,0:T(8,128)(2,1)S(1)}, bf16[32,4096]{1,0:T(8,128)(2,1)S(1)}, u32[]{:S(2)}, u32[]{:S(2)}) collective-permute-start(bf16[32,4096]{1,0:T(8,128)(2,1)S(1)} %add_convert_fusion.12), channel_id=1, source_target_pairs={{0,2},{1,3},{4,0},{5,1},{8,4},{9,5},{12,8},{13,9},{14,12},{15,13},... | collective-permute-start | bytes 786440 | tf_op jit(solution)/shard_map/ppermute | solution.py:151
  168.9 6.4 %collective-permute-start.59 = (bf16[32,4096]{1,0:T(8,128)(2,1)S(1)}, bf16[32,4096]{1,0:T(8,128)(2,1)S(1)}, u32[]{:S(2)}, u32[]{:S(2)}) collective-permute-start(bf16[32,4096]{1,0:T(8,128)(2,1)S(1)} %add_convert_fusion.1), channel_id=1, source_target_pairs={{0,4},{1,5},{4,8},{5,9},{8,12},{9,13},{12,14},{13,15},{14,10},{15,... | collective-permute-start | bytes 786440 | tf_op jit(solution)/shard_map/ppermute | solution.py:151
  (3 other events, 2.4 us)

commit v2 on v1

v2 whole, which is shorter than its diff:
```python
import functools

import jax
import jax.numpy as jnp
from jax import lax
from jax.experimental import pallas as pl
from jax.experimental.pallas import tpu as pltpu
from jax.sharding import PartitionSpec as P

LANES = 128
FF_TILE = 256
OUT_TILE = 512
MIB = 1 << 20


def encode_kernel(tokens_ref, routes_ref, codes_ref, out_ref):
    rows, width = tokens_ref.shape
    for b in range(width // LANES):
        cols = slice(b * LANES, (b + 1) * LANES)
        block = tokens_ref[:, cols].astype(jnp.float32)
        largest = jnp.max(jnp.abs(block), axis=1, keepdims=True)
        scale = ((largest + 1e-6) / 448.0).astype(jnp.bfloat16).astype(jnp.float32)
        coded = (block / scale).astype(jnp.bfloat16).astype(jnp.float32)
        out_ref[:, cols] = (coded * scale).astype(jnp.bfloat16)
    lane = lax.broadcasted_iota(jnp.int32, (rows, LANES), 1)
    table = jnp.zeros((rows, LANES), jnp.float32)
    for k in range(routes_ref.shape[1]):
        code = codes_ref[:, k : k + 1].astype(jnp.float32)
        table = table + jnp.where(lane == routes_ref[:, k : k + 1], code, 0.0)
    out_ref[:, width:] = table.astype(jnp.bfloat16)


def encode(tokens, routes, gate_codes):
    rows, width = tokens.shape
    return pl.pallas_call(
        encode_kernel,
        out_shape=jax.ShapeDtypeStruct((rows, width + LANES), jnp.bfloat16),
        compiler_params=pltpu.CompilerParams(vmem_limit_bytes=8 * MIB),
    )(tokens, routes, gate_codes)


def expert_kernel(count, me_ref, *refs):
    x_refs = refs[:count]
    gate_w, up_w, down_w = refs[count : count + 3]
    own_out, other_out = refs[count + 3 : count + 5]
    x, hidden, scale = refs[count + 5 :]
    width, ff = gate_w.shape
    half = own_out.shape[0]

    rows = x_refs[0].shape[0]
    lane = lax.broadcasted_iota(jnp.int32, (rows, LANES), 1)
    for i, ref in enumerate(x_refs):
        span = slice(i * rows, (i + 1) * rows)
        x[span, :] = ref[:, :width]
        codes = ref[:, width:].astype(jnp.float32)
        total = jnp.sum(codes, axis=1, keepdims=True)
        mine = jnp.sum(jnp.where(lane == me_ref[0], codes, 0.0), axis=1, keepdims=True)
        scale[span, :] = jnp.broadcast_to(mine / total, (rows, LANES))

    @pl.loop(0, ff // FF_TILE)
    def _(t):
        cols = pl.ds(pl.multiple_of(t * FF_TILE, FF_TILE), FF_TILE)
        gate = jnp.dot(x[...], gate_w[:, cols], preferred_element_type=jnp.float32)
        up = jnp.dot(x[...], up_w[:, cols], preferred_element_type=jnp.float32)
        hidden[:, cols] = (gate / (1.0 + jnp.exp(-gate)) * up).astype(jnp.bfloat16)

    @pl.loop(0, width // OUT_TILE)
    def _(t):
        cols = pl.ds(pl.multiple_of(t * OUT_TILE, OUT_TILE), OUT_TILE)
        result = jnp.dot(hidden[...], down_w[:, cols], preferred_element_type=jnp.float32)
        result = (result * scale[:, 0:1]).astype(jnp.bfloat16)
        own_out[:, cols] = result[:half]
        other_out[:, cols] = result[half:]


def expert(me, own, other, weights):
    blocks = [*own, *other]
    rows = blocks[0].shape[0]
    width, ff = weights[0].shape
    half = rows * len(own)
    out = jax.ShapeDtypeStruct((half, width), jnp.bfloat16)
    vmem = pl.BlockSpec(memory_space=pltpu.VMEM)
    pinned = [pltpu.with_memory_space_constraint(w, pltpu.VMEM) for w in weights]
    return pl.pallas_call(
        functools.partial(expert_kernel, len(blocks)),
        in_specs=[pl.BlockSpec(memory_space=pltpu.SMEM)] + [vmem] * (len(blocks) + 3),
        out_specs=[vmem, vmem],
        out_shape=[out, out],
        scratch_shapes=[
            pltpu.VMEM((2 * half, width), jnp.bfloat16),
            pltpu.VMEM((2 * half, ff), jnp.bfloat16),
            pltpu.VMEM((2 * half, LANES), jnp.float32),
        ],
        cost_estimate=pl.CostEstimate(
            flops=12 * half * width * ff,
            bytes_accessed=8 * half * width,
            transcendentals=2 * half * ff,
        ),
        compiler_params=pltpu.CompilerParams(vmem_limit_bytes=16 * MIB),
    )(me, *blocks, *pinned)


def ring_order(nodes, groups):
    chips = nodes // 2
    if groups == 2:
        return list(range(0, chips, 2)) + list(range(1, chips, 2))[::-1]
    return list(range(chips))


def after(value, *others):
    return lax.optimization_barrier((value, *others))[0]


def add(*terms):
    return functools.reduce(lambda a, b: a + b, [t.astype(jnp.float32) for t in terms])


def local(nodes, groups, tokens, routes, gate_codes, w_gate, w_up, w_down):
    order = ring_order(nodes, groups)
    chips = len(order)
    far = chips // 2
    rows = tokens.shape[0]
    node = lax.axis_index("node").astype(jnp.int32)
    first_core = (node % 2) == 0
    me = node.reshape(1)
    weights = (w_gate[0], w_up[0], w_down[0])

    def hop(value, *steps):
        steps = steps * (3 - len(steps))
        pairs = [
            (2 * order[i] + core, 2 * order[(i + steps[core]) % chips] + core)
            for i in range(chips)
            for core in (0, 1)
        ]
        return lax.ppermute(value, "node", pairs)

    def swap(value):
        return lax.ppermute(value, "node", [(i, i ^ 1) for i in range(nodes)])

    block = encode(tokens, routes, gate_codes)
    batches = [[block]]
    for s in range(1, far):
        batches.append([hop(batches[-1][0], 1), hop(batches[-1][-1], -1)])
    batches.append([hop(jnp.where(first_core, batches[-1][0], batches[-1][-1]), 1, -1)])

    mine, theirs = [], []
    for batch in batches:
        outs = expert(me, batch, [swap(b) for b in batch], weights)
        mine.append(outs[0])
        theirs.append(swap(outs[1]))

    def part(s, behind):
        span = slice(rows, None) if behind else slice(0, rows)
        return add(mine[s][span], theirs[s][span])

    low = jnp.bfloat16
    edge = hop(add(mine[far], theirs[far]).astype(low), -1, 1)
    up, down = None, None
    for s in range(far - 1, 0, -1):
        if up is None:
            up = part(s, False) + jnp.where(first_core, edge, 0).astype(jnp.float32)
            down = part(s, True) + jnp.where(first_core, 0, edge).astype(jnp.float32)
        else:
            up, down = part(s, False) + up.astype(jnp.float32), part(s, True) + down.astype(jnp.float32)
        up, down = hop(up.astype(low), -1), hop(down.astype(low), 1)
    return add(mine[0], theirs[0], up, down).astype(low)


def solution(mesh):
    return jax.shard_map(
        functools.partial(local, mesh.shape["node"], mesh.shape["groups"]),
        mesh=mesh,
        in_specs=(
            P(("groups", "node"), None),
            P(("groups", "node"), None),
            P(("groups", "node"), None),
            P("node", None, None),
            P("node", None, None),
            P("node", None, None),
        ),
        out_specs=P(("groups", "node"), None),
        check_vma=False,
    )
```

time: 177 us -> 133 us (0.75)
  waiting for transfers between devices: 86.2 us -> 67.5 us
  starting transfers between devices: 37.4 us -> 19.3 us
  Pallas kernels: 41.3 us -> 32.6 us
  local copies, waits for them, and re-layouts: 8.69 us -> 10.9 us
    ppermute x28 -> x14, starting transfers between devices: 32.7 us -> 15.6 us  [hop(): return lax.ppermute(value, 'node', pairs)]
    ppermute x28 -> x14, waiting for transfers between devices: 81.9 us -> 66 us  [hop(): return lax.ppermute(value, 'node', pairs)]
    pallas_call x6, Pallas kernels: 41.3 us -> 32.6 us  [the longest x5 32 us: expert(): pl.pallas_call(functools.partial(expert_kernel, len(blocks)), in_specs=[p...]
    ppermute x32 -> x13, waiting for transfers between devices: 4.27 us -> 1.45 us  [swap(): return lax.ppermute(value, 'node', [(i, i ^ 1) for i in range(nodes)])]
    unnamed x16 -> x12, local copies, waits for them, and re-layouts: 8.69 us -> 10.9 us
    ppermute x32 -> x13, starting transfers between devices: 4.77 us -> 3.71 us  [swap(): return lax.ppermute(value, 'node', [(i, i ^ 1) for i in range(nodes)])]
  transfers between devices with their start and end apart: 60 -> 27, of which waited for: 24 -> 12; matrix products, arithmetic and copies ran while one was open for 1% -> 1% of each run, Pallas kernels for 23% -> 24%
where the time goes in v2:
time: 133 us
  waiting for transfers between devices  67.5 us (51%)
  Pallas kernels  32.6 us (25%)
  starting transfers between devices  19.3 us (15%)
  local copies, waits for them, and re-layouts  10.9 us (8%)
  other arithmetic  2.6 us (2%)
    ppermute x14, waiting for transfers between devices, hop(): return lax.ppermute(value, 'node', pairs)  66 us
    pallas_call x5, Pallas kernels, expert(): pl.pallas_call(functools.partial(expert_kernel, len(blocks)), in_specs=[p...  32 us
    ppermute x14, starting transfers between devices, hop(): return lax.ppermute(value, 'node', pairs)  15.6 us
    unnamed x12, local copies, waits for them, and re-layouts  10.9 us
    ppermute x13, starting transfers between devices, swap(): return lax.ppermute(value, 'node', [(i, i ^ 1) for i in range(nodes)])  3.71 us
  transfers between devices with their start and end apart: 27, of which 12 were waited for; matrix products, arithmetic and copies ran while one was open for 1% of the time, Pallas kernels for 24%

profile of v2, /device:TPU:0, one launch (start us, length us, event | category | flops | bytes accessed | tf_op | source)
XLA Modules:
  0.0 133.1 jit_solution(15377836814365439963)
XLA Ops:
  0.0 0.8 copy.7.routes_ref
  0.8 0.8 copy.8.codes_ref
  1.5 1.0 copy-done.4
  2.6 0.6 shard_map.64.refs_0_
  3.2 3.1 %collective-permute-start.2 = (bf16[64,4224]{1,0:T(8,128)(2,1)S(1)}, bf16[64,4224]{1,0:T(8,128)(2,1)S(1)}, u32[]{:S(2)}, u32[]{:S(2)}) collective-permute-start(bf16[64,4224]{1,0:T(8,128)(2,1)S(1)} %shard_map.64.refs_0_), channel_id=1, source_target_pairs={{0,4},{1,5},{4,8},{5,9},{8,12},{9,13},{12,14},{13,15},{14,10},{15,... | collective-permute-start | bytes 1622024 | tf_op jit(solution)/shard_map/ppermute | solution.py:135
  6.3 0.0 collective-permute-start.3
  6.3 12.2 %collective-permute-done.2.refs_0_ = bf16[64,4224]{1,0:T(8,128)(2,1)S(1)} collective-permute-done((bf16[64,4224]{1,0:T(8,128)(2,1)S(1)}, bf16[64,4224]{1,0:T(8,128)(2,1)S(1)}, u32[]{:S(2)}, u32[]{:S(2)}) %collective-permute-start.2) | collective-permute-done | bytes 540704 | tf_op jit(solution)/shard_map/ppermute | solution.py:135
  18.5 1.8 %collective-permute-start.7 = (bf16[64,4224]{1,0:T(8,128)(2,1)S(1)}, bf16[64,4224]{1,0:T(8,128)(2,1)S(1)}, u32[]{:S(2)}, u32[]{:S(2)}) collective-permute-start(bf16[64,4224]{1,0:T(8,128)(2,1)S(1)} %collective-permute-done.2.refs_0_), channel_id=1, source_target_pairs={{0,4},{1,5},{4,8},{5,9},{8,12},{9,13},{12,14},{13,15},{14,10},{15,... | collective-permute-start | bytes 1622024 | tf_op jit(solution)/shard_map/ppermute | solution.py:135
  20.3 0.0 collective-permute-done.3.refs_1_
  20.3 0.2 collective-permute-start.8
  20.5 11.4 %collective-permute-done.7.refs_0_ = bf16[64,4224]{1,0:T(8,128)(2,1)S(1)} collective-permute-done((bf16[64,4224]{1,0:T(8,128)(2,1)S(1)}, bf16[64,4224]{1,0:T(8,128)(2,1)S(1)}, u32[]{:S(2)}, u32[]{:S(2)}) %collective-permute-start.7) | collective-permute-done | bytes 540704 | tf_op jit(solution)/shard_map/ppermute | solution.py:135
  31.9 1.5 %collective-permute-start.12 = (bf16[64,4224]{1,0:T(8,128)(2,1)S(1)}, bf16[64,4224]{1,0:T(8,128)(2,1)S(1)}, u32[]{:S(2)}, u32[]{:S(2)}) collective-permute-start(bf16[64,4224]{1,0:T(8,128)(2,1)S(1)} %collective-permute-done.7.refs_0_), channel_id=1, source_target_pairs={{0,4},{1,5},{4,8},{5,9},{8,12},{9,13},{12,14},{13,15},{14,10},{15,... | collective-permute-start | bytes 1622024 | tf_op jit(solution)/shard_map/ppermute | solution.py:135
  33.4 0.5 collective-permute-start.13
  34.0 10.6 %collective-permute-done.12.refs_0_ = bf16[64,4224]{1,0:T(8,128)(2,1)S(1)} collective-permute-done((bf16[64,4224]{1,0:T(8,128)(2,1)S(1)}, bf16[64,4224]{1,0:T(8,128)(2,1)S(1)}, u32[]{:S(2)}, u32[]{:S(2)}) %collective-permute-start.12) | collective-permute-done | bytes 540704 | tf_op jit(solution)/shard_map/ppermute | solution.py:135
  44.6 1.4 %collective-permute-done.13.refs_1_ = bf16[64,4224]{1,0:T(8,128)(2,1)S(1)} collective-permute-done((bf16[64,4224]{1,0:T(8,128)(2,1)}, bf16[64,4224]{1,0:T(8,128)(2,1)S(1)}, u32[]{:S(2)}, u32[]{:S(2)}) %collective-permute-start.13) | collective-permute-done | bytes 540704 | tf_op jit(solution)/shard_map/ppermute | solution.py:135
  46.0 0.1 broadcast_select_fusion
  46.0 1.6 %collective-permute-start.17 = (bf16[64,4224]{1,0:T(8,128)(2,1)S(1)}, bf16[64,4224]{1,0:T(8,128)(2,1)S(1)}, u32[]{:S(2)}, u32[]{:S(2)}) collective-permute-start(bf16[64,4224]{1,0:T(8,128)(2,1)S(1)} %broadcast_select_fusion), channel_id=1, source_target_pairs={{0,4},{1,3},{4,8},{5,1},{8,12},{9,5},{12,14},{13,9},{14,10},{15,13... | collective-permute-start | bytes 1622024 | tf_op jit(solution)/shard_map/ppermute | solution.py:135
  47.7 7.8 %collective-permute-done.17.refs_0_ = bf16[64,4224]{1,0:T(8,128)(2,1)S(1)} collective-permute-done((bf16[64,4224]{1,0:T(8,128)(2,1)S(1)}, bf16[64,4224]{1,0:T(8,128)(2,1)S(1)}, u32[]{:S(2)}, u32[]{:S(2)}) %collective-permute-start.17) | collective-permute-done | bytes 540704 | tf_op jit(solution)/shard_map/ppermute | solution.py:135
  55.4 0.0 collective-permute-start.18
  55.4 0.5 collective-permute-start.14
  56.0 0.0 collective-permute-start.15
  56.0 1.4 %collective-permute-done.18.refs_1_ = bf16[64,4224]{1,0:T(8,128)(2,1)S(1)} collective-permute-done((bf16[64,4224]{1,0:T(8,128)(2,1)S(1)}, bf16[64,4224]{1,0:T(8,128)(2,1)S(1)}, u32[]{:S(2)}, u32[]{:S(2)}) %collective-permute-start.18) | collective-permute-done | bytes 540704 | tf_op jit(solution)/shard_map/ppermute | solution.py:138
  57.4 2.8 %copy-done = bf16[1,4096,768]{2,1,0:T(8,128)(2,1)S(1)} copy-done((bf16[1,4096,768]{2,1,0:T(8,128)(2,1)S(1)}, bf16[1,4096,768]{2,1,0:T(8,128)(2,1)}, u32[]{:S(2)}) %copy-start) | copy-done | bytes 6291480
  60.2 2.8 %copy-done.2 = bf16[1,4096,768]{2,1,0:T(8,128)(2,1)S(1)} copy-done((bf16[1,4096,768]{2,1,0:T(8,128)(2,1)S(1)}, bf16[1,4096,768]{2,1,0:T(8,128)(2,1)}, u32[]{:S(2)}) %copy-start.2) | copy-done | bytes 6291480
  62.9 2.8 %copy-done.3 = bf16[1,768,4096]{2,1,0:T(8,128)(2,1)S(1)} copy-done((bf16[1,768,4096]{2,1,0:T(8,128)(2,1)S(1)}, bf16[1,768,4096]{2,1,0:T(8,128)(2,1)}, u32[]{:S(2)}) %copy-start.3) | copy-done | bytes 6291480
  65.7 4.7 %shard_map.69 = (bf16[64,4096]{1,0:T(8,128)(2,1)S(1)}, bf16[64,4096]{1,0:T(8,128)(2,1)S(1)}) custom-call(s32[1]{0:T(128)} %bitcast.me_ref, bf16[64,4224]{1,0:T(8,128)(2,1)S(1)} %collective-permute-done.17.refs_0_, bf16[64,4224]{1,0:T(8,128)(2,1)S(1)} %collective-permute-done.18.refs_1_, bf16[4096,768]{1,0:T(8,128)(2,1)S(1)} %bitcast.4, ...), custom_call_target="tpu_custom_call" | custom-call | flops 2415919104 | bytes 2097152 | tf_op jit(solution)/shard_map/pallas_call | solution.py:84
  70.5 0.2 collective-permute-start.19
  70.6 0.4 collective-permute-start.9
  71.0 0.1 collective-permute-start.10
  71.2 0.0 collective-permute-done.14.refs_2_
  71.2 0.0 collective-permute-done.15.refs_3_
  71.2 7.2 %shard_map.68 = (bf16[128,4096]{1,0:T(8,128)(2,1)S(1)}, bf16[128,4096]{1,0:T(8,128)(2,1)S(1)}) custom-call(s32[1]{0:T(128)} %bitcast.me_ref, bf16[64,4224]{1,0:T(8,128)(2,1)S(1)} %collective-permute-done.12.refs_0_, bf16[64,4224]{1,0:T(8,128)(2,1)S(1)} %collective-permute-done.13.refs_1_, bf16[64,4224]{1,0:T(8,128)(2,1)S(1)} %collective-permute-done.14.refs_2_, ...), custom_call_target="tpu_custom_call" | custom-call | flops 4831838208 | bytes 4194304 | tf_op jit(solution)/shard_map/pallas_call | solution.py:84
  78.3 0.4 collective-permute-start.16
  78.8 0.0 collective-permute-done.19
  78.8 0.1 add_convert_fusion.7
  78.9 0.6 collective-permute-start.20
  79.6 0.8 collective-permute-start.4
  80.4 0.0 collective-permute-done.9.refs_2_
  80.4 0.0 collective-permute-start.5
  80.4 8.2 %shard_map.67 = (bf16[128,4096]{1,0:T(8,128)(2,1)S(1)}, bf16[128,4096]{1,0:T(8,128)(2,1)S(1)}) custom-call(s32[1]{0:T(128)} %bitcast.me_ref, bf16[64,4224]{1,0:T(8,128)(2,1)S(1)} %collective-permute-done.7.refs_0_, bf16[64,4224]{1,0:T(8,128)(2,1)} %collective-permute-done.8.refs_1_, bf16[64,4224]{1,0:T(8,128)(2,1)S(1)} %collective-permute-done.9.refs_2_, ...), custom_call_target="tpu_custom_call" | custom-call | flops 4831838208 | bytes 4194304 | tf_op jit(solution)/shard_map/pallas_call | solution.py:84
  88.7 0.6 collective-permute-start.11
  89.2 0.0 collective-permute-done.16
  89.3 0.0 collective-permute-done.20
  89.3 0.4 add_convert_fusion.6
  89.7 0.6 collective-permute-start.21
  90.3 1.4 %collective-permute-start.24 = (bf16[64,4096]{1,0:T(8,128)(2,1)S(1)}, bf16[64,4096]{1,0:T(8,128)(2,1)S(1)}, u32[]{:S(2)}, u32[]{:S(2)}) collective-permute-start(bf16[64,4096]{1,0:T(8,128)(2,1)S(1)} %get-tuple-element.26), channel_id=1, source_target_pairs={{0,4},{1,5},{4,8},{5,9},{8,12},{9,13},{12,14},{13,15},{14,10},{15,... | collective-permute-start | bytes 1572872 | tf_op jit(solution)/shard_map/ppermute | solution.py:135
  91.8 0.0 collective-permute-start
  91.8 7.2 %shard_map.66 = (bf16[128,4096]{1,0:T(8,128)(2,1)S(1)}, bf16[128,4096]{1,0:T(8,128)(2,1)S(1)}) custom-call(s32[1]{0:T(128)} %bitcast.me_ref, bf16[64,4224]{1,0:T(8,128)(2,1)S(1)} %collective-permute-done.2.refs_0_, bf16[64,4224]{1,0:T(8,128)(2,1)S(1)} %collective-permute-done.3.refs_1_, bf16[64,4224]{1,0:T(8,128)(2,1)S(1)} %collective-permute-done.4.refs_2_, ...), custom_call_target="tpu_custom_call" | custom-call | flops 4831838208 | bytes 4194304 | tf_op jit(solution)/shard_map/pallas_call | solution.py:84
  98.9 0.6 collective-permute-start.6
  99.5 4.1 %collective-permute-done.21 = bf16[64,4096]{1,0:T(8,128)(2,1)S(1)} collective-permute-done((bf16[64,4096]{1,0:T(8,128)(2,1)S(1)}, bf16[64,4096]{1,0:T(8,128)(2,1)S(1)}, u32[]{:S(2)}, u32[]{:S(2)}) %collective-permute-start.21) | collective-permute-done | bytes 524320 | tf_op jit(solution)/shard_map/ppermute | solution.py:135
  103.6 0.7 collective-permute-done.24
  104.3 0.5 add_convert_fusion.5
  104.8 1.6 %collective-permute-start.22 = (bf16[64,4096]{1,0:T(8,128)(2,1)S(1)}, bf16[64,4096]{1,0:T(8,128)(2,1)S(1)}, u32[]{:S(2)}, u32[]{:S(2)}) collective-permute-start(bf16[64,4096]{1,0:T(8,128)(2,1)S(1)} %get-tuple-element.29), channel_id=1, source_target_pairs={{0,2},{1,3},{4,0},{5,1},{8,4},{9,5},{12,8},{13,9},{14,12},{15,13},... | collective-permute-start | bytes 1572872 | tf_op jit(solution)/shard_map/ppermute | solution.py:135
  106.4 0.4 collective-permute-start.25
  106.9 4.7 %shard_map.65 = (bf16[64,4096]{1,0:T(8,128)(2,1)S(1)}, bf16[64,4096]{1,0:T(8,128)(2,1)S(1)}) custom-call(s32[1]{0:T(128)} %bitcast.me_ref, bf16[64,4224]{1,0:T(8,128)(2,1)S(1)} %shard_map.64.refs_0_, bf16[64,4224]{1,0:T(8,128)(2,1)S(1)} %collective-permute-done.refs_1_, bf16[4096,768]{1,0:T(8,128)(2,1)S(1)} %bitcast.8, bf16[4096,768]{1,0:T(8,128)(2,1)S(1)} %bitcast.13, ...), custom_call_target="tpu_custom_call" | custom-call | flops 2415919104 | bytes 2097152 | tf_op jit(solution)/shard_map/pallas_call | solution.py:84
  111.6 0.1 collective-permute-start.1
  111.7 6.4 %collective-permute-done.22 = bf16[64,4096]{1,0:T(8,128)(2,1)S(1)} collective-permute-done((bf16[64,4096]{1,0:T(8,128)(2,1)S(1)}, bf16[64,4096]{1,0:T(8,128)(2,1)S(1)}, u32[]{:S(2)}, u32[]{:S(2)}) %collective-permute-start.22) | collective-permute-done | bytes 524320 | tf_op jit(solution)/shard_map/ppermute | solution.py:135
  118.0 1.3 collective-permute-done.25
  119.3 0.5 add_convert_fusion.4
  119.8 0.5 collective-permute-start.26
  120.3 1.6 %collective-permute-start.23 = (bf16[64,4096]{1,0:T(8,128)(2,1)S(1)}, bf16[64,4096]{1,0:T(8,128)(2,1)S(1)}, u32[]{:S(2)}, u32[]{:S(2)}) collective-permute-start(bf16[64,4096]{1,0:T(8,128)(2,1)S(1)} %get-tuple-element.27), channel_id=1, source_target_pairs={{0,2},{1,3},{4,0},{5,1},{8,4},{9,5},{12,8},{13,9},{14,12},{15,13},... | collective-permute-start | bytes 1572872 | tf_op jit(solution)/shard_map/ppermute | solution.py:135
  121.9 10.0 %collective-permute-done.26 = bf16[64,4096]{1,0:T(8,128)(2,1)S(1)} collective-permute-done((bf16[64,4096]{1,0:T(8,128)(2,1)S(1)}, bf16[64,4096]{1,0:T(8,128)(2,1)S(1)}, u32[]{:S(2)}, u32[]{:S(2)}) %collective-permute-start.26) | collective-permute-done | bytes 524320 | tf_op jit(solution)/shard_map/ppermute | solution.py:135
  131.9 0.2 collective-permute-done.23
  132.1 1.1 add_convert_fusion
  (14 shorter events, 0.0 us)
Async XLA Ops:
  1.5 1.0 copy-start.4
  3.2 15.3 %collective-permute-start.2 = (bf16[64,4224]{1,0:T(8,128)(2,1)S(1)}, bf16[64,4224]{1,0:T(8,128)(2,1)S(1)}, u32[]{:S(2)}, u32[]{:S(2)}) collective-permute-start(bf16[64,4224]{1,0:T(8,128)(2,1)S(1)} %shard_map.64.refs_0_), channel_id=1, source_target_pairs={{0,4},{1,5},{4,8},{5,9},{8,12},{9,13},{12,14},{13,15},{14,10},{15,... | collective-permute-start | bytes 1622024 | tf_op jit(solution)/shard_map/ppermute | solution.py:135
  6.3 14.0 %collective-permute-start.3 = (bf16[64,4224]{1,0:T(8,128)(2,1)S(1)}, bf16[64,4224]{1,0:T(8,128)(2,1)S(1)}, u32[]{:S(2)}, u32[]{:S(2)}) collective-permute-start(bf16[64,4224]{1,0:T(8,128)(2,1)S(1)} %shard_map.64.refs_0_), channel_id=1, source_target_pairs={{0,2},{1,3},{4,0},{5,1},{8,4},{9,5},{12,8},{13,9},{14,12},{15,13},... | collective-permute-start | bytes 1622024 | tf_op jit(solution)/shard_map/ppermute | solution.py:135
  18.5 13.5 %collective-permute-start.7 = (bf16[64,4224]{1,0:T(8,128)(2,1)S(1)}, bf16[64,4224]{1,0:T(8,128)(2,1)S(1)}, u32[]{:S(2)}, u32[]{:S(2)}) collective-permute-start(bf16[64,4224]{1,0:T(8,128)(2,1)S(1)} %collective-permute-done.2.refs_0_), channel_id=1, source_target_pairs={{0,4},{1,5},{4,8},{5,9},{8,12},{9,13},{12,14},{13,15},{14,10},{15,... | collective-permute-start | bytes 1622024 | tf_op jit(solution)/shard_map/ppermute | solution.py:135
  20.3 13.1 %collective-permute-start.8 = (bf16[64,4224]{1,0:T(8,128)(2,1)S(1)}, bf16[64,4224]{1,0:T(8,128)(2,1)}, u32[]{:S(2)}, u32[]{:S(2)}) collective-permute-start(bf16[64,4224]{1,0:T(8,128)(2,1)S(1)} %collective-permute-done.3.refs_1_), channel_id=1, source_target_pairs={{0,2},{1,3},{4,0},{5,1},{8,4},{9,5},{12,8},{13,9},{14,12},{15,13},... | collective-permute-start | bytes 1622024 | tf_op jit(solution)/shard_map/ppermute | solution.py:135
  31.9 12.6 %collective-permute-start.12 = (bf16[64,4224]{1,0:T(8,128)(2,1)S(1)}, bf16[64,4224]{1,0:T(8,128)(2,1)S(1)}, u32[]{:S(2)}, u32[]{:S(2)}) collective-permute-start(bf16[64,4224]{1,0:T(8,128)(2,1)S(1)} %collective-permute-done.7.refs_0_), channel_id=1, source_target_pairs={{0,4},{1,5},{4,8},{5,9},{8,12},{9,13},{12,14},{13,15},{14,10},{15,... | collective-permute-start | bytes 1622024 | tf_op jit(solution)/shard_map/ppermute | solution.py:135
  33.4 12.5 %collective-permute-start.13 = (bf16[64,4224]{1,0:T(8,128)(2,1)}, bf16[64,4224]{1,0:T(8,128)(2,1)S(1)}, u32[]{:S(2)}, u32[]{:S(2)}) collective-permute-start(bf16[64,4224]{1,0:T(8,128)(2,1)} %collective-permute-done.8.refs_1_), channel_id=1, source_target_pairs={{0,2},{1,3},{4,0},{5,1},{8,4},{9,5},{12,8},{13,9},{14,12},{15,13},... | collective-permute-start | bytes 1622024 | tf_op jit(solution)/shard_map/ppermute | solution.py:135
  46.0 9.4 %collective-permute-start.17 = (bf16[64,4224]{1,0:T(8,128)(2,1)S(1)}, bf16[64,4224]{1,0:T(8,128)(2,1)S(1)}, u32[]{:S(2)}, u32[]{:S(2)}) collective-permute-start(bf16[64,4224]{1,0:T(8,128)(2,1)S(1)} %broadcast_select_fusion), channel_id=1, source_target_pairs={{0,4},{1,3},{4,8},{5,1},{8,12},{9,5},{12,14},{13,9},{14,10},{15,13... | collective-permute-start | bytes 1622024 | tf_op jit(solution)/shard_map/ppermute | solution.py:135
  55.4 1.9 %collective-permute-start.18 = (bf16[64,4224]{1,0:T(8,128)(2,1)S(1)}, bf16[64,4224]{1,0:T(8,128)(2,1)S(1)}, u32[]{:S(2)}, u32[]{:S(2)}) collective-permute-start(bf16[64,4224]{1,0:T(8,128)(2,1)S(1)} %collective-permute-done.17.refs_0_), channel_id=1, source_target_pairs={{0,1},{1,0},{2,3},{3,2},{4,5},{5,4},{6,7},{7,6},{8,9},{9,8},{10,11... | collective-permute-start | bytes 1622024 | tf_op jit(solution)/shard_map/ppermute | solution.py:138
  55.4 15.7 %collective-permute-start.14 = (bf16[64,4224]{1,0:T(8,128)(2,1)S(1)}, bf16[64,4224]{1,0:T(8,128)(2,1)S(1)}, u32[]{:S(2)}, u32[]{:S(2)}) collective-permute-start(bf16[64,4224]{1,0:T(8,128)(2,1)S(1)} %collective-permute-done.12.refs_0_), channel_id=1, source_target_pairs={{0,1},{1,0},{2,3},{3,2},{4,5},{5,4},{6,7},{7,6},{8,9},{9,8},{10,11... | collective-permute-start | bytes 1622024 | tf_op jit(solution)/shard_map/ppermute | solution.py:138
  56.0 15.2 %collective-permute-start.15 = (bf16[64,4224]{1,0:T(8,128)(2,1)S(1)}, bf16[64,4224]{1,0:T(8,128)(2,1)S(1)}, u32[]{:S(2)}, u32[]{:S(2)}) collective-permute-start(bf16[64,4224]{1,0:T(8,128)(2,1)S(1)} %collective-permute-done.13.refs_1_), channel_id=1, source_target_pairs={{0,1},{1,0},{2,3},{3,2},{4,5},{5,4},{6,7},{7,6},{8,9},{9,8},{10,11... | collective-permute-start | bytes 1622024 | tf_op jit(solution)/shard_map/ppermute | solution.py:138
  57.4 2.8 %copy-start = (bf16[1,4096,768]{2,1,0:T(8,128)(2,1)S(1)}, bf16[1,4096,768]{2,1,0:T(8,128)(2,1)}, u32[]{:S(2)}) copy-start(bf16[1,4096,768]{2,1,0:T(8,128)(2,1)} %param.9) | copy-start | bytes 18874372
  60.2 2.8 %copy-start.2 = (bf16[1,4096,768]{2,1,0:T(8,128)(2,1)S(1)}, bf16[1,4096,768]{2,1,0:T(8,128)(2,1)}, u32[]{:S(2)}) copy-start(bf16[1,4096,768]{2,1,0:T(8,128)(2,1)} %param.10) | copy-start | bytes 18874372
  62.9 2.8 %copy-start.3 = (bf16[1,768,4096]{2,1,0:T(8,128)(2,1)S(1)}, bf16[1,768,4096]{2,1,0:T(8,128)(2,1)}, u32[]{:S(2)}) copy-start(bf16[1,768,4096]{2,1,0:T(8,128)(2,1)} %param.11) | copy-start | bytes 18874372
  65.7 5.4 %copy-start.1 = (bf16[1,4096,768]{2,1,0:T(8,128)(2,1)S(1)}, bf16[1,4096,768]{2,1,0:T(8,128)(2,1)}, u32[]{:S(2)}) copy-start(bf16[1,4096,768]{2,1,0:T(8,128)(2,1)} %param.9) | copy-start | bytes 18874372
  70.5 8.3 %collective-permute-start.19 = (bf16[64,4096]{1,0:T(8,128)(2,1)S(1)}, bf16[64,4096]{1,0:T(8,128)(2,1)S(1)}, u32[]{:S(2)}, u32[]{:S(2)}) collective-permute-start(bf16[64,4096]{1,0:T(8,128)(2,1)S(1)} %get-tuple-element.24), channel_id=1, source_target_pairs={{0,1},{1,0},{2,3},{3,2},{4,5},{5,4},{6,7},{7,6},{8,9},{9,8},{10,11... | collective-permute-start | bytes 1572872 | tf_op jit(solution)/shard_map/ppermute | solution.py:138
  70.6 9.8 %collective-permute-start.9 = (bf16[64,4224]{1,0:T(8,128)(2,1)S(1)}, bf16[64,4224]{1,0:T(8,128)(2,1)S(1)}, u32[]{:S(2)}, u32[]{:S(2)}) collective-permute-start(bf16[64,4224]{1,0:T(8,128)(2,1)S(1)} %collective-permute-done.7.refs_0_), channel_id=1, source_target_pairs={{0,1},{1,0},{2,3},{3,2},{4,5},{5,4},{6,7},{7,6},{8,9},{9,8},{10,11... | collective-permute-start | bytes 1622024 | tf_op jit(solution)/shard_map/ppermute | solution.py:138
  71.0 9.4 %collective-permute-start.10 = (bf16[64,4224]{1,0:T(8,128)(2,1)}, bf16[64,4224]{1,0:T(8,128)(2,1)S(1)}, u32[]{:S(2)}, u32[]{:S(2)}) collective-permute-start(bf16[64,4224]{1,0:T(8,128)(2,1)} %collective-permute-done.8.refs_1_), channel_id=1, source_target_pairs={{0,1},{1,0},{2,3},{3,2},{4,5},{5,4},{6,7},{7,6},{8,9},{9,8},{10,11... | collective-permute-start | bytes 1622024 | tf_op jit(solution)/shard_map/ppermute | solution.py:138
  78.3 10.9 %collective-permute-start.16 = (bf16[128,4096]{1,0:T(8,128)(2,1)S(1)}, bf16[128,4096]{1,0:T(8,128)(2,1)S(1)}, u32[]{:S(2)}, u32[]{:S(2)}) collective-permute-start(bf16[128,4096]{1,0:T(8,128)(2,1)S(1)} %get-tuple-element.22), channel_id=1, source_target_pairs={{0,1},{1,0},{2,3},{3,2},{4,5},{5,4},{6,7},{7,6},{8,9},{9,8},{10,11... | collective-permute-start | bytes 3145736 | tf_op jit(solution)/shard_map/ppermute | solution.py:138
  78.9 10.3 %collective-permute-start.20 = (bf16[64,4096]{1,0:T(8,128)(2,1)S(1)}, bf16[64,4096]{1,0:T(8,128)(2,1)S(1)}, u32[]{:S(2)}, u32[]{:S(2)}) collective-permute-start(bf16[64,4096]{1,0:T(8,128)(2,1)S(1)} %add_convert_fusion.7), channel_id=1, source_target_pairs={{0,2},{1,5},{4,0},{5,9},{8,4},{9,13},{12,8},{13,15},{14,12},{15,11... | collective-permute-start | bytes 1572872 | tf_op jit(solution)/shard_map/ppermute | solution.py:135
  79.6 12.2 %collective-permute-start.4 = (bf16[64,4224]{1,0:T(8,128)(2,1)S(1)}, bf16[64,4224]{1,0:T(8,128)(2,1)S(1)}, u32[]{:S(2)}, u32[]{:S(2)}) collective-permute-start(bf16[64,4224]{1,0:T(8,128)(2,1)S(1)} %collective-permute-done.2.refs_0_), channel_id=1, source_target_pairs={{0,1},{1,0},{2,3},{3,2},{4,5},{5,4},{6,7},{7,6},{8,9},{9,8},{10,11... | collective-permute-start | bytes 1622024 | tf_op jit(solution)/shard_map/ppermute | solution.py:138
  80.4 11.3 %collective-permute-start.5 = (bf16[64,4224]{1,0:T(8,128)(2,1)S(1)}, bf16[64,4224]{1,0:T(8,128)(2,1)S(1)}, u32[]{:S(2)}, u32[]{:S(2)}) collective-permute-start(bf16[64,4224]{1,0:T(8,128)(2,1)S(1)} %collective-permute-done.3.refs_1_), channel_id=1, source_target_pairs={{0,1},{1,0},{2,3},{3,2},{4,5},{5,4},{6,7},{7,6},{8,9},{9,8},{10,11... | collective-permute-start | bytes 1622024 | tf_op jit(solution)/shard_map/ppermute | solution.py:138
  88.7 10.8 %collective-permute-start.11 = (bf16[128,4096]{1,0:T(8,128)(2,1)S(1)}, bf16[128,4096]{1,0:T(8,128)(2,1)S(1)}, u32[]{:S(2)}, u32[]{:S(2)}) collective-permute-start(bf16[128,4096]{1,0:T(8,128)(2,1)S(1)} %get-tuple-element.20), channel_id=1, source_target_pairs={{0,1},{1,0},{2,3},{3,2},{4,5},{5,4},{6,7},{7,6},{8,9},{9,8},{10,11... | collective-permute-start | bytes 3145736 | tf_op jit(solution)/shard_map/ppermute | solution.py:138
  89.7 13.9 %collective-permute-start.21 = (bf16[64,4096]{1,0:T(8,128)(2,1)S(1)}, bf16[64,4096]{1,0:T(8,128)(2,1)S(1)}, u32[]{:S(2)}, u32[]{:S(2)}) collective-permute-start(bf16[64,4096]{1,0:T(8,128)(2,1)S(1)} %get-tuple-element.25), channel_id=1, source_target_pairs={{0,2},{1,3},{4,0},{5,1},{8,4},{9,5},{12,8},{13,9},{14,12},{15,13},... | collective-permute-start | bytes 1572872 | tf_op jit(solution)/shard_map/ppermute | solution.py:135
  90.3 14.0 %collective-permute-start.24 = (bf16[64,4096]{1,0:T(8,128)(2,1)S(1)}, bf16[64,4096]{1,0:T(8,128)(2,1)S(1)}, u32[]{:S(2)}, u32[]{:S(2)}) collective-permute-start(bf16[64,4096]{1,0:T(8,128)(2,1)S(1)} %get-tuple-element.26), channel_id=1, source_target_pairs={{0,4},{1,5},{4,8},{5,9},{8,12},{9,13},{12,14},{13,15},{14,10},{15,... | collective-permute-start | bytes 1572872 | tf_op jit(solution)/shard_map/ppermute | solution.py:135
  91.8 15.1 %collective-permute-start = (bf16[64,4224]{1,0:T(8,128)(2,1)S(1)}, bf16[64,4224]{1,0:T(8,128)(2,1)S(1)}, u32[]{:S(2)}, u32[]{:S(2)}) collective-permute-start(bf16[64,4224]{1,0:T(8,128)(2,1)S(1)} %shard_map.64.refs_0_), channel_id=1, source_target_pairs={{0,1},{1,0},{2,3},{3,2},{4,5},{5,4},{6,7},{7,6},{8,9},{9,8},{10,11... | collective-permute-start | bytes 1622024 | tf_op jit(solution)/shard_map/ppermute | solution.py:138
  98.9 12.7 %collective-permute-start.6 = (bf16[128,4096]{1,0:T(8,128)(2,1)S(1)}, bf16[128,4096]{1,0:T(8,128)(2,1)S(1)}, u32[]{:S(2)}, u32[]{:S(2)}) collective-permute-start(bf16[128,4096]{1,0:T(8,128)(2,1)S(1)} %get-tuple-element.18), channel_id=1, source_target_pairs={{0,1},{1,0},{2,3},{3,2},{4,5},{5,4},{6,7},{7,6},{8,9},{9,8},{10,11... | collective-permute-start | bytes 3145736 | tf_op jit(solution)/shard_map/ppermute | solution.py:138
  104.8 13.3 %collective-permute-start.22 = (bf16[64,4096]{1,0:T(8,128)(2,1)S(1)}, bf16[64,4096]{1,0:T(8,128)(2,1)S(1)}, u32[]{:S(2)}, u32[]{:S(2)}) collective-permute-start(bf16[64,4096]{1,0:T(8,128)(2,1)S(1)} %get-tuple-element.29), channel_id=1, source_target_pairs={{0,2},{1,3},{4,0},{5,1},{8,4},{9,5},{12,8},{13,9},{14,12},{15,13},... | collective-permute-start | bytes 1572872 | tf_op jit(solution)/shard_map/ppermute | solution.py:135
  106.4 12.9 %collective-permute-start.25 = (bf16[64,4096]{1,0:T(8,128)(2,1)S(1)}, bf16[64,4096]{1,0:T(8,128)(2,1)S(1)}, u32[]{:S(2)}, u32[]{:S(2)}) collective-permute-start(bf16[64,4096]{1,0:T(8,128)(2,1)S(1)} %get-tuple-element.30), channel_id=1, source_target_pairs={{0,4},{1,5},{4,8},{5,9},{8,12},{9,13},{12,14},{13,15},{14,10},{15,... | collective-permute-start | bytes 1572872 | tf_op jit(solution)/shard_map/ppermute | solution.py:135
  111.6 10.3 %collective-permute-start.1 = (bf16[64,4096]{1,0:T(8,128)(2,1)S(1)}, bf16[64,4096]{1,0:T(8,128)(2,1)S(1)}, u32[]{:S(2)}, u32[]{:S(2)}) collective-permute-start(bf16[64,4096]{1,0:T(8,128)(2,1)S(1)} %get-tuple-element.16), channel_id=1, source_target_pairs={{0,1},{1,0},{2,3},{3,2},{4,5},{5,4},{6,7},{7,6},{8,9},{9,8},{10,11... | collective-permute-start | bytes 1572872 | tf_op jit(solution)/shard_map/ppermute | solution.py:138
  119.8 12.1 %collective-permute-start.26 = (bf16[64,4096]{1,0:T(8,128)(2,1)S(1)}, bf16[64,4096]{1,0:T(8,128)(2,1)S(1)}, u32[]{:S(2)}, u32[]{:S(2)}) collective-permute-start(bf16[64,4096]{1,0:T(8,128)(2,1)S(1)} %get-tuple-element.28), channel_id=1, source_target_pairs={{0,4},{1,5},{4,8},{5,9},{8,12},{9,13},{12,14},{13,15},{14,10},{15,... | collective-permute-start | bytes 1572872 | tf_op jit(solution)/shard_map/ppermute | solution.py:135
  120.3 11.7 %collective-permute-start.23 = (bf16[64,4096]{1,0:T(8,128)(2,1)S(1)}, bf16[64,4096]{1,0:T(8,128)(2,1)S(1)}, u32[]{:S(2)}, u32[]{:S(2)}) collective-permute-start(bf16[64,4096]{1,0:T(8,128)(2,1)S(1)} %get-tuple-element.27), channel_id=1, source_target_pairs={{0,2},{1,3},{4,0},{5,1},{8,4},{9,5},{12,8},{13,9},{14,12},{15,13},... | collective-permute-start | bytes 1572872 | tf_op jit(solution)/shard_map/ppermute | solution.py:135

commit v3 on v2

v3 whole, which is shorter than its diff:
```python
import functools

import jax
import jax.numpy as jnp
from jax import lax
from jax.experimental import pallas as pl
from jax.experimental.pallas import tpu as pltpu
from jax.sharding import PartitionSpec as P

LANES = 128
FF_TILE = 256
OUT_TILE = 512
MIB = 1 << 20
LOADS = 4
SUM_FLOPS = 0
OUT_PIECES = 1
BACK_PIECES = 1


def encode_kernel(tokens_ref, routes_ref, codes_ref, *out_refs):
    rows, width = tokens_ref.shape
    part = rows // len(out_refs)
    for b in range(width // LANES):
        cols = slice(b * LANES, (b + 1) * LANES)
        block = tokens_ref[:, cols].astype(jnp.float32)
        largest = jnp.max(jnp.abs(block), axis=1, keepdims=True)
        scale = ((largest + 1e-6) / 448.0).astype(jnp.bfloat16).astype(jnp.float32)
        coded = (block / scale).astype(jnp.bfloat16).astype(jnp.float32)
        value = (coded * scale).astype(jnp.bfloat16)
        for i, ref in enumerate(out_refs):
            ref[:, cols] = value[i * part : (i + 1) * part]
    expert = lax.broadcasted_iota(jnp.int32, (LANES, rows), 0)
    table = jnp.zeros((LANES, rows), jnp.float32)
    for k in range(routes_ref.shape[0]):
        code = codes_ref[k : k + 1, :].astype(jnp.float32)
        table = table + jnp.where(expert == routes_ref[k : k + 1, :], code, 0.0)
    table = table.T.astype(jnp.bfloat16)
    for i, ref in enumerate(out_refs):
        ref[:, width:] = table[i * part : (i + 1) * part]


def encode(tokens, routes, gate_codes):
    rows, width = tokens.shape
    out = jax.ShapeDtypeStruct((rows // OUT_PIECES, width + LANES), jnp.bfloat16)
    return pl.pallas_call(
        encode_kernel,
        out_shape=[out] * OUT_PIECES,
        compiler_params=pltpu.CompilerParams(vmem_limit_bytes=8 * MIB),
    )(*[pltpu.with_memory_space_constraint(a, pltpu.HBM) for a in (tokens, routes.T, gate_codes.T)])


def expert_kernel(count, me_ref, *refs):
    x_refs = refs[:count]
    gate_w, up_w, down_w = refs[count : count + 3]
    own_out, other_out = refs[count + 3 : count + 5]
    hidden, scale = refs[count + 5 :]
    width, ff = gate_w.shape
    half = own_out.shape[0]

    rows = x_refs[0].shape[0]
    lane = lax.broadcasted_iota(jnp.int32, (rows, LANES), 1)
    for i, ref in enumerate(x_refs):
        codes = ref[:, width:].astype(jnp.float32)
        total = jnp.sum(codes, axis=1, keepdims=True)
        mine = jnp.sum(jnp.where(lane == me_ref[0], codes, 0.0), axis=1, keepdims=True)
        scale[i * rows : (i + 1) * rows, :] = jnp.broadcast_to(mine / total, (rows, LANES))

    for t in range(ff // FF_TILE):
        cols = slice(t * FF_TILE, (t + 1) * FF_TILE)
        x = jnp.concatenate([ref[:, :width] for ref in x_refs], axis=0)
        gate = jnp.dot(x, gate_w[:, cols], preferred_element_type=jnp.float32)
        up = jnp.dot(x, up_w[:, cols], preferred_element_type=jnp.float32)
        hidden[:, cols] = (gate / (1.0 + jnp.exp(-gate)) * up).astype(jnp.bfloat16)

    for t in range(width // OUT_TILE):
        cols = slice(t * OUT_TILE, (t + 1) * OUT_TILE)
        result = jnp.dot(hidden[...], down_w[:, cols], preferred_element_type=jnp.float32)
        result = (result * scale[:, 0:1]).astype(jnp.bfloat16)
        own_out[:, cols] = result[:half]
        other_out[:, cols] = result[half:]


def expert(me, own, other, weights):
    blocks = [*own, *other]
    rows = blocks[0].shape[0]
    width, ff = weights[0].shape
    half = rows * len(own)
    out = jax.ShapeDtypeStruct((half, width), jnp.bfloat16)
    vmem = pl.BlockSpec(memory_space=pltpu.VMEM)
    pinned = [pltpu.with_memory_space_constraint(w, pltpu.VMEM) for w in weights]
    return pl.pallas_call(
        functools.partial(expert_kernel, len(blocks)),
        in_specs=[pl.BlockSpec(memory_space=pltpu.SMEM)] + [vmem] * (len(blocks) + 3),
        out_specs=[vmem, vmem],
        out_shape=[out, out],
        scratch_shapes=[
            pltpu.VMEM((2 * half, ff), jnp.bfloat16),
            pltpu.VMEM((2 * half, LANES), jnp.float32),
        ],
        cost_estimate=pl.CostEstimate(
            flops=12 * half * width * ff,
            bytes_accessed=8 * half * width,
            transcendentals=2 * half * ff,
        ),
        compiler_params=pltpu.CompilerParams(vmem_limit_bytes=8 * MIB),
    )(me, *blocks, *pinned)


def load_kernel(*refs):
    count = len(refs) // 2
    copies = []
    for i in range(count):
        rows = refs[i].shape[0] // LOADS
        for j in range(LOADS):
            span = slice(j * rows, (j + 1) * rows)
            copies.append(pltpu.make_async_copy(refs[i].at[span], refs[count + i].at[span], refs[-1].at[i, j]))
    for copy in copies:
        copy.start()
    for copy in copies:
        copy.wait()


def load(weights):
    return pl.pallas_call(
        load_kernel,
        in_specs=[pl.BlockSpec(memory_space=pltpu.HBM)] * len(weights),
        out_specs=[pl.BlockSpec(memory_space=pltpu.VMEM)] * len(weights),
        out_shape=[pltpu.VMEM(w.shape, w.dtype) for w in weights],
        scratch_shapes=[pltpu.SemaphoreType.DMA((len(weights), LOADS))],
        cost_estimate=pl.CostEstimate(flops=0, bytes_accessed=sum(4 * w.size for w in weights), transcendentals=0),
        compiler_params=pltpu.CompilerParams(vmem_limit_bytes=MIB),
    )(*[pltpu.with_memory_space_constraint(w, pltpu.HBM) for w in weights])


def add_kernel(first, second, core_ref, *refs):
    ins, outs = refs[: len(refs) - len(first)], refs[len(refs) - len(first) :]
    for core, terms in ((0, first), (1, second)):

        @pl.when(core_ref[0] == core)
        def _():
            for out_ref, listed in zip(outs, terms, strict=True):
                rows = out_ref.shape[0]
                total = None
                for index, start in listed:
                    value = ins[index][start : start + rows, :].astype(jnp.float32)
                    total = value if total is None else total + value
                out_ref[...] = total.astype(out_ref.dtype)


def add_rows(core, first, second, cost):
    arrays, places = [], {}
    for sums in (first, second):
        for terms in sums:
            for array, _ in terms:
                if id(array) not in places:
                    places[id(array)] = len(arrays)
                    arrays.append(array)
    layout = [[[(places[id(array)], start) for array, start in terms] for terms in sums] for sums in (first, second)]
    vmem = pl.BlockSpec(memory_space=pltpu.VMEM)
    rows, width = cost[1]
    out = jax.ShapeDtypeStruct((rows, width), jnp.bfloat16)
    return pl.pallas_call(
        functools.partial(add_kernel, *layout),
        in_specs=[pl.BlockSpec(memory_space=pltpu.SMEM)] + [vmem] * len(arrays),
        out_specs=[vmem] * len(first),
        out_shape=[out] * len(first),
        cost_estimate=pl.CostEstimate(flops=cost[0], bytes_accessed=0, transcendentals=0),
        compiler_params=pltpu.CompilerParams(vmem_limit_bytes=4 * MIB),
    )(core, *arrays)


def ring_order(nodes, groups):
    chips = nodes // 2
    if groups == 2:
        return list(range(0, chips, 2)) + list(range(1, chips, 2))[::-1]
    return list(range(chips))


def after(values, others):
    return list(lax.optimization_barrier((*values, *others)))[: len(values)]


def local(nodes, groups, tokens, routes, gate_codes, w_gate, w_up, w_down):
    order = ring_order(nodes, groups)
    chips = len(order)
    far = chips // 2
    node = lax.axis_index("node").astype(jnp.int32)
    first_core = (node % 2) == 0
    me = node.reshape(1)
    core = (node % 2).reshape(1)

    def hop(value, *steps):
        steps = steps * (3 - len(steps))
        pairs = [
            (2 * order[i] + core, 2 * order[(i + steps[core]) % chips] + core)
            for i in range(chips)
            for core in (0, 1)
        ]
        return lax.ppermute(value, "node", pairs)

    def swap(value):
        return lax.ppermute(value, "node", [(i, i ^ 1) for i in range(nodes)])

    def pick(on_first, on_second):
        return jnp.where(first_core, on_first, on_second)

    ahead = [encode(tokens, routes, gate_codes)]
    behind = [ahead[0]]
    for _ in range(1, far):
        ahead.append([hop(piece, 1) for piece in ahead[-1]])
        behind.append([hop(piece, -1) for piece in behind[-1]])
    weights = load(after([w_gate[0], w_up[0], w_down[0]], ahead[far - 2]))
    sources = after([*ahead[-1], *behind[-1]], [weights[0]])
    last = [hop(pick(a, b), 1, -1) for a, b in zip(sources[:OUT_PIECES], sources[OUT_PIECES:], strict=True)]
    batches = [ahead[0]] + [a + b for a, b in zip(ahead[1:], behind[1:], strict=True)] + [last]

    others = [[swap(piece) for piece in batch] for batch in batches]
    sent = {}

    def run(s, *awaited):
        own = after(batches[s], awaited)
        outs = expert(me, own, others[s], weights)
        sent[s] = (outs[0], swap(outs[1]))

    shape = (tokens.shape[0] // BACK_PIECES, tokens.shape[1])

    def part(piece, s, place):
        start = (place * BACK_PIECES if 0 < s < far else 0) + piece
        return [(rows, start * shape[0]) for rows in sent[s]]

    def sums(first, second):
        return add_rows(core, first, second, (SUM_FLOPS, shape))

    pieces = range(BACK_PIECES)
    run(far)
    run(far - 1, sent[far][0])
    edges = [hop(sums([part(i, far, 0)], [part(i, far, 0)])[0], -1, 1) for i in pieces]
    moving = [(None, None)] * BACK_PIECES
    for s in range(far - 1, 0, -1):
        if s > 1:
            run(s - 1, sent[s][0])
        for i in pieces:
            up, down = [part(i, s, 0)] * 2, [part(i, s, 1)] * 2
            if s == far - 1:
                up[0], down[1] = [(edges[i], 0), *up[0]], [(edges[i], 0), *down[1]]
            else:
                up, down = [[moving[i][0], *terms] for terms in up], [[moving[i][1], *terms] for terms in down]
            totals = sums([up[0], down[0]], [up[1], down[1]])
            moving[i] = ((hop(totals[0], -1), 0), (hop(totals[1], 1), 0))
    run(0, sent[1][0])
    outs = []
    for i in pieces:
        terms = [[*moving[i], *part(i, 0, 0)]]
        outs += sums(terms, terms)
    return outs[0] if len(outs) == 1 else jnp.concatenate(outs, axis=0)


def solution(mesh):
    return jax.shard_map(
        functools.partial(local, mesh.shape["node"], mesh.shape["groups"]),
        mesh=mesh,
        in_specs=(
            P(("groups", "node"), None),
            P(("groups", "node"), None),
            P(("groups", "node"), None),
            P("node", None, None),
            P("node", None, None),
            P("node", None, None),
        ),
        out_specs=P(("groups", "node"), None),
        check_vma=False,
    )
```

time: 133 us -> 115 us (0.86)
  local copies, waits for them, and re-layouts: 10.9 us -> 0 us
  waiting for transfers between devices: 67.5 us -> 63 us
  other arithmetic: 2.6 us -> 0.06 us
    unnamed x12 -> x0, local copies, waits for them, and re-layouts: 10.9 us -> none
    pallas_call x5, Pallas kernels: 32 us -> 21.9 us  [expert(): pl.pallas_call(functools.partial(expert_kernel, len(blocks)), in_specs=[p...]
    pallas_call x1 -> x7, Pallas kernels: 0.61 us -> 10.4 us  [the longest x1 6.52 us: load(): pl.pallas_call(load_kernel, in_specs=[pl.BlockSpec(memory_space=pltpu.HBM...]
    ppermute x14, waiting for transfers between devices: 66 us -> 62 us  [hop(): return lax.ppermute(value, 'node', pairs)]
    convert_element_type x5 -> x0, other arithmetic: 2.53 us -> none  [the longest x3 1.35 us: local(): up, down = (hop(up.astype(low), -1), hop(down.astype(low), 1))]
  transfers between devices with their start and end apart: 27 -> 27, of which waited for: 12 -> 13; matrix products, arithmetic and copies ran while one was open for 1% -> 0% of each run, Pallas kernels for 24% -> 26%
where the time goes in v3:
time: 115 us
  waiting for transfers between devices  63 us (55%)
  Pallas kernels  32.3 us (28%)
  starting transfers between devices  19.5 us (17%)
    ppermute x14, waiting for transfers between devices, hop(): return lax.ppermute(value, 'node', pairs)  62 us
    pallas_call x5, Pallas kernels, expert(): pl.pallas_call(functools.partial(expert_kernel, len(blocks)), in_specs=[p...  21.9 us
    ppermute x14, starting transfers between devices, hop(): return lax.ppermute(value, 'node', pairs)  15.8 us
    pallas_call x1, Pallas kernels, load(): pl.pallas_call(load_kernel, in_specs=[pl.BlockSpec(memory_space=pltpu.HBM...  6.52 us
    ppermute x13, starting transfers between devices, swap(): return lax.ppermute(value, 'node', [(i, i ^ 1) for i in range(nodes)])  3.72 us
  transfers between devices with their start and end apart: 27, of which 13 were waited for; matrix products, arithmetic and copies ran while one was open for 0% of the time, Pallas kernels for 26%

profile of v3, /device:TPU:0, one launch (start us, length us, event | category | flops | bytes accessed | tf_op | source)
XLA Modules:
  0.0 115.0 jit_solution(18334491877404584450)
XLA Ops:
  0.0 1.6 %shard_map.64.refs_0_ = bf16[64,4224]{1,0:T(8,128)(2,1)S(1)} custom-call(bf16[64,4096]{1,0:T(8,128)(2,1)} %tokens_ref.1, s32[8,64]{1,0:T(8,128)} %bitcast.10, s32[8,64]{1,0:T(8,128)} %bitcast.11), custom_call_target="tpu_custom_call" | custom-call | tf_op jit(solution)/shard_map/pallas_call | solution.py:45
  1.6 3.1 %collective-permute-start = (bf16[64,4224]{1,0:T(8,128)(2,1)S(1)}, bf16[64,4224]{1,0:T(8,128)(2,1)S(1)}, u32[]{:S(2)}, u32[]{:S(2)}) collective-permute-start(bf16[64,4224]{1,0:T(8,128)(2,1)S(1)} %shard_map.64.refs_0_), channel_id=1, source_target_pairs={{0,4},{1,5},{4,8},{5,9},{8,12},{9,13},{12,14},{13,15},{14,10},{15,... | collective-permute-start | bytes 1622024 | tf_op jit(solution)/shard_map/ppermute | solution.py:199
  4.7 0.0 collective-permute-start.3
  4.7 12.2 %collective-permute-done.refs_0_ = bf16[64,4224]{1,0:T(8,128)(2,1)S(1)} collective-permute-done((bf16[64,4224]{1,0:T(8,128)(2,1)S(1)}, bf16[64,4224]{1,0:T(8,128)(2,1)S(1)}, u32[]{:S(2)}, u32[]{:S(2)}) %collective-permute-start) | collective-permute-done | bytes 540704 | tf_op jit(solution)/shard_map/ppermute | solution.py:199
  16.9 1.8 %collective-permute-start.1 = (bf16[64,4224]{1,0:T(8,128)(2,1)S(1)}, bf16[64,4224]{1,0:T(8,128)(2,1)S(1)}, u32[]{:S(2)}, u32[]{:S(2)}) collective-permute-start(bf16[64,4224]{1,0:T(8,128)(2,1)S(1)} %collective-permute-done.refs_0_), channel_id=1, source_target_pairs={{0,4},{1,5},{4,8},{5,9},{8,12},{9,13},{12,14},{13,15},{14,10},{15,... | collective-permute-start | bytes 1622024 | tf_op jit(solution)/shard_map/ppermute | solution.py:199
  18.7 0.0 collective-permute-done.3.refs_1_
  18.7 0.2 collective-permute-start.4
  18.9 11.4 %collective-permute-done.1.refs_0_ = bf16[64,4224]{1,0:T(8,128)(2,1)S(1)} collective-permute-done((bf16[64,4224]{1,0:T(8,128)(2,1)S(1)}, bf16[64,4224]{1,0:T(8,128)(2,1)S(1)}, u32[]{:S(2)}, u32[]{:S(2)}) %collective-permute-start.1) | collective-permute-done | bytes 540704 | tf_op jit(solution)/shard_map/ppermute | solution.py:199
  30.4 1.5 %collective-permute-start.2 = (bf16[64,4224]{1,0:T(8,128)(2,1)S(1)}, bf16[64,4224]{1,0:T(8,128)(2,1)S(1)}, u32[]{:S(2)}, u32[]{:S(2)}) collective-permute-start(bf16[64,4224]{1,0:T(8,128)(2,1)S(1)} %collective-permute-done.1.refs_0_), channel_id=1, source_target_pairs={{0,4},{1,5},{4,8},{5,9},{8,12},{9,13},{12,14},{13,15},{14,10},{15,... | collective-permute-start | bytes 1622024 | tf_op jit(solution)/shard_map/ppermute | solution.py:199
  31.8 0.0 collective-permute-done.4.refs_1_
  31.8 0.5 collective-permute-start.5
  32.4 6.5 %shard_map.65 = (bf16[4096,768]{1,0:T(8,128)(2,1)S(1)}, bf16[4096,768]{1,0:T(8,128)(2,1)S(1)}, bf16[768,4096]{1,0:T(8,128)(2,1)S(1)}) custom-call(bf16[4096,768]{1,0:T(8,128)(2,1)} %bitcast.7, bf16[4096,768]{1,0:T(8,128)(2,1)} %bitcast.8, bf16[768,4096]{1,0:T(8,128)(2,1)} %bitcast.9), custom_call_target="tpu_custom_call" | custom-call | bytes 37748736 | tf_op jit(solution)/shard_map/pallas_call | solution.py:124
  38.9 4.1 %collective-permute-done.2.refs_0_ = bf16[64,4224]{1,0:T(8,128)(2,1)S(1)} collective-permute-done((bf16[64,4224]{1,0:T(8,128)(2,1)S(1)}, bf16[64,4224]{1,0:T(8,128)(2,1)S(1)}, u32[]{:S(2)}, u32[]{:S(2)}) %collective-permute-start.2) | collective-permute-done | bytes 540704 | tf_op jit(solution)/shard_map/ppermute | solution.py:199
  43.0 1.4 %collective-permute-done.5.refs_1_ = bf16[64,4224]{1,0:T(8,128)(2,1)S(1)} collective-permute-done((bf16[64,4224]{1,0:T(8,128)(2,1)}, bf16[64,4224]{1,0:T(8,128)(2,1)S(1)}, u32[]{:S(2)}, u32[]{:S(2)}) %collective-permute-start.5) | collective-permute-done | bytes 540704 | tf_op jit(solution)/shard_map/ppermute | solution.py:199
  44.4 0.1 broadcast_select_fusion
  44.4 1.6 %collective-permute-start.6 = (bf16[64,4224]{1,0:T(8,128)(2,1)S(1)}, bf16[64,4224]{1,0:T(8,128)(2,1)S(1)}, u32[]{:S(2)}, u32[]{:S(2)}) collective-permute-start(bf16[64,4224]{1,0:T(8,128)(2,1)S(1)} %broadcast_select_fusion), channel_id=1, source_target_pairs={{0,4},{1,3},{4,8},{5,1},{8,12},{9,5},{12,14},{13,9},{14,10},{15,13... | collective-permute-start | bytes 1622024 | tf_op jit(solution)/shard_map/ppermute | solution.py:199
  46.1 7.8 %collective-permute-done.6.refs_0_ = bf16[64,4224]{1,0:T(8,128)(2,1)S(1)} collective-permute-done((bf16[64,4224]{1,0:T(8,128)(2,1)S(1)}, bf16[64,4224]{1,0:T(8,128)(2,1)S(1)}, u32[]{:S(2)}, u32[]{:S(2)}) %collective-permute-start.6) | collective-permute-done | bytes 540704 | tf_op jit(solution)/shard_map/ppermute | solution.py:199
  53.9 0.0 collective-permute-start.7
  53.9 0.5 collective-permute-start.10
  54.4 0.0 collective-permute-start.11
  54.4 0.5 collective-permute-start.14
  54.9 0.0 collective-permute-start.15
  54.9 0.9 collective-permute-done.7.refs_1_
  55.8 2.7 %shard_map.66 = (bf16[64,4096]{1,0:T(8,128)(2,1)S(1)}, bf16[64,4096]{1,0:T(8,128)(2,1)S(1)}) custom-call(s32[1]{0:T(128)} %bitcast.1.me_ref, bf16[64,4224]{1,0:T(8,128)(2,1)S(1)} %collective-permute-done.6.refs_0_, bf16[64,4224]{1,0:T(8,128)(2,1)S(1)} %collective-permute-done.7.refs_1_, bf16[4096,768]{1,0:T(8,128)(2,1)S(1)} %get-tuple-element.39.refs_2_.refs_4_, ...), custom_call_target="tpu_custom_call" | custom-call | flops 2415919104 | bytes 2097152 | tf_op jit(solution)/shard_map/pallas_call | solution.py:91
  58.5 0.2 collective-permute-start.8
  58.7 0.0 collective-permute-done.10.refs_2_
  58.7 0.0 collective-permute-done.11.refs_3_
  58.7 5.1 %shard_map.68 = (bf16[128,4096]{1,0:T(8,128)(2,1)S(1)}, bf16[128,4096]{1,0:T(8,128)(2,1)S(1)}) custom-call(s32[1]{0:T(128)} %bitcast.1.me_ref, bf16[64,4224]{1,0:T(8,128)(2,1)S(1)} %collective-permute-done.2.refs_0_, bf16[64,4224]{1,0:T(8,128)(2,1)S(1)} %collective-permute-done.5.refs_1_, bf16[64,4224]{1,0:T(8,128)(2,1)S(1)} %collective-permute-done.10.refs_2_, ...), custom_call_target="tpu_custom_call" | custom-call | flops 4831838208 | bytes 4194304 | tf_op jit(solution)/shard_map/pallas_call | solution.py:91
  63.9 0.5 collective-permute-start.12
  64.3 0.1 collective-permute-start.19
  64.4 0.0 collective-permute-done.8.refs_1_
  64.4 0.4 collective-permute-start.20
  64.8 0.1 shard_map.67
  65.0 0.0 collective-permute-done.14.refs_2_
  65.0 0.8 collective-permute-start.9
  65.8 0.0 collective-permute-done.15.refs_3_
  65.8 6.2 %shard_map.70 = (bf16[128,4096]{1,0:T(8,128)(2,1)S(1)}, bf16[128,4096]{1,0:T(8,128)(2,1)S(1)}) custom-call(s32[1]{0:T(128)} %bitcast.1.me_ref, bf16[64,4224]{1,0:T(8,128)(2,1)S(1)} %collective-permute-done.1.refs_0_, bf16[64,4224]{1,0:T(8,128)(2,1)} %collective-permute-done.4.refs_1_, bf16[64,4224]{1,0:T(8,128)(2,1)S(1)} %collective-permute-done.14.refs_2_, ...), custom_call_target="tpu_custom_call" | custom-call | flops 4831838208 | bytes 4194304 | tf_op jit(solution)/shard_map/pallas_call | solution.py:91
  72.0 0.9 collective-permute-start.16
  72.9 1.5 %collective-permute-done.9.refs_0_ = bf16[64,4096]{1,0:T(8,128)(2,1)S(1)} collective-permute-done((bf16[64,4096]{1,0:T(8,128)(2,1)S(1)}, bf16[64,4096]{1,0:T(8,128)(2,1)S(1)}, u32[]{:S(2)}, u32[]{:S(2)}) %collective-permute-start.9) | collective-permute-done | bytes 524320 | tf_op jit(solution)/shard_map/ppermute | solution.py:199
  74.4 0.3 shard_map.69
  74.7 0.6 collective-permute-start.13
  75.3 1.4 %collective-permute-start.17 = (bf16[64,4096]{1,0:T(8,128)(2,1)S(1)}, bf16[64,4096]{1,0:T(8,128)(2,1)S(1)}, u32[]{:S(2)}, u32[]{:S(2)}) collective-permute-start(bf16[64,4096]{1,0:T(8,128)(2,1)S(1)} %get-tuple-element.55), channel_id=1, source_target_pairs={{0,4},{1,5},{4,8},{5,9},{8,12},{9,13},{12,14},{13,15},{14,10},{15,... | collective-permute-start | bytes 1572872 | tf_op jit(solution)/shard_map/ppermute | solution.py:199
  76.8 0.0 collective-permute-done.19.refs_2_
  76.8 0.0 collective-permute-done.20.refs_3_
  76.8 5.1 %shard_map.72 = (bf16[128,4096]{1,0:T(8,128)(2,1)S(1)}, bf16[128,4096]{1,0:T(8,128)(2,1)S(1)}) custom-call(s32[1]{0:T(128)} %bitcast.1.me_ref, bf16[64,4224]{1,0:T(8,128)(2,1)S(1)} %collective-permute-done.refs_0_, bf16[64,4224]{1,0:T(8,128)(2,1)S(1)} %collective-permute-done.3.refs_1_, bf16[64,4224]{1,0:T(8,128)(2,1)S(1)} %collective-permute-done.19.refs_2_, ...), custom_call_target="tpu_custom_call" | custom-call | flops 4831838208 | bytes 4194304 | tf_op jit(solution)/shard_map/pallas_call | solution.py:91
  81.9 0.1 collective-permute-start.21
  82.0 0.5 collective-permute-start.25
  82.5 0.0 collective-permute-done.16.refs_2_
  82.5 5.3 %collective-permute-done.13.refs_0_ = bf16[64,4096]{1,0:T(8,128)(2,1)S(1)} collective-permute-done((bf16[64,4096]{1,0:T(8,128)(2,1)S(1)}, bf16[64,4096]{1,0:T(8,128)(2,1)S(1)}, u32[]{:S(2)}, u32[]{:S(2)}) %collective-permute-start.13) | collective-permute-done | bytes 524320 | tf_op jit(solution)/shard_map/ppermute | solution.py:199
  87.8 0.3 collective-permute-done.17.refs_3_
  88.2 0.4 shard_map.71
  88.5 1.4 %collective-permute-start.18 = (bf16[64,4096]{1,0:T(8,128)(2,1)S(1)}, bf16[64,4096]{1,0:T(8,128)(2,1)S(1)}, u32[]{:S(2)}, u32[]{:S(2)}) collective-permute-start(bf16[64,4096]{1,0:T(8,128)(2,1)S(1)} %get-tuple-element.56), channel_id=1, source_target_pairs={{0,2},{1,3},{4,0},{5,1},{8,4},{9,5},{12,8},{13,9},{14,12},{15,13},... | collective-permute-start | bytes 1572872 | tf_op jit(solution)/shard_map/ppermute | solution.py:199
  90.0 0.7 collective-permute-start.22
  90.6 2.7 %shard_map.74 = (bf16[64,4096]{1,0:T(8,128)(2,1)S(1)}, bf16[64,4096]{1,0:T(8,128)(2,1)S(1)}) custom-call(s32[1]{0:T(128)} %bitcast.1.me_ref, bf16[64,4224]{1,0:T(8,128)(2,1)S(1)} %shard_map.64.refs_0_, bf16[64,4224]{1,0:T(8,128)(2,1)S(1)} %collective-permute-done.25.refs_1_, bf16[4096,768]{1,0:T(8,128)(2,1)S(1)} %get-tuple-element.39.refs_2_.refs_4_, ...), custom_call_target="tpu_custom_call" | custom-call | flops 2415919104 | bytes 2097152 | tf_op jit(solution)/shard_map/pallas_call | solution.py:91
  93.4 0.1 collective-permute-start.26
  93.5 0.0 collective-permute-done.21.refs_2_
  93.5 7.0 %collective-permute-done.18.refs_0_ = bf16[64,4096]{1,0:T(8,128)(2,1)S(1)} collective-permute-done((bf16[64,4096]{1,0:T(8,128)(2,1)S(1)}, bf16[64,4096]{1,0:T(8,128)(2,1)S(1)}, u32[]{:S(2)}, u32[]{:S(2)}) %collective-permute-start.18) | collective-permute-done | bytes 524320 | tf_op jit(solution)/shard_map/ppermute | solution.py:199
  100.5 1.1 collective-permute-done.22.refs_3_
  101.6 0.4 shard_map.73
  101.9 1.6 %collective-permute-start.23 = (bf16[64,4096]{1,0:T(8,128)(2,1)S(1)}, bf16[64,4096]{1,0:T(8,128)(2,1)S(1)}, u32[]{:S(2)}, u32[]{:S(2)}) collective-permute-start(bf16[64,4096]{1,0:T(8,128)(2,1)S(1)} %get-tuple-element.62), channel_id=1, source_target_pairs={{0,2},{1,3},{4,0},{5,1},{8,4},{9,5},{12,8},{13,9},{14,12},{15,13},... | collective-permute-start | bytes 1572872 | tf_op jit(solution)/shard_map/ppermute | solution.py:199
  103.6 0.5 collective-permute-start.24
  104.0 8.6 %collective-permute-done.23.refs_0_ = bf16[64,4096]{1,0:T(8,128)(2,1)S(1)} collective-permute-done((bf16[64,4096]{1,0:T(8,128)(2,1)S(1)}, bf16[64,4096]{1,0:T(8,128)(2,1)S(1)}, u32[]{:S(2)}, u32[]{:S(2)}) %collective-permute-start.23) | collective-permute-done | bytes 524320 | tf_op jit(solution)/shard_map/ppermute | solution.py:199
  112.7 1.3 %collective-permute-done.24.refs_1_ = bf16[64,4096]{1,0:T(8,128)(2,1)S(1)} collective-permute-done((bf16[64,4096]{1,0:T(8,128)(2,1)S(1)}, bf16[64,4096]{1,0:T(8,128)(2,1)S(1)}, u32[]{:S(2)}, u32[]{:S(2)}) %collective-permute-start.24) | collective-permute-done | bytes 524320 | tf_op jit(solution)/shard_map/ppermute | solution.py:199
  114.0 1.1 shard_map.75
  (3 shorter events, 0.0 us)
Async XLA Ops:
  1.6 15.3 %collective-permute-start = (bf16[64,4224]{1,0:T(8,128)(2,1)S(1)}, bf16[64,4224]{1,0:T(8,128)(2,1)S(1)}, u32[]{:S(2)}, u32[]{:S(2)}) collective-permute-start(bf16[64,4224]{1,0:T(8,128)(2,1)S(1)} %shard_map.64.refs_0_), channel_id=1, source_target_pairs={{0,4},{1,5},{4,8},{5,9},{8,12},{9,13},{12,14},{13,15},{14,10},{15,... | collective-permute-start | bytes 1622024 | tf_op jit(solution)/shard_map/ppermute | solution.py:199
  4.7 14.0 %collective-permute-start.3 = (bf16[64,4224]{1,0:T(8,128)(2,1)S(1)}, bf16[64,4224]{1,0:T(8,128)(2,1)S(1)}, u32[]{:S(2)}, u32[]{:S(2)}) collective-permute-start(bf16[64,4224]{1,0:T(8,128)(2,1)S(1)} %shard_map.64.refs_0_), channel_id=1, source_target_pairs={{0,2},{1,3},{4,0},{5,1},{8,4},{9,5},{12,8},{13,9},{14,12},{15,13},... | collective-permute-start | bytes 1622024 | tf_op jit(solution)/shard_map/ppermute | solution.py:199
  16.9 13.5 %collective-permute-start.1 = (bf16[64,4224]{1,0:T(8,128)(2,1)S(1)}, bf16[64,4224]{1,0:T(8,128)(2,1)S(1)}, u32[]{:S(2)}, u32[]{:S(2)}) collective-permute-start(bf16[64,4224]{1,0:T(8,128)(2,1)S(1)} %collective-permute-done.refs_0_), channel_id=1, source_target_pairs={{0,4},{1,5},{4,8},{5,9},{8,12},{9,13},{12,14},{13,15},{14,10},{15,... | collective-permute-start | bytes 1622024 | tf_op jit(solution)/shard_map/ppermute | solution.py:199
  18.7 13.1 %collective-permute-start.4 = (bf16[64,4224]{1,0:T(8,128)(2,1)S(1)}, bf16[64,4224]{1,0:T(8,128)(2,1)}, u32[]{:S(2)}, u32[]{:S(2)}) collective-permute-start(bf16[64,4224]{1,0:T(8,128)(2,1)S(1)} %collective-permute-done.3.refs_1_), channel_id=1, source_target_pairs={{0,2},{1,3},{4,0},{5,1},{8,4},{9,5},{12,8},{13,9},{14,12},{15,13},... | collective-permute-start | bytes 1622024 | tf_op jit(solution)/shard_map/ppermute | solution.py:199
  30.4 12.6 %collective-permute-start.2 = (bf16[64,4224]{1,0:T(8,128)(2,1)S(1)}, bf16[64,4224]{1,0:T(8,128)(2,1)S(1)}, u32[]{:S(2)}, u32[]{:S(2)}) collective-permute-start(bf16[64,4224]{1,0:T(8,128)(2,1)S(1)} %collective-permute-done.1.refs_0_), channel_id=1, source_target_pairs={{0,4},{1,5},{4,8},{5,9},{8,12},{9,13},{12,14},{13,15},{14,10},{15,... | collective-permute-start | bytes 1622024 | tf_op jit(solution)/shard_map/ppermute | solution.py:199
  31.8 12.5 %collective-permute-start.5 = (bf16[64,4224]{1,0:T(8,128)(2,1)}, bf16[64,4224]{1,0:T(8,128)(2,1)S(1)}, u32[]{:S(2)}, u32[]{:S(2)}) collective-permute-start(bf16[64,4224]{1,0:T(8,128)(2,1)} %collective-permute-done.4.refs_1_), channel_id=1, source_target_pairs={{0,2},{1,3},{4,0},{5,1},{8,4},{9,5},{12,8},{13,9},{14,12},{15,13},... | collective-permute-start | bytes 1622024 | tf_op jit(solution)/shard_map/ppermute | solution.py:199
  44.4 9.4 %collective-permute-start.6 = (bf16[64,4224]{1,0:T(8,128)(2,1)S(1)}, bf16[64,4224]{1,0:T(8,128)(2,1)S(1)}, u32[]{:S(2)}, u32[]{:S(2)}) collective-permute-start(bf16[64,4224]{1,0:T(8,128)(2,1)S(1)} %broadcast_select_fusion), channel_id=1, source_target_pairs={{0,4},{1,3},{4,8},{5,1},{8,12},{9,5},{12,14},{13,9},{14,10},{15,13... | collective-permute-start | bytes 1622024 | tf_op jit(solution)/shard_map/ppermute | solution.py:199
  53.9 1.9 %collective-permute-start.7 = (bf16[64,4224]{1,0:T(8,128)(2,1)S(1)}, bf16[64,4224]{1,0:T(8,128)(2,1)S(1)}, u32[]{:S(2)}, u32[]{:S(2)}) collective-permute-start(bf16[64,4224]{1,0:T(8,128)(2,1)S(1)} %collective-permute-done.6.refs_0_), channel_id=1, source_target_pairs={{0,1},{1,0},{2,3},{3,2},{4,5},{5,4},{6,7},{7,6},{8,9},{9,8},{10,11... | collective-permute-start | bytes 1622024 | tf_op jit(solution)/shard_map/ppermute | solution.py:202
  53.9 4.8 %collective-permute-start.10 = (bf16[64,4224]{1,0:T(8,128)(2,1)S(1)}, bf16[64,4224]{1,0:T(8,128)(2,1)S(1)}, u32[]{:S(2)}, u32[]{:S(2)}) collective-permute-start(bf16[64,4224]{1,0:T(8,128)(2,1)S(1)} %collective-permute-done.2.refs_0_), channel_id=1, source_target_pairs={{0,1},{1,0},{2,3},{3,2},{4,5},{5,4},{6,7},{7,6},{8,9},{9,8},{10,11... | collective-permute-start | bytes 1622024 | tf_op jit(solution)/shard_map/ppermute | solution.py:202
  54.4 4.3 %collective-permute-start.11 = (bf16[64,4224]{1,0:T(8,128)(2,1)S(1)}, bf16[64,4224]{1,0:T(8,128)(2,1)S(1)}, u32[]{:S(2)}, u32[]{:S(2)}) collective-permute-start(bf16[64,4224]{1,0:T(8,128)(2,1)S(1)} %collective-permute-done.5.refs_1_), channel_id=1, source_target_pairs={{0,1},{1,0},{2,3},{3,2},{4,5},{5,4},{6,7},{7,6},{8,9},{9,8},{10,11... | collective-permute-start | bytes 1622024 | tf_op jit(solution)/shard_map/ppermute | solution.py:202
  54.4 10.6 %collective-permute-start.14 = (bf16[64,4224]{1,0:T(8,128)(2,1)S(1)}, bf16[64,4224]{1,0:T(8,128)(2,1)S(1)}, u32[]{:S(2)}, u32[]{:S(2)}) collective-permute-start(bf16[64,4224]{1,0:T(8,128)(2,1)S(1)} %collective-permute-done.1.refs_0_), channel_id=1, source_target_pairs={{0,1},{1,0},{2,3},{3,2},{4,5},{5,4},{6,7},{7,6},{8,9},{9,8},{10,11... | collective-permute-start | bytes 1622024 | tf_op jit(solution)/shard_map/ppermute | solution.py:202
  54.9 10.9 %collective-permute-start.15 = (bf16[64,4224]{1,0:T(8,128)(2,1)}, bf16[64,4224]{1,0:T(8,128)(2,1)S(1)}, u32[]{:S(2)}, u32[]{:S(2)}) collective-permute-start(bf16[64,4224]{1,0:T(8,128)(2,1)} %collective-permute-done.4.refs_1_), channel_id=1, source_target_pairs={{0,1},{1,0},{2,3},{3,2},{4,5},{5,4},{6,7},{7,6},{8,9},{9,8},{10,11... | collective-permute-start | bytes 1622024 | tf_op jit(solution)/shard_map/ppermute | solution.py:202
  58.5 5.9 %collective-permute-start.8 = (bf16[64,4096]{1,0:T(8,128)(2,1)S(1)}, bf16[64,4096]{1,0:T(8,128)(2,1)S(1)}, u32[]{:S(2)}, u32[]{:S(2)}) collective-permute-start(bf16[64,4096]{1,0:T(8,128)(2,1)S(1)} %get-tuple-element.45), channel_id=1, source_target_pairs={{0,1},{1,0},{2,3},{3,2},{4,5},{5,4},{6,7},{7,6},{8,9},{9,8},{10,11... | collective-permute-start | bytes 1572872 | tf_op jit(solution)/shard_map/ppermute | solution.py:202
  63.9 10.5 %collective-permute-start.12 = (bf16[128,4096]{1,0:T(8,128)(2,1)S(1)}, bf16[128,4096]{1,0:T(8,128)(2,1)S(1)}, u32[]{:S(2)}, u32[]{:S(2)}) collective-permute-start(bf16[128,4096]{1,0:T(8,128)(2,1)S(1)} %get-tuple-element.49), channel_id=1, source_target_pairs={{0,1},{1,0},{2,3},{3,2},{4,5},{5,4},{6,7},{7,6},{8,9},{9,8},{10,11... | collective-permute-start | bytes 3145736 | tf_op jit(solution)/shard_map/ppermute | solution.py:202
  64.3 12.5 %collective-permute-start.19 = (bf16[64,4224]{1,0:T(8,128)(2,1)S(1)}, bf16[64,4224]{1,0:T(8,128)(2,1)S(1)}, u32[]{:S(2)}, u32[]{:S(2)}) collective-permute-start(bf16[64,4224]{1,0:T(8,128)(2,1)S(1)} %collective-permute-done.refs_0_), channel_id=1, source_target_pairs={{0,1},{1,0},{2,3},{3,2},{4,5},{5,4},{6,7},{7,6},{8,9},{9,8},{10,11... | collective-permute-start | bytes 1622024 | tf_op jit(solution)/shard_map/ppermute | solution.py:202
  64.4 12.4 %collective-permute-start.20 = (bf16[64,4224]{1,0:T(8,128)(2,1)S(1)}, bf16[64,4224]{1,0:T(8,128)(2,1)S(1)}, u32[]{:S(2)}, u32[]{:S(2)}) collective-permute-start(bf16[64,4224]{1,0:T(8,128)(2,1)S(1)} %collective-permute-done.3.refs_1_), channel_id=1, source_target_pairs={{0,1},{1,0},{2,3},{3,2},{4,5},{5,4},{6,7},{7,6},{8,9},{9,8},{10,11... | collective-permute-start | bytes 1622024 | tf_op jit(solution)/shard_map/ppermute | solution.py:202
  65.0 9.4 %collective-permute-start.9 = (bf16[64,4096]{1,0:T(8,128)(2,1)S(1)}, bf16[64,4096]{1,0:T(8,128)(2,1)S(1)}, u32[]{:S(2)}, u32[]{:S(2)}) collective-permute-start(bf16[64,4096]{1,0:T(8,128)(2,1)S(1)} %shard_map.67), channel_id=1, source_target_pairs={{0,2},{1,5},{4,0},{5,9},{8,4},{9,13},{12,8},{13,15},{14,12},{15,11... | collective-permute-start | bytes 1572872 | tf_op jit(solution)/shard_map/ppermute | solution.py:199
  72.0 10.5 %collective-permute-start.16 = (bf16[128,4096]{1,0:T(8,128)(2,1)S(1)}, bf16[128,4096]{1,0:T(8,128)(2,1)S(1)}, u32[]{:S(2)}, u32[]{:S(2)}) collective-permute-start(bf16[128,4096]{1,0:T(8,128)(2,1)S(1)} %get-tuple-element.54), channel_id=1, source_target_pairs={{0,1},{1,0},{2,3},{3,2},{4,5},{5,4},{6,7},{7,6},{8,9},{9,8},{10,11... | collective-permute-start | bytes 3145736 | tf_op jit(solution)/shard_map/ppermute | solution.py:202
  74.7 13.1 %collective-permute-start.13 = (bf16[64,4096]{1,0:T(8,128)(2,1)S(1)}, bf16[64,4096]{1,0:T(8,128)(2,1)S(1)}, u32[]{:S(2)}, u32[]{:S(2)}) collective-permute-start(bf16[64,4096]{1,0:T(8,128)(2,1)S(1)} %get-tuple-element.50), channel_id=1, source_target_pairs={{0,2},{1,3},{4,0},{5,1},{8,4},{9,5},{12,8},{13,9},{14,12},{15,13},... | collective-permute-start | bytes 1572872 | tf_op jit(solution)/shard_map/ppermute | solution.py:199
  75.3 12.8 %collective-permute-start.17 = (bf16[64,4096]{1,0:T(8,128)(2,1)S(1)}, bf16[64,4096]{1,0:T(8,128)(2,1)S(1)}, u32[]{:S(2)}, u32[]{:S(2)}) collective-permute-start(bf16[64,4096]{1,0:T(8,128)(2,1)S(1)} %get-tuple-element.55), channel_id=1, source_target_pairs={{0,4},{1,5},{4,8},{5,9},{8,12},{9,13},{12,14},{13,15},{14,10},{15,... | collective-permute-start | bytes 1572872 | tf_op jit(solution)/shard_map/ppermute | solution.py:199
  81.9 11.5 %collective-permute-start.21 = (bf16[128,4096]{1,0:T(8,128)(2,1)S(1)}, bf16[128,4096]{1,0:T(8,128)(2,1)S(1)}, u32[]{:S(2)}, u32[]{:S(2)}) collective-permute-start(bf16[128,4096]{1,0:T(8,128)(2,1)S(1)} %get-tuple-element.60), channel_id=1, source_target_pairs={{0,1},{1,0},{2,3},{3,2},{4,5},{5,4},{6,7},{7,6},{8,9},{9,8},{10,11... | collective-permute-start | bytes 3145736 | tf_op jit(solution)/shard_map/ppermute | solution.py:202
  82.0 8.6 %collective-permute-start.25 = (bf16[64,4224]{1,0:T(8,128)(2,1)S(1)}, bf16[64,4224]{1,0:T(8,128)(2,1)S(1)}, u32[]{:S(2)}, u32[]{:S(2)}) collective-permute-start(bf16[64,4224]{1,0:T(8,128)(2,1)S(1)} %shard_map.64.refs_0_), channel_id=1, source_target_pairs={{0,1},{1,0},{2,3},{3,2},{4,5},{5,4},{6,7},{7,6},{8,9},{9,8},{10,11... | collective-permute-start | bytes 1622024 | tf_op jit(solution)/shard_map/ppermute | solution.py:202
  88.5 11.9 %collective-permute-start.18 = (bf16[64,4096]{1,0:T(8,128)(2,1)S(1)}, bf16[64,4096]{1,0:T(8,128)(2,1)S(1)}, u32[]{:S(2)}, u32[]{:S(2)}) collective-permute-start(bf16[64,4096]{1,0:T(8,128)(2,1)S(1)} %get-tuple-element.56), channel_id=1, source_target_pairs={{0,2},{1,3},{4,0},{5,1},{8,4},{9,5},{12,8},{13,9},{14,12},{15,13},... | collective-permute-start | bytes 1572872 | tf_op jit(solution)/shard_map/ppermute | solution.py:199
  90.0 11.6 %collective-permute-start.22 = (bf16[64,4096]{1,0:T(8,128)(2,1)S(1)}, bf16[64,4096]{1,0:T(8,128)(2,1)S(1)}, u32[]{:S(2)}, u32[]{:S(2)}) collective-permute-start(bf16[64,4096]{1,0:T(8,128)(2,1)S(1)} %get-tuple-element.61), channel_id=1, source_target_pairs={{0,4},{1,5},{4,8},{5,9},{8,12},{9,13},{12,14},{13,15},{14,10},{15,... | collective-permute-start | bytes 1572872 | tf_op jit(solution)/shard_map/ppermute | solution.py:199
  93.4 10.7 %collective-permute-start.26 = (bf16[64,4096]{1,0:T(8,128)(2,1)S(1)}, bf16[64,4096]{1,0:T(8,128)(2,1)S(1)}, u32[]{:S(2)}, u32[]{:S(2)}) collective-permute-start(bf16[64,4096]{1,0:T(8,128)(2,1)S(1)} %get-tuple-element.66), channel_id=1, source_target_pairs={{0,1},{1,0},{2,3},{3,2},{4,5},{5,4},{6,7},{7,6},{8,9},{9,8},{10,11... | collective-permute-start | bytes 1572872 | tf_op jit(solution)/shard_map/ppermute | solution.py:202
  101.9 10.7 %collective-permute-start.23 = (bf16[64,4096]{1,0:T(8,128)(2,1)S(1)}, bf16[64,4096]{1,0:T(8,128)(2,1)S(1)}, u32[]{:S(2)}, u32[]{:S(2)}) collective-permute-start(bf16[64,4096]{1,0:T(8,128)(2,1)S(1)} %get-tuple-element.62), channel_id=1, source_target_pairs={{0,2},{1,3},{4,0},{5,1},{8,4},{9,5},{12,8},{13,9},{14,12},{15,13},... | collective-permute-start | bytes 1572872 | tf_op jit(solution)/shard_map/ppermute | solution.py:199
  103.6 10.4 %collective-permute-start.24 = (bf16[64,4096]{1,0:T(8,128)(2,1)S(1)}, bf16[64,4096]{1,0:T(8,128)(2,1)S(1)}, u32[]{:S(2)}, u32[]{:S(2)}) collective-permute-start(bf16[64,4096]{1,0:T(8,128)(2,1)S(1)} %get-tuple-element.63), channel_id=1, source_target_pairs={{0,4},{1,5},{4,8},{5,9},{8,12},{9,13},{12,14},{13,15},{14,10},{15,... | collective-permute-start | bytes 1572872 | tf_op jit(solution)/shard_map/ppermute | solution.py:199

commit v4 on v3

--- a/solution.py
+++ b/solution.py
@@ -232,8 +232,8 @@
         return add_rows(core, first, second, (SUM_FLOPS, shape))
 
     pieces = range(BACK_PIECES)
-    run(far)
-    run(far - 1, sent[far][0])
+    run(far - 1)
+    run(far, sent[far - 1][1])
     edges = [hop(sums([part(i, far, 0)], [part(i, far, 0)])[0], -1, 1) for i in pieces]
     moving = [(None, None)] * BACK_PIECES
     for s in range(far - 1, 0, -1):

time: 115 us -> 111 us (0.965)
  waiting for transfers between devices: 63 us -> 59.1 us
    ppermute x14, waiting for transfers between devices: 62 us -> 55.9 us  [hop(): return lax.ppermute(value, 'node', pairs)]
    ppermute x13, waiting for transfers between devices: 0.94 us -> 3.2 us  [swap(): return lax.ppermute(value, 'node', [(i, i ^ 1) for i in range(nodes)])]
  transfers between devices with their start and end apart: 27 -> 27, of which waited for: 13 -> 16; matrix products, arithmetic and copies ran while one was open for 0% -> 0% of each run, Pallas kernels for 26% -> 27%
where the time goes in v4:
time: 111 us
  waiting for transfers between devices  59.1 us (53%)
  Pallas kernels  32.4 us (29%)
  starting transfers between devices  19.3 us (17%)
    ppermute x14, waiting for transfers between devices, hop(): return lax.ppermute(value, 'node', pairs)  55.9 us
    pallas_call x5, Pallas kernels, expert(): pl.pallas_call(functools.partial(expert_kernel, len(blocks)), in_specs=[p...  22 us
    ppermute x14, starting transfers between devices, hop(): return lax.ppermute(value, 'node', pairs)  16.1 us
    pallas_call x1, Pallas kernels, load(): pl.pallas_call(load_kernel, in_specs=[pl.BlockSpec(memory_space=pltpu.HBM...  6.52 us
    ppermute x13, waiting for transfers between devices, swap(): return lax.ppermute(value, 'node', [(i, i ^ 1) for i in range(nodes)])  3.2 us
    ppermute x13, starting transfers between devices, swap(): return lax.ppermute(value, 'node', [(i, i ^ 1) for i in range(nodes)])  3.2 us
    pallas_call x5, Pallas kernels, add_rows(): pl.pallas_call(functools.partial(add_kernel, *layout), in_specs=[pl.Block...  2.26 us
  transfers between devices with their start and end apart: 27, of which 16 were waited for; matrix products, arithmetic and copies ran while one was open for 0% of the time, Pallas kernels for 27%

profile of v4, /device:TPU:0, one launch (start us, length us, event | category | flops | bytes accessed | tf_op | source)
XLA Modules:
  0.0 110.9 jit_solution(12275810333694569998)
XLA Ops:
  0.0 1.6 %shard_map.64.refs_0_ = bf16[64,4224]{1,0:T(8,128)(2,1)S(1)} custom-call(bf16[64,4096]{1,0:T(8,128)(2,1)} %tokens_ref.1, s32[8,64]{1,0:T(8,128)} %bitcast.10, s32[8,64]{1,0:T(8,128)} %bitcast.11), custom_call_target="tpu_custom_call" | custom-call | tf_op jit(solution)/shard_map/pallas_call | solution.py:45
  1.6 3.1 %collective-permute-start = (bf16[64,4224]{1,0:T(8,128)(2,1)S(1)}, bf16[64,4224]{1,0:T(8,128)(2,1)S(1)}, u32[]{:S(2)}, u32[]{:S(2)}) collective-permute-start(bf16[64,4224]{1,0:T(8,128)(2,1)S(1)} %shard_map.64.refs_0_), channel_id=1, source_target_pairs={{0,4},{1,5},{4,8},{5,9},{8,12},{9,13},{12,14},{13,15},{14,10},{15,... | collective-permute-start | bytes 1622024 | tf_op jit(solution)/shard_map/ppermute | solution.py:199
  4.7 0.0 collective-permute-start.3
  4.7 12.2 %collective-permute-done.refs_0_ = bf16[64,4224]{1,0:T(8,128)(2,1)S(1)} collective-permute-done((bf16[64,4224]{1,0:T(8,128)(2,1)S(1)}, bf16[64,4224]{1,0:T(8,128)(2,1)S(1)}, u32[]{:S(2)}, u32[]{:S(2)}) %collective-permute-start) | collective-permute-done | bytes 540704 | tf_op jit(solution)/shard_map/ppermute | solution.py:199
  16.9 1.8 %collective-permute-start.1 = (bf16[64,4224]{1,0:T(8,128)(2,1)S(1)}, bf16[64,4224]{1,0:T(8,128)(2,1)S(1)}, u32[]{:S(2)}, u32[]{:S(2)}) collective-permute-start(bf16[64,4224]{1,0:T(8,128)(2,1)S(1)} %collective-permute-done.refs_0_), channel_id=1, source_target_pairs={{0,4},{1,5},{4,8},{5,9},{8,12},{9,13},{12,14},{13,15},{14,10},{15,... | collective-permute-start | bytes 1622024 | tf_op jit(solution)/shard_map/ppermute | solution.py:199
  18.7 0.0 collective-permute-done.3.refs_1_
  18.7 0.2 collective-permute-start.4
  18.9 11.4 %collective-permute-done.1.refs_0_ = bf16[64,4224]{1,0:T(8,128)(2,1)S(1)} collective-permute-done((bf16[64,4224]{1,0:T(8,128)(2,1)S(1)}, bf16[64,4224]{1,0:T(8,128)(2,1)S(1)}, u32[]{:S(2)}, u32[]{:S(2)}) %collective-permute-start.1) | collective-permute-done | bytes 540704 | tf_op jit(solution)/shard_map/ppermute | solution.py:199
  30.4 1.5 %collective-permute-start.2 = (bf16[64,4224]{1,0:T(8,128)(2,1)S(1)}, bf16[64,4224]{1,0:T(8,128)(2,1)S(1)}, u32[]{:S(2)}, u32[]{:S(2)}) collective-permute-start(bf16[64,4224]{1,0:T(8,128)(2,1)S(1)} %collective-permute-done.1.refs_0_), channel_id=1, source_target_pairs={{0,4},{1,5},{4,8},{5,9},{8,12},{9,13},{12,14},{13,15},{14,10},{15,... | collective-permute-start | bytes 1622024 | tf_op jit(solution)/shard_map/ppermute | solution.py:199
  31.8 0.5 collective-permute-start.5
  32.4 6.5 %shard_map.65 = (bf16[4096,768]{1,0:T(8,128)(2,1)S(1)}, bf16[4096,768]{1,0:T(8,128)(2,1)S(1)}, bf16[768,4096]{1,0:T(8,128)(2,1)S(1)}) custom-call(bf16[4096,768]{1,0:T(8,128)(2,1)} %bitcast.7, bf16[4096,768]{1,0:T(8,128)(2,1)} %bitcast.8, bf16[768,4096]{1,0:T(8,128)(2,1)} %bitcast.9), custom_call_target="tpu_custom_call" | custom-call | bytes 37748736 | tf_op jit(solution)/shard_map/pallas_call | solution.py:124
  38.9 4.1 %collective-permute-done.2.refs_0_ = bf16[64,4224]{1,0:T(8,128)(2,1)S(1)} collective-permute-done((bf16[64,4224]{1,0:T(8,128)(2,1)S(1)}, bf16[64,4224]{1,0:T(8,128)(2,1)S(1)}, u32[]{:S(2)}, u32[]{:S(2)}) %collective-permute-start.2) | collective-permute-done | bytes 540704 | tf_op jit(solution)/shard_map/ppermute | solution.py:199
  43.0 1.1 collective-permute-done.5.refs_1_
  44.1 0.5 collective-permute-start.8
  44.6 0.1 broadcast_select_fusion
  44.7 1.6 %collective-permute-start.6 = (bf16[64,4224]{1,0:T(8,128)(2,1)S(1)}, bf16[64,4224]{1,0:T(8,128)(2,1)S(1)}, u32[]{:S(2)}, u32[]{:S(2)}) collective-permute-start(bf16[64,4224]{1,0:T(8,128)(2,1)S(1)} %broadcast_select_fusion), channel_id=1, source_target_pairs={{0,4},{1,3},{4,8},{5,1},{8,12},{9,5},{12,14},{13,9},{14,10},{15,13... | collective-permute-start | bytes 1622024 | tf_op jit(solution)/shard_map/ppermute | solution.py:199
  46.3 0.0 collective-permute-done.7.refs_2_
  46.3 0.5 collective-permute-done.8.refs_3_
  46.8 5.1 %shard_map.66 = (bf16[128,4096]{1,0:T(8,128)(2,1)S(1)}, bf16[128,4096]{1,0:T(8,128)(2,1)S(1)}) custom-call(s32[1]{0:T(128)} %bitcast.1.me_ref, bf16[64,4224]{1,0:T(8,128)(2,1)S(1)} %collective-permute-done.2.refs_0_, bf16[64,4224]{1,0:T(8,128)(2,1)S(1)} %collective-permute-done.5.refs_1_, bf16[64,4224]{1,0:T(8,128)(2,1)S(1)} %collective-permute-done.7.refs_2_, ...), custom_call_target="tpu_custom_call" | custom-call | flops 4831838208 | bytes 4194304 | tf_op jit(solution)/shard_map/pallas_call | solution.py:91
  52.0 0.2 collective-permute-start.9
  52.2 1.9 %collective-permute-done.6.refs_0_ = bf16[64,4224]{1,0:T(8,128)(2,1)S(1)} collective-permute-done((bf16[64,4224]{1,0:T(8,128)(2,1)S(1)}, bf16[64,4224]{1,0:T(8,128)(2,1)S(1)}, u32[]{:S(2)}, u32[]{:S(2)}) %collective-permute-start.6) | collective-permute-done | bytes 540704 | tf_op jit(solution)/shard_map/ppermute | solution.py:199
  54.1 0.0 collective-permute-start.10
  54.1 0.5 collective-permute-start.14
  54.6 0.0 collective-permute-start.15
  54.6 0.1 collective-permute-done.9.refs_2_
  54.7 1.3 %collective-permute-done.10.refs_1_ = bf16[64,4224]{1,0:T(8,128)(2,1)S(1)} collective-permute-done((bf16[64,4224]{1,0:T(8,128)(2,1)S(1)}, bf16[64,4224]{1,0:T(8,128)(2,1)S(1)}, u32[]{:S(2)}, u32[]{:S(2)}) %collective-permute-start.10) | collective-permute-done | bytes 540704 | tf_op jit(solution)/shard_map/ppermute | solution.py:202
  56.0 2.7 %shard_map.67 = (bf16[64,4096]{1,0:T(8,128)(2,1)S(1)}, bf16[64,4096]{1,0:T(8,128)(2,1)S(1)}) custom-call(s32[1]{0:T(128)} %bitcast.1.me_ref, bf16[64,4224]{1,0:T(8,128)(2,1)S(1)} %collective-permute-done.6.refs_0_, bf16[64,4224]{1,0:T(8,128)(2,1)S(1)} %collective-permute-done.10.refs_1_, bf16[4096,768]{1,0:T(8,128)(2,1)S(1)} %get-tuple-element.40.refs_4_.refs_2_, ...), custom_call_target="tpu_custom_call" | custom-call | flops 2415919104 | bytes 2097152 | tf_op jit(solution)/shard_map/pallas_call | solution.py:91
  58.7 0.2 collective-permute-start.11
  58.9 0.4 collective-permute-start.19
  59.3 0.1 collective-permute-start.20
  59.4 1.3 %collective-permute-done.11.refs_1_ = bf16[64,4096]{1,0:T(8,128)(2,1)S(1)} collective-permute-done((bf16[64,4096]{1,0:T(8,128)(2,1)S(1)}, bf16[64,4096]{1,0:T(8,128)(2,1)S(1)}, u32[]{:S(2)}, u32[]{:S(2)}) %collective-permute-start.11) | collective-permute-done | bytes 524320 | tf_op jit(solution)/shard_map/ppermute | solution.py:202
  60.7 0.1 shard_map.68
  60.8 1.1 collective-permute-start.12
  61.9 0.0 collective-permute-done.14.refs_2_
  61.9 0.0 collective-permute-done.15.refs_3_
  61.9 6.2 %shard_map.70 = (bf16[128,4096]{1,0:T(8,128)(2,1)S(1)}, bf16[128,4096]{1,0:T(8,128)(2,1)S(1)}) custom-call(s32[1]{0:T(128)} %bitcast.1.me_ref, bf16[64,4224]{1,0:T(8,128)(2,1)S(1)} %collective-permute-done.1.refs_0_, bf16[64,4224]{1,0:T(8,128)(2,1)} %collective-permute-done.4.refs_1_, bf16[64,4224]{1,0:T(8,128)(2,1)S(1)} %collective-permute-done.14.refs_2_, ...), custom_call_target="tpu_custom_call" | custom-call | flops 4831838208 | bytes 4194304 | tf_op jit(solution)/shard_map/pallas_call | solution.py:91
  68.1 0.6 collective-permute-start.16
  68.8 1.5 %collective-permute-done.12.refs_0_ = bf16[64,4096]{1,0:T(8,128)(2,1)S(1)} collective-permute-done((bf16[64,4096]{1,0:T(8,128)(2,1)S(1)}, bf16[64,4096]{1,0:T(8,128)(2,1)S(1)}, u32[]{:S(2)}, u32[]{:S(2)}) %collective-permute-start.12) | collective-permute-done | bytes 524320 | tf_op jit(solution)/shard_map/ppermute | solution.py:199
  70.3 0.3 shard_map.69
  70.6 0.9 collective-permute-start.13
  71.5 1.2 %collective-permute-start.17 = (bf16[64,4096]{1,0:T(8,128)(2,1)S(1)}, bf16[64,4096]{1,0:T(8,128)(2,1)S(1)}, u32[]{:S(2)}, u32[]{:S(2)}) collective-permute-start(bf16[64,4096]{1,0:T(8,128)(2,1)S(1)} %get-tuple-element.57), channel_id=1, source_target_pairs={{0,4},{1,5},{4,8},{5,9},{8,12},{9,13},{12,14},{13,15},{14,10},{15,... | collective-permute-start | bytes 1572872 | tf_op jit(solution)/shard_map/ppermute | solution.py:199
  72.6 0.0 collective-permute-done.19.refs_2_
  72.7 0.0 collective-permute-done.20.refs_3_
  72.7 5.2 %shard_map.72 = (bf16[128,4096]{1,0:T(8,128)(2,1)S(1)}, bf16[128,4096]{1,0:T(8,128)(2,1)S(1)}) custom-call(s32[1]{0:T(128)} %bitcast.1.me_ref, bf16[64,4224]{1,0:T(8,128)(2,1)S(1)} %collective-permute-done.refs_0_, bf16[64,4224]{1,0:T(8,128)(2,1)S(1)} %collective-permute-done.3.refs_1_, bf16[64,4224]{1,0:T(8,128)(2,1)S(1)} %collective-permute-done.19.refs_2_, ...), custom_call_target="tpu_custom_call" | custom-call | flops 4831838208 | bytes 4194304 | tf_op jit(solution)/shard_map/pallas_call | solution.py:91
  77.8 0.1 collective-permute-start.21
  77.9 0.5 collective-permute-start.25
  78.4 0.0 collective-permute-done.16.refs_2_
  78.4 5.3 %collective-permute-done.13.refs_0_ = bf16[64,4096]{1,0:T(8,128)(2,1)S(1)} collective-permute-done((bf16[64,4096]{1,0:T(8,128)(2,1)S(1)}, bf16[64,4096]{1,0:T(8,128)(2,1)S(1)}, u32[]{:S(2)}, u32[]{:S(2)}) %collective-permute-start.13) | collective-permute-done | bytes 524320 | tf_op jit(solution)/shard_map/ppermute | solution.py:199
  83.7 0.6 collective-permute-done.17.refs_3_
  84.3 0.4 shard_map.71
  84.7 1.2 %collective-permute-start.18 = (bf16[64,4096]{1,0:T(8,128)(2,1)S(1)}, bf16[64,4096]{1,0:T(8,128)(2,1)S(1)}, u32[]{:S(2)}, u32[]{:S(2)}) collective-permute-start(bf16[64,4096]{1,0:T(8,128)(2,1)S(1)} %get-tuple-element.58), channel_id=1, source_target_pairs={{0,2},{1,3},{4,0},{5,1},{8,4},{9,5},{12,8},{13,9},{14,12},{15,13},... | collective-permute-start | bytes 1572872 | tf_op jit(solution)/shard_map/ppermute | solution.py:199
  85.8 0.9 collective-permute-start.22
  86.8 0.0 collective-permute-done.25.refs_1_
  86.8 2.8 %shard_map.74 = (bf16[64,4096]{1,0:T(8,128)(2,1)S(1)}, bf16[64,4096]{1,0:T(8,128)(2,1)S(1)}) custom-call(s32[1]{0:T(128)} %bitcast.1.me_ref, bf16[64,4224]{1,0:T(8,128)(2,1)S(1)} %shard_map.64.refs_0_, bf16[64,4224]{1,0:T(8,128)(2,1)S(1)} %collective-permute-done.25.refs_1_, bf16[4096,768]{1,0:T(8,128)(2,1)S(1)} %get-tuple-element.40.refs_4_.refs_2_, ...), custom_call_target="tpu_custom_call" | custom-call | flops 2415919104 | bytes 2097152 | tf_op jit(solution)/shard_map/pallas_call | solution.py:91
  89.6 0.1 collective-permute-start.26
  89.7 0.0 collective-permute-done.21.refs_2_
  89.7 7.0 %collective-permute-done.18.refs_0_ = bf16[64,4096]{1,0:T(8,128)(2,1)S(1)} collective-permute-done((bf16[64,4096]{1,0:T(8,128)(2,1)S(1)}, bf16[64,4096]{1,0:T(8,128)(2,1)S(1)}, u32[]{:S(2)}, u32[]{:S(2)}) %collective-permute-start.18) | collective-permute-done | bytes 524320 | tf_op jit(solution)/shard_map/ppermute | solution.py:199
  96.6 0.8 collective-permute-done.22.refs_3_
  97.5 0.4 shard_map.73
  97.9 1.6 %collective-permute-start.23 = (bf16[64,4096]{1,0:T(8,128)(2,1)S(1)}, bf16[64,4096]{1,0:T(8,128)(2,1)S(1)}, u32[]{:S(2)}, u32[]{:S(2)}) collective-permute-start(bf16[64,4096]{1,0:T(8,128)(2,1)S(1)} %get-tuple-element.64), channel_id=1, source_target_pairs={{0,2},{1,3},{4,0},{5,1},{8,4},{9,5},{12,8},{13,9},{14,12},{15,13},... | collective-permute-start | bytes 1572872 | tf_op jit(solution)/shard_map/ppermute | solution.py:199
  99.5 0.4 collective-permute-start.24
  99.9 8.6 %collective-permute-done.23.refs_0_ = bf16[64,4096]{1,0:T(8,128)(2,1)S(1)} collective-permute-done((bf16[64,4096]{1,0:T(8,128)(2,1)S(1)}, bf16[64,4096]{1,0:T(8,128)(2,1)S(1)}, u32[]{:S(2)}, u32[]{:S(2)}) %collective-permute-start.23) | collective-permute-done | bytes 524320 | tf_op jit(solution)/shard_map/ppermute | solution.py:199
  108.6 1.3 %collective-permute-done.24.refs_1_ = bf16[64,4096]{1,0:T(8,128)(2,1)S(1)} collective-permute-done((bf16[64,4096]{1,0:T(8,128)(2,1)S(1)}, bf16[64,4096]{1,0:T(8,128)(2,1)S(1)}, u32[]{:S(2)}, u32[]{:S(2)}) %collective-permute-start.24) | collective-permute-done | bytes 524320 | tf_op jit(solution)/shard_map/ppermute | solution.py:199
  109.9 1.1 shard_map.75
  (3 shorter events, 0.0 us)
Async XLA Ops:
  1.6 15.3 %collective-permute-start = (bf16[64,4224]{1,0:T(8,128)(2,1)S(1)}, bf16[64,4224]{1,0:T(8,128)(2,1)S(1)}, u32[]{:S(2)}, u32[]{:S(2)}) collective-permute-start(bf16[64,4224]{1,0:T(8,128)(2,1)S(1)} %shard_map.64.refs_0_), channel_id=1, source_target_pairs={{0,4},{1,5},{4,8},{5,9},{8,12},{9,13},{12,14},{13,15},{14,10},{15,... | collective-permute-start | bytes 1622024 | tf_op jit(solution)/shard_map/ppermute | solution.py:199
  4.7 14.0 %collective-permute-start.3 = (bf16[64,4224]{1,0:T(8,128)(2,1)S(1)}, bf16[64,4224]{1,0:T(8,128)(2,1)S(1)}, u32[]{:S(2)}, u32[]{:S(2)}) collective-permute-start(bf16[64,4224]{1,0:T(8,128)(2,1)S(1)} %shard_map.64.refs_0_), channel_id=1, source_target_pairs={{0,2},{1,3},{4,0},{5,1},{8,4},{9,5},{12,8},{13,9},{14,12},{15,13},... | collective-permute-start | bytes 1622024 | tf_op jit(solution)/shard_map/ppermute | solution.py:199
  16.9 13.5 %collective-permute-start.1 = (bf16[64,4224]{1,0:T(8,128)(2,1)S(1)}, bf16[64,4224]{1,0:T(8,128)(2,1)S(1)}, u32[]{:S(2)}, u32[]{:S(2)}) collective-permute-start(bf16[64,4224]{1,0:T(8,128)(2,1)S(1)} %collective-permute-done.refs_0_), channel_id=1, source_target_pairs={{0,4},{1,5},{4,8},{5,9},{8,12},{9,13},{12,14},{13,15},{14,10},{15,... | collective-permute-start | bytes 1622024 | tf_op jit(solution)/shard_map/ppermute | solution.py:199
  18.7 13.1 %collective-permute-start.4 = (bf16[64,4224]{1,0:T(8,128)(2,1)S(1)}, bf16[64,4224]{1,0:T(8,128)(2,1)}, u32[]{:S(2)}, u32[]{:S(2)}) collective-permute-start(bf16[64,4224]{1,0:T(8,128)(2,1)S(1)} %collective-permute-done.3.refs_1_), channel_id=1, source_target_pairs={{0,2},{1,3},{4,0},{5,1},{8,4},{9,5},{12,8},{13,9},{14,12},{15,13},... | collective-permute-start | bytes 1622024 | tf_op jit(solution)/shard_map/ppermute | solution.py:199
  30.4 12.6 %collective-permute-start.2 = (bf16[64,4224]{1,0:T(8,128)(2,1)S(1)}, bf16[64,4224]{1,0:T(8,128)(2,1)S(1)}, u32[]{:S(2)}, u32[]{:S(2)}) collective-permute-start(bf16[64,4224]{1,0:T(8,128)(2,1)S(1)} %collective-permute-done.1.refs_0_), channel_id=1, source_target_pairs={{0,4},{1,5},{4,8},{5,9},{8,12},{9,13},{12,14},{13,15},{14,10},{15,... | collective-permute-start | bytes 1622024 | tf_op jit(solution)/shard_map/ppermute | solution.py:199
  31.8 12.3 %collective-permute-start.5 = (bf16[64,4224]{1,0:T(8,128)(2,1)}, bf16[64,4224]{1,0:T(8,128)(2,1)S(1)}, u32[]{:S(2)}, u32[]{:S(2)}) collective-permute-start(bf16[64,4224]{1,0:T(8,128)(2,1)} %collective-permute-done.4.refs_1_), channel_id=1, source_target_pairs={{0,2},{1,3},{4,0},{5,1},{8,4},{9,5},{12,8},{13,9},{14,12},{15,13},... | collective-permute-start | bytes 1622024 | tf_op jit(solution)/shard_map/ppermute | solution.py:199
  44.1 2.2 %collective-permute-start.7 = (bf16[64,4224]{1,0:T(8,128)(2,1)S(1)}, bf16[64,4224]{1,0:T(8,128)(2,1)S(1)}, u32[]{:S(2)}, u32[]{:S(2)}) collective-permute-start(bf16[64,4224]{1,0:T(8,128)(2,1)S(1)} %collective-permute-done.2.refs_0_), channel_id=1, source_target_pairs={{0,1},{1,0},{2,3},{3,2},{4,5},{5,4},{6,7},{7,6},{8,9},{9,8},{10,11... | collective-permute-start | bytes 1622024 | tf_op jit(solution)/shard_map/ppermute | solution.py:202
  44.1 2.7 %collective-permute-start.8 = (bf16[64,4224]{1,0:T(8,128)(2,1)S(1)}, bf16[64,4224]{1,0:T(8,128)(2,1)S(1)}, u32[]{:S(2)}, u32[]{:S(2)}) collective-permute-start(bf16[64,4224]{1,0:T(8,128)(2,1)S(1)} %collective-permute-done.5.refs_1_), channel_id=1, source_target_pairs={{0,1},{1,0},{2,3},{3,2},{4,5},{5,4},{6,7},{7,6},{8,9},{9,8},{10,11... | collective-permute-start | bytes 1622024 | tf_op jit(solution)/shard_map/ppermute | solution.py:202
  44.7 9.4 %collective-permute-start.6 = (bf16[64,4224]{1,0:T(8,128)(2,1)S(1)}, bf16[64,4224]{1,0:T(8,128)(2,1)S(1)}, u32[]{:S(2)}, u32[]{:S(2)}) collective-permute-start(bf16[64,4224]{1,0:T(8,128)(2,1)S(1)} %broadcast_select_fusion), channel_id=1, source_target_pairs={{0,4},{1,3},{4,8},{5,1},{8,12},{9,5},{12,14},{13,9},{14,10},{15,13... | collective-permute-start | bytes 1622024 | tf_op jit(solution)/shard_map/ppermute | solution.py:199
  52.0 2.7 %collective-permute-start.9 = (bf16[128,4096]{1,0:T(8,128)(2,1)S(1)}, bf16[128,4096]{1,0:T(8,128)(2,1)S(1)}, u32[]{:S(2)}, u32[]{:S(2)}) collective-permute-start(bf16[128,4096]{1,0:T(8,128)(2,1)S(1)} %get-tuple-element.47), channel_id=1, source_target_pairs={{0,1},{1,0},{2,3},{3,2},{4,5},{5,4},{6,7},{7,6},{8,9},{9,8},{10,11... | collective-permute-start | bytes 3145736 | tf_op jit(solution)/shard_map/ppermute | solution.py:202
  54.1 1.9 %collective-permute-start.10 = (bf16[64,4224]{1,0:T(8,128)(2,1)S(1)}, bf16[64,4224]{1,0:T(8,128)(2,1)S(1)}, u32[]{:S(2)}, u32[]{:S(2)}) collective-permute-start(bf16[64,4224]{1,0:T(8,128)(2,1)S(1)} %collective-permute-done.6.refs_0_), channel_id=1, source_target_pairs={{0,1},{1,0},{2,3},{3,2},{4,5},{5,4},{6,7},{7,6},{8,9},{9,8},{10,11... | collective-permute-start | bytes 1622024 | tf_op jit(solution)/shard_map/ppermute | solution.py:202
  54.1 7.8 %collective-permute-start.14 = (bf16[64,4224]{1,0:T(8,128)(2,1)S(1)}, bf16[64,4224]{1,0:T(8,128)(2,1)S(1)}, u32[]{:S(2)}, u32[]{:S(2)}) collective-permute-start(bf16[64,4224]{1,0:T(8,128)(2,1)S(1)} %collective-permute-done.1.refs_0_), channel_id=1, source_target_pairs={{0,1},{1,0},{2,3},{3,2},{4,5},{5,4},{6,7},{7,6},{8,9},{9,8},{10,11... | collective-permute-start | bytes 1622024 | tf_op jit(solution)/shard_map/ppermute | solution.py:202
  54.6 7.3 %collective-permute-start.15 = (bf16[64,4224]{1,0:T(8,128)(2,1)}, bf16[64,4224]{1,0:T(8,128)(2,1)S(1)}, u32[]{:S(2)}, u32[]{:S(2)}) collective-permute-start(bf16[64,4224]{1,0:T(8,128)(2,1)} %collective-permute-done.4.refs_1_), channel_id=1, source_target_pairs={{0,1},{1,0},{2,3},{3,2},{4,5},{5,4},{6,7},{7,6},{8,9},{9,8},{10,11... | collective-permute-start | bytes 1622024 | tf_op jit(solution)/shard_map/ppermute | solution.py:202
  58.7 2.0 %collective-permute-start.11 = (bf16[64,4096]{1,0:T(8,128)(2,1)S(1)}, bf16[64,4096]{1,0:T(8,128)(2,1)S(1)}, u32[]{:S(2)}, u32[]{:S(2)}) collective-permute-start(bf16[64,4096]{1,0:T(8,128)(2,1)S(1)} %get-tuple-element.50), channel_id=1, source_target_pairs={{0,1},{1,0},{2,3},{3,2},{4,5},{5,4},{6,7},{7,6},{8,9},{9,8},{10,11... | collective-permute-start | bytes 1572872 | tf_op jit(solution)/shard_map/ppermute | solution.py:202
  58.9 13.7 %collective-permute-start.19 = (bf16[64,4224]{1,0:T(8,128)(2,1)S(1)}, bf16[64,4224]{1,0:T(8,128)(2,1)S(1)}, u32[]{:S(2)}, u32[]{:S(2)}) collective-permute-start(bf16[64,4224]{1,0:T(8,128)(2,1)S(1)} %collective-permute-done.refs_0_), channel_id=1, source_target_pairs={{0,1},{1,0},{2,3},{3,2},{4,5},{5,4},{6,7},{7,6},{8,9},{9,8},{10,11... | collective-permute-start | bytes 1622024 | tf_op jit(solution)/shard_map/ppermute | solution.py:202
  59.3 13.3 %collective-permute-start.20 = (bf16[64,4224]{1,0:T(8,128)(2,1)S(1)}, bf16[64,4224]{1,0:T(8,128)(2,1)S(1)}, u32[]{:S(2)}, u32[]{:S(2)}) collective-permute-start(bf16[64,4224]{1,0:T(8,128)(2,1)S(1)} %collective-permute-done.3.refs_1_), channel_id=1, source_target_pairs={{0,1},{1,0},{2,3},{3,2},{4,5},{5,4},{6,7},{7,6},{8,9},{9,8},{10,11... | collective-permute-start | bytes 1622024 | tf_op jit(solution)/shard_map/ppermute | solution.py:202
  60.8 9.4 %collective-permute-start.12 = (bf16[64,4096]{1,0:T(8,128)(2,1)S(1)}, bf16[64,4096]{1,0:T(8,128)(2,1)S(1)}, u32[]{:S(2)}, u32[]{:S(2)}) collective-permute-start(bf16[64,4096]{1,0:T(8,128)(2,1)S(1)} %shard_map.68), channel_id=1, source_target_pairs={{0,2},{1,5},{4,0},{5,9},{8,4},{9,13},{12,8},{13,15},{14,12},{15,11... | collective-permute-start | bytes 1572872 | tf_op jit(solution)/shard_map/ppermute | solution.py:199
  68.1 10.3 %collective-permute-start.16 = (bf16[128,4096]{1,0:T(8,128)(2,1)S(1)}, bf16[128,4096]{1,0:T(8,128)(2,1)S(1)}, u32[]{:S(2)}, u32[]{:S(2)}) collective-permute-start(bf16[128,4096]{1,0:T(8,128)(2,1)S(1)} %get-tuple-element.56), channel_id=1, source_target_pairs={{0,1},{1,0},{2,3},{3,2},{4,5},{5,4},{6,7},{7,6},{8,9},{9,8},{10,11... | collective-permute-start | bytes 3145736 | tf_op jit(solution)/shard_map/ppermute | solution.py:202
  70.6 13.2 %collective-permute-start.13 = (bf16[64,4096]{1,0:T(8,128)(2,1)S(1)}, bf16[64,4096]{1,0:T(8,128)(2,1)S(1)}, u32[]{:S(2)}, u32[]{:S(2)}) collective-permute-start(bf16[64,4096]{1,0:T(8,128)(2,1)S(1)} %get-tuple-element.52), channel_id=1, source_target_pairs={{0,2},{1,3},{4,0},{5,1},{8,4},{9,5},{12,8},{13,9},{14,12},{15,13},... | collective-permute-start | bytes 1572872 | tf_op jit(solution)/shard_map/ppermute | solution.py:199
  71.5 12.8 %collective-permute-start.17 = (bf16[64,4096]{1,0:T(8,128)(2,1)S(1)}, bf16[64,4096]{1,0:T(8,128)(2,1)S(1)}, u32[]{:S(2)}, u32[]{:S(2)}) collective-permute-start(bf16[64,4096]{1,0:T(8,128)(2,1)S(1)} %get-tuple-element.57), channel_id=1, source_target_pairs={{0,4},{1,5},{4,8},{5,9},{8,12},{9,13},{12,14},{13,15},{14,10},{15,... | collective-permute-start | bytes 1572872 | tf_op jit(solution)/shard_map/ppermute | solution.py:199
  77.8 11.8 %collective-permute-start.21 = (bf16[128,4096]{1,0:T(8,128)(2,1)S(1)}, bf16[128,4096]{1,0:T(8,128)(2,1)S(1)}, u32[]{:S(2)}, u32[]{:S(2)}) collective-permute-start(bf16[128,4096]{1,0:T(8,128)(2,1)S(1)} %get-tuple-element.62), channel_id=1, source_target_pairs={{0,1},{1,0},{2,3},{3,2},{4,5},{5,4},{6,7},{7,6},{8,9},{9,8},{10,11... | collective-permute-start | bytes 3145736 | tf_op jit(solution)/shard_map/ppermute | solution.py:202
  77.9 8.9 %collective-permute-start.25 = (bf16[64,4224]{1,0:T(8,128)(2,1)S(1)}, bf16[64,4224]{1,0:T(8,128)(2,1)S(1)}, u32[]{:S(2)}, u32[]{:S(2)}) collective-permute-start(bf16[64,4224]{1,0:T(8,128)(2,1)S(1)} %shard_map.64.refs_0_), channel_id=1, source_target_pairs={{0,1},{1,0},{2,3},{3,2},{4,5},{5,4},{6,7},{7,6},{8,9},{9,8},{10,11... | collective-permute-start | bytes 1622024 | tf_op jit(solution)/shard_map/ppermute | solution.py:202
  84.7 11.9 %collective-permute-start.18 = (bf16[64,4096]{1,0:T(8,128)(2,1)S(1)}, bf16[64,4096]{1,0:T(8,128)(2,1)S(1)}, u32[]{:S(2)}, u32[]{:S(2)}) collective-permute-start(bf16[64,4096]{1,0:T(8,128)(2,1)S(1)} %get-tuple-element.58), channel_id=1, source_target_pairs={{0,2},{1,3},{4,0},{5,1},{8,4},{9,5},{12,8},{13,9},{14,12},{15,13},... | collective-permute-start | bytes 1572872 | tf_op jit(solution)/shard_map/ppermute | solution.py:199
  85.8 11.6 %collective-permute-start.22 = (bf16[64,4096]{1,0:T(8,128)(2,1)S(1)}, bf16[64,4096]{1,0:T(8,128)(2,1)S(1)}, u32[]{:S(2)}, u32[]{:S(2)}) collective-permute-start(bf16[64,4096]{1,0:T(8,128)(2,1)S(1)} %get-tuple-element.63), channel_id=1, source_target_pairs={{0,4},{1,5},{4,8},{5,9},{8,12},{9,13},{12,14},{13,15},{14,10},{15,... | collective-permute-start | bytes 1572872 | tf_op jit(solution)/shard_map/ppermute | solution.py:199
  89.6 10.4 %collective-permute-start.26 = (bf16[64,4096]{1,0:T(8,128)(2,1)S(1)}, bf16[64,4096]{1,0:T(8,128)(2,1)S(1)}, u32[]{:S(2)}, u32[]{:S(2)}) collective-permute-start(bf16[64,4096]{1,0:T(8,128)(2,1)S(1)} %get-tuple-element.68), channel_id=1, source_target_pairs={{0,1},{1,0},{2,3},{3,2},{4,5},{5,4},{6,7},{7,6},{8,9},{9,8},{10,11... | collective-permute-start | bytes 1572872 | tf_op jit(solution)/shard_map/ppermute | solution.py:202
  97.9 10.7 %collective-permute-start.23 = (bf16[64,4096]{1,0:T(8,128)(2,1)S(1)}, bf16[64,4096]{1,0:T(8,128)(2,1)S(1)}, u32[]{:S(2)}, u32[]{:S(2)}) collective-permute-start(bf16[64,4096]{1,0:T(8,128)(2,1)S(1)} %get-tuple-element.64), channel_id=1, source_target_pairs={{0,2},{1,3},{4,0},{5,1},{8,4},{9,5},{12,8},{13,9},{14,12},{15,13},... | collective-permute-start | bytes 1572872 | tf_op jit(solution)/shard_map/ppermute | solution.py:199
  99.5 10.4 %collective-permute-start.24 = (bf16[64,4096]{1,0:T(8,128)(2,1)S(1)}, bf16[64,4096]{1,0:T(8,128)(2,1)S(1)}, u32[]{:S(2)}, u32[]{:S(2)}) collective-permute-start(bf16[64,4096]{1,0:T(8,128)(2,1)S(1)} %get-tuple-element.65), channel_id=1, source_target_pairs={{0,4},{1,5},{4,8},{5,9},{8,12},{9,13},{12,14},{13,15},{14,10},{15,... | collective-permute-start | bytes 1572872 | tf_op jit(solution)/shard_map/ppermute | solution.py:199

commit v5 on v4

--- a/solution.py
+++ b/solution.py
@@ -9,7 +9,7 @@
 
 LANES = 128
 FF_TILE = 256
-OUT_TILE = 512
+OUT_TILE = 1024
 MIB = 1 << 20
 LOADS = 4
 SUM_FLOPS = 0

time: 111 us -> 111 us (level)
  no operation moved by 1% of the time
where the time goes in v5:
time: 111 us
  waiting for transfers between devices  59.1 us (53%)
  Pallas kernels  32.4 us (29%)
  starting transfers between devices  19.3 us (17%)
    ppermute x14, waiting for transfers between devices, hop(): return lax.ppermute(value, 'node', pairs)  55.9 us
    pallas_call x5, Pallas kernels, expert(): pl.pallas_call(functools.partial(expert_kernel, len(blocks)), in_specs=[p...  22 us
    ppermute x14, starting transfers between devices, hop(): return lax.ppermute(value, 'node', pairs)  16.1 us
    pallas_call x1, Pallas kernels, load(): pl.pallas_call(load_kernel, in_specs=[pl.BlockSpec(memory_space=pltpu.HBM...  6.52 us
    ppermute x13, waiting for transfers between devices, swap(): return lax.ppermute(value, 'node', [(i, i ^ 1) for i in range(nodes)])  3.2 us
    ppermute x13, starting transfers between devices, swap(): return lax.ppermute(value, 'node', [(i, i ^ 1) for i in range(nodes)])  3.2 us
    pallas_call x5, Pallas kernels, add_rows(): pl.pallas_call(functools.partial(add_kernel, *layout), in_specs=[pl.Block...  2.26 us
  transfers between devices with their start and end apart: 27, of which 16 were waited for; matrix products, arithmetic and copies ran while one was open for 0% of the time, Pallas kernels for 27%

profile of v5, /device:TPU:0, one launch (start us, length us, event | category | flops | bytes accessed | tf_op | source)
XLA Modules:
  0.0 110.9 jit_solution(396852046501991802)
XLA Ops:
  0.0 1.6 %shard_map.64.refs_0_ = bf16[64,4224]{1,0:T(8,128)(2,1)S(1)} custom-call(bf16[64,4096]{1,0:T(8,128)(2,1)} %tokens_ref.1, s32[8,64]{1,0:T(8,128)} %bitcast.10, s32[8,64]{1,0:T(8,128)} %bitcast.11), custom_call_target="tpu_custom_call" | custom-call | tf_op jit(solution)/shard_map/pallas_call | solution.py:45
  1.6 3.1 %collective-permute-start = (bf16[64,4224]{1,0:T(8,128)(2,1)S(1)}, bf16[64,4224]{1,0:T(8,128)(2,1)S(1)}, u32[]{:S(2)}, u32[]{:S(2)}) collective-permute-start(bf16[64,4224]{1,0:T(8,128)(2,1)S(1)} %shard_map.64.refs_0_), channel_id=1, source_target_pairs={{0,4},{1,5},{4,8},{5,9},{8,12},{9,13},{12,14},{13,15},{14,10},{15,... | collective-permute-start | bytes 1622024 | tf_op jit(solution)/shard_map/ppermute | solution.py:199
  4.7 0.0 collective-permute-start.3
  4.7 12.2 %collective-permute-done.refs_0_ = bf16[64,4224]{1,0:T(8,128)(2,1)S(1)} collective-permute-done((bf16[64,4224]{1,0:T(8,128)(2,1)S(1)}, bf16[64,4224]{1,0:T(8,128)(2,1)S(1)}, u32[]{:S(2)}, u32[]{:S(2)}) %collective-permute-start) | collective-permute-done | bytes 540704 | tf_op jit(solution)/shard_map/ppermute | solution.py:199
  16.9 1.8 %collective-permute-start.1 = (bf16[64,4224]{1,0:T(8,128)(2,1)S(1)}, bf16[64,4224]{1,0:T(8,128)(2,1)S(1)}, u32[]{:S(2)}, u32[]{:S(2)}) collective-permute-start(bf16[64,4224]{1,0:T(8,128)(2,1)S(1)} %collective-permute-done.refs_0_), channel_id=1, source_target_pairs={{0,4},{1,5},{4,8},{5,9},{8,12},{9,13},{12,14},{13,15},{14,10},{15,... | collective-permute-start | bytes 1622024 | tf_op jit(solution)/shard_map/ppermute | solution.py:199
  18.7 0.0 collective-permute-done.3.refs_1_
  18.7 0.2 collective-permute-start.4
  18.9 11.4 %collective-permute-done.1.refs_0_ = bf16[64,4224]{1,0:T(8,128)(2,1)S(1)} collective-permute-done((bf16[64,4224]{1,0:T(8,128)(2,1)S(1)}, bf16[64,4224]{1,0:T(8,128)(2,1)S(1)}, u32[]{:S(2)}, u32[]{:S(2)}) %collective-permute-start.1) | collective-permute-done | bytes 540704 | tf_op jit(solution)/shard_map/ppermute | solution.py:199
  30.4 1.5 %collective-permute-start.2 = (bf16[64,4224]{1,0:T(8,128)(2,1)S(1)}, bf16[64,4224]{1,0:T(8,128)(2,1)S(1)}, u32[]{:S(2)}, u32[]{:S(2)}) collective-permute-start(bf16[64,4224]{1,0:T(8,128)(2,1)S(1)} %collective-permute-done.1.refs_0_), channel_id=1, source_target_pairs={{0,4},{1,5},{4,8},{5,9},{8,12},{9,13},{12,14},{13,15},{14,10},{15,... | collective-permute-start | bytes 1622024 | tf_op jit(solution)/shard_map/ppermute | solution.py:199
  31.8 0.5 collective-permute-start.5
  32.4 6.5 %shard_map.65 = (bf16[4096,768]{1,0:T(8,128)(2,1)S(1)}, bf16[4096,768]{1,0:T(8,128)(2,1)S(1)}, bf16[768,4096]{1,0:T(8,128)(2,1)S(1)}) custom-call(bf16[4096,768]{1,0:T(8,128)(2,1)} %bitcast.7, bf16[4096,768]{1,0:T(8,128)(2,1)} %bitcast.8, bf16[768,4096]{1,0:T(8,128)(2,1)} %bitcast.9), custom_call_target="tpu_custom_call" | custom-call | bytes 37748736 | tf_op jit(solution)/shard_map/pallas_call | solution.py:124
  38.9 4.1 %collective-permute-done.2.refs_0_ = bf16[64,4224]{1,0:T(8,128)(2,1)S(1)} collective-permute-done((bf16[64,4224]{1,0:T(8,128)(2,1)S(1)}, bf16[64,4224]{1,0:T(8,128)(2,1)S(1)}, u32[]{:S(2)}, u32[]{:S(2)}) %collective-permute-start.2) | collective-permute-done | bytes 540704 | tf_op jit(solution)/shard_map/ppermute | solution.py:199
  43.0 1.1 collective-permute-done.5.refs_1_
  44.1 0.5 collective-permute-start.8
  44.6 0.1 broadcast_select_fusion
  44.7 1.6 %collective-permute-start.6 = (bf16[64,4224]{1,0:T(8,128)(2,1)S(1)}, bf16[64,4224]{1,0:T(8,128)(2,1)S(1)}, u32[]{:S(2)}, u32[]{:S(2)}) collective-permute-start(bf16[64,4224]{1,0:T(8,128)(2,1)S(1)} %broadcast_select_fusion), channel_id=1, source_target_pairs={{0,4},{1,3},{4,8},{5,1},{8,12},{9,5},{12,14},{13,9},{14,10},{15,13... | collective-permute-start | bytes 1622024 | tf_op jit(solution)/shard_map/ppermute | solution.py:199
  46.3 0.0 collective-permute-done.7.refs_2_
  46.3 0.5 collective-permute-done.8.refs_3_
  46.8 5.1 %shard_map.66 = (bf16[128,4096]{1,0:T(8,128)(2,1)S(1)}, bf16[128,4096]{1,0:T(8,128)(2,1)S(1)}) custom-call(s32[1]{0:T(128)} %bitcast.1.me_ref, bf16[64,4224]{1,0:T(8,128)(2,1)S(1)} %collective-permute-done.2.refs_0_, bf16[64,4224]{1,0:T(8,128)(2,1)S(1)} %collective-permute-done.5.refs_1_, bf16[64,4224]{1,0:T(8,128)(2,1)S(1)} %collective-permute-done.7.refs_2_, ...), custom_call_target="tpu_custom_call" | custom-call | flops 4831838208 | bytes 4194304 | tf_op jit(solution)/shard_map/pallas_call | solution.py:91
  52.0 0.2 collective-permute-start.9
  52.2 1.9 %collective-permute-done.6.refs_0_ = bf16[64,4224]{1,0:T(8,128)(2,1)S(1)} collective-permute-done((bf16[64,4224]{1,0:T(8,128)(2,1)S(1)}, bf16[64,4224]{1,0:T(8,128)(2,1)S(1)}, u32[]{:S(2)}, u32[]{:S(2)}) %collective-permute-start.6) | collective-permute-done | bytes 540704 | tf_op jit(solution)/shard_map/ppermute | solution.py:199
  54.1 0.0 collective-permute-start.10
  54.1 0.5 collective-permute-start.14
  54.6 0.0 collective-permute-start.15
  54.6 0.1 collective-permute-done.9.refs_2_
  54.7 1.3 %collective-permute-done.10.refs_1_ = bf16[64,4224]{1,0:T(8,128)(2,1)S(1)} collective-permute-done((bf16[64,4224]{1,0:T(8,128)(2,1)S(1)}, bf16[64,4224]{1,0:T(8,128)(2,1)S(1)}, u32[]{:S(2)}, u32[]{:S(2)}) %collective-permute-start.10) | collective-permute-done | bytes 540704 | tf_op jit(solution)/shard_map/ppermute | solution.py:202
  56.0 2.7 %shard_map.67 = (bf16[64,4096]{1,0:T(8,128)(2,1)S(1)}, bf16[64,4096]{1,0:T(8,128)(2,1)S(1)}) custom-call(s32[1]{0:T(128)} %bitcast.1.me_ref, bf16[64,4224]{1,0:T(8,128)(2,1)S(1)} %collective-permute-done.6.refs_0_, bf16[64,4224]{1,0:T(8,128)(2,1)S(1)} %collective-permute-done.10.refs_1_, bf16[4096,768]{1,0:T(8,128)(2,1)S(1)} %get-tuple-element.40.refs_4_.refs_2_, ...), custom_call_target="tpu_custom_call" | custom-call | flops 2415919104 | bytes 2097152 | tf_op jit(solution)/shard_map/pallas_call | solution.py:91
  58.7 0.2 collective-permute-start.11
  58.9 0.4 collective-permute-start.19
  59.3 0.1 collective-permute-start.20
  59.4 1.3 %collective-permute-done.11.refs_1_ = bf16[64,4096]{1,0:T(8,128)(2,1)S(1)} collective-permute-done((bf16[64,4096]{1,0:T(8,128)(2,1)S(1)}, bf16[64,4096]{1,0:T(8,128)(2,1)S(1)}, u32[]{:S(2)}, u32[]{:S(2)}) %collective-permute-start.11) | collective-permute-done | bytes 524320 | tf_op jit(solution)/shard_map/ppermute | solution.py:202
  60.7 0.1 shard_map.68
  60.8 1.1 collective-permute-start.12
  61.9 0.0 collective-permute-done.14.refs_2_
  61.9 0.0 collective-permute-done.15.refs_3_
  61.9 6.2 %shard_map.70 = (bf16[128,4096]{1,0:T(8,128)(2,1)S(1)}, bf16[128,4096]{1,0:T(8,128)(2,1)S(1)}) custom-call(s32[1]{0:T(128)} %bitcast.1.me_ref, bf16[64,4224]{1,0:T(8,128)(2,1)S(1)} %collective-permute-done.1.refs_0_, bf16[64,4224]{1,0:T(8,128)(2,1)} %collective-permute-done.4.refs_1_, bf16[64,4224]{1,0:T(8,128)(2,1)S(1)} %collective-permute-done.14.refs_2_, ...), custom_call_target="tpu_custom_call" | custom-call | flops 4831838208 | bytes 4194304 | tf_op jit(solution)/shard_map/pallas_call | solution.py:91
  68.1 0.6 collective-permute-start.16
  68.8 1.5 %collective-permute-done.12.refs_0_ = bf16[64,4096]{1,0:T(8,128)(2,1)S(1)} collective-permute-done((bf16[64,4096]{1,0:T(8,128)(2,1)S(1)}, bf16[64,4096]{1,0:T(8,128)(2,1)S(1)}, u32[]{:S(2)}, u32[]{:S(2)}) %collective-permute-start.12) | collective-permute-done | bytes 524320 | tf_op jit(solution)/shard_map/ppermute | solution.py:199
  70.3 0.3 shard_map.69
  70.6 0.9 collective-permute-start.13
  71.5 1.2 %collective-permute-start.17 = (bf16[64,4096]{1,0:T(8,128)(2,1)S(1)}, bf16[64,4096]{1,0:T(8,128)(2,1)S(1)}, u32[]{:S(2)}, u32[]{:S(2)}) collective-permute-start(bf16[64,4096]{1,0:T(8,128)(2,1)S(1)} %get-tuple-element.57), channel_id=1, source_target_pairs={{0,4},{1,5},{4,8},{5,9},{8,12},{9,13},{12,14},{13,15},{14,10},{15,... | collective-permute-start | bytes 1572872 | tf_op jit(solution)/shard_map/ppermute | solution.py:199
  72.6 0.0 collective-permute-done.19.refs_2_
  72.7 0.0 collective-permute-done.20.refs_3_
  72.7 5.2 %shard_map.72 = (bf16[128,4096]{1,0:T(8,128)(2,1)S(1)}, bf16[128,4096]{1,0:T(8,128)(2,1)S(1)}) custom-call(s32[1]{0:T(128)} %bitcast.1.me_ref, bf16[64,4224]{1,0:T(8,128)(2,1)S(1)} %collective-permute-done.refs_0_, bf16[64,4224]{1,0:T(8,128)(2,1)S(1)} %collective-permute-done.3.refs_1_, bf16[64,4224]{1,0:T(8,128)(2,1)S(1)} %collective-permute-done.19.refs_2_, ...), custom_call_target="tpu_custom_call" | custom-call | flops 4831838208 | bytes 4194304 | tf_op jit(solution)/shard_map/pallas_call | solution.py:91
  77.8 0.1 collective-permute-start.21
  77.9 0.5 collective-permute-start.25
  78.4 0.0 collective-permute-done.16.refs_2_
  78.4 5.3 %collective-permute-done.13.refs_0_ = bf16[64,4096]{1,0:T(8,128)(2,1)S(1)} collective-permute-done((bf16[64,4096]{1,0:T(8,128)(2,1)S(1)}, bf16[64,4096]{1,0:T(8,128)(2,1)S(1)}, u32[]{:S(2)}, u32[]{:S(2)}) %collective-permute-start.13) | collective-permute-done | bytes 524320 | tf_op jit(solution)/shard_map/ppermute | solution.py:199
  83.7 0.6 collective-permute-done.17.refs_3_
  84.3 0.4 shard_map.71
  84.7 1.2 %collective-permute-start.18 = (bf16[64,4096]{1,0:T(8,128)(2,1)S(1)}, bf16[64,4096]{1,0:T(8,128)(2,1)S(1)}, u32[]{:S(2)}, u32[]{:S(2)}) collective-permute-start(bf16[64,4096]{1,0:T(8,128)(2,1)S(1)} %get-tuple-element.58), channel_id=1, source_target_pairs={{0,2},{1,3},{4,0},{5,1},{8,4},{9,5},{12,8},{13,9},{14,12},{15,13},... | collective-permute-start | bytes 1572872 | tf_op jit(solution)/shard_map/ppermute | solution.py:199
  85.8 0.9 collective-permute-start.22
  86.8 0.0 collective-permute-done.25.refs_1_
  86.8 2.8 %shard_map.74 = (bf16[64,4096]{1,0:T(8,128)(2,1)S(1)}, bf16[64,4096]{1,0:T(8,128)(2,1)S(1)}) custom-call(s32[1]{0:T(128)} %bitcast.1.me_ref, bf16[64,4224]{1,0:T(8,128)(2,1)S(1)} %shard_map.64.refs_0_, bf16[64,4224]{1,0:T(8,128)(2,1)S(1)} %collective-permute-done.25.refs_1_, bf16[4096,768]{1,0:T(8,128)(2,1)S(1)} %get-tuple-element.40.refs_4_.refs_2_, ...), custom_call_target="tpu_custom_call" | custom-call | flops 2415919104 | bytes 2097152 | tf_op jit(solution)/shard_map/pallas_call | solution.py:91
  89.6 0.1 collective-permute-start.26
  89.7 0.0 collective-permute-done.21.refs_2_
  89.7 7.0 %collective-permute-done.18.refs_0_ = bf16[64,4096]{1,0:T(8,128)(2,1)S(1)} collective-permute-done((bf16[64,4096]{1,0:T(8,128)(2,1)S(1)}, bf16[64,4096]{1,0:T(8,128)(2,1)S(1)}, u32[]{:S(2)}, u32[]{:S(2)}) %collective-permute-start.18) | collective-permute-done | bytes 524320 | tf_op jit(solution)/shard_map/ppermute | solution.py:199
  96.6 0.8 collective-permute-done.22.refs_3_
  97.5 0.4 shard_map.73
  97.9 1.6 %collective-permute-start.23 = (bf16[64,4096]{1,0:T(8,128)(2,1)S(1)}, bf16[64,4096]{1,0:T(8,128)(2,1)S(1)}, u32[]{:S(2)}, u32[]{:S(2)}) collective-permute-start(bf16[64,4096]{1,0:T(8,128)(2,1)S(1)} %get-tuple-element.64), channel_id=1, source_target_pairs={{0,2},{1,3},{4,0},{5,1},{8,4},{9,5},{12,8},{13,9},{14,12},{15,13},... | collective-permute-start | bytes 1572872 | tf_op jit(solution)/shard_map/ppermute | solution.py:199
  99.5 0.4 collective-permute-start.24
  99.9 8.6 %collective-permute-done.23.refs_0_ = bf16[64,4096]{1,0:T(8,128)(2,1)S(1)} collective-permute-done((bf16[64,4096]{1,0:T(8,128)(2,1)S(1)}, bf16[64,4096]{1,0:T(8,128)(2,1)S(1)}, u32[]{:S(2)}, u32[]{:S(2)}) %collective-permute-start.23) | collective-permute-done | bytes 524320 | tf_op jit(solution)/shard_map/ppermute | solution.py:199
  108.6 1.3 %collective-permute-done.24.refs_1_ = bf16[64,4096]{1,0:T(8,128)(2,1)S(1)} collective-permute-done((bf16[64,4096]{1,0:T(8,128)(2,1)S(1)}, bf16[64,4096]{1,0:T(8,128)(2,1)S(1)}, u32[]{:S(2)}, u32[]{:S(2)}) %collective-permute-start.24) | collective-permute-done | bytes 524320 | tf_op jit(solution)/shard_map/ppermute | solution.py:199
  109.9 1.1 shard_map.75
  (3 shorter events, 0.0 us)
Async XLA Ops:
  1.6 15.3 %collective-permute-start = (bf16[64,4224]{1,0:T(8,128)(2,1)S(1)}, bf16[64,4224]{1,0:T(8,128)(2,1)S(1)}, u32[]{:S(2)}, u32[]{:S(2)}) collective-permute-start(bf16[64,4224]{1,0:T(8,128)(2,1)S(1)} %shard_map.64.refs_0_), channel_id=1, source_target_pairs={{0,4},{1,5},{4,8},{5,9},{8,12},{9,13},{12,14},{13,15},{14,10},{15,... | collective-permute-start | bytes 1622024 | tf_op jit(solution)/shard_map/ppermute | solution.py:199
  4.7 14.0 %collective-permute-start.3 = (bf16[64,4224]{1,0:T(8,128)(2,1)S(1)}, bf16[64,4224]{1,0:T(8,128)(2,1)S(1)}, u32[]{:S(2)}, u32[]{:S(2)}) collective-permute-start(bf16[64,4224]{1,0:T(8,128)(2,1)S(1)} %shard_map.64.refs_0_), channel_id=1, source_target_pairs={{0,2},{1,3},{4,0},{5,1},{8,4},{9,5},{12,8},{13,9},{14,12},{15,13},... | collective-permute-start | bytes 1622024 | tf_op jit(solution)/shard_map/ppermute | solution.py:199
  16.9 13.5 %collective-permute-start.1 = (bf16[64,4224]{1,0:T(8,128)(2,1)S(1)}, bf16[64,4224]{1,0:T(8,128)(2,1)S(1)}, u32[]{:S(2)}, u32[]{:S(2)}) collective-permute-start(bf16[64,4224]{1,0:T(8,128)(2,1)S(1)} %collective-permute-done.refs_0_), channel_id=1, source_target_pairs={{0,4},{1,5},{4,8},{5,9},{8,12},{9,13},{12,14},{13,15},{14,10},{15,... | collective-permute-start | bytes 1622024 | tf_op jit(solution)/shard_map/ppermute | solution.py:199
  18.7 13.1 %collective-permute-start.4 = (bf16[64,4224]{1,0:T(8,128)(2,1)S(1)}, bf16[64,4224]{1,0:T(8,128)(2,1)}, u32[]{:S(2)}, u32[]{:S(2)}) collective-permute-start(bf16[64,4224]{1,0:T(8,128)(2,1)S(1)} %collective-permute-done.3.refs_1_), channel_id=1, source_target_pairs={{0,2},{1,3},{4,0},{5,1},{8,4},{9,5},{12,8},{13,9},{14,12},{15,13},... | collective-permute-start | bytes 1622024 | tf_op jit(solution)/shard_map/ppermute | solution.py:199
  30.4 12.6 %collective-permute-start.2 = (bf16[64,4224]{1,0:T(8,128)(2,1)S(1)}, bf16[64,4224]{1,0:T(8,128)(2,1)S(1)}, u32[]{:S(2)}, u32[]{:S(2)}) collective-permute-start(bf16[64,4224]{1,0:T(8,128)(2,1)S(1)} %collective-permute-done.1.refs_0_), channel_id=1, source_target_pairs={{0,4},{1,5},{4,8},{5,9},{8,12},{9,13},{12,14},{13,15},{14,10},{15,... | collective-permute-start | bytes 1622024 | tf_op jit(solution)/shard_map/ppermute | solution.py:199
  31.8 12.3 %collective-permute-start.5 = (bf16[64,4224]{1,0:T(8,128)(2,1)}, bf16[64,4224]{1,0:T(8,128)(2,1)S(1)}, u32[]{:S(2)}, u32[]{:S(2)}) collective-permute-start(bf16[64,4224]{1,0:T(8,128)(2,1)} %collective-permute-done.4.refs_1_), channel_id=1, source_target_pairs={{0,2},{1,3},{4,0},{5,1},{8,4},{9,5},{12,8},{13,9},{14,12},{15,13},... | collective-permute-start | bytes 1622024 | tf_op jit(solution)/shard_map/ppermute | solution.py:199
  44.1 2.2 %collective-permute-start.7 = (bf16[64,4224]{1,0:T(8,128)(2,1)S(1)}, bf16[64,4224]{1,0:T(8,128)(2,1)S(1)}, u32[]{:S(2)}, u32[]{:S(2)}) collective-permute-start(bf16[64,4224]{1,0:T(8,128)(2,1)S(1)} %collective-permute-done.2.refs_0_), channel_id=1, source_target_pairs={{0,1},{1,0},{2,3},{3,2},{4,5},{5,4},{6,7},{7,6},{8,9},{9,8},{10,11... | collective-permute-start | bytes 1622024 | tf_op jit(solution)/shard_map/ppermute | solution.py:202
  44.1 2.7 %collective-permute-start.8 = (bf16[64,4224]{1,0:T(8,128)(2,1)S(1)}, bf16[64,4224]{1,0:T(8,128)(2,1)S(1)}, u32[]{:S(2)}, u32[]{:S(2)}) collective-permute-start(bf16[64,4224]{1,0:T(8,128)(2,1)S(1)} %collective-permute-done.5.refs_1_), channel_id=1, source_target_pairs={{0,1},{1,0},{2,3},{3,2},{4,5},{5,4},{6,7},{7,6},{8,9},{9,8},{10,11... | collective-permute-start | bytes 1622024 | tf_op jit(solution)/shard_map/ppermute | solution.py:202
  44.7 9.4 %collective-permute-start.6 = (bf16[64,4224]{1,0:T(8,128)(2,1)S(1)}, bf16[64,4224]{1,0:T(8,128)(2,1)S(1)}, u32[]{:S(2)}, u32[]{:S(2)}) collective-permute-start(bf16[64,4224]{1,0:T(8,128)(2,1)S(1)} %broadcast_select_fusion), channel_id=1, source_target_pairs={{0,4},{1,3},{4,8},{5,1},{8,12},{9,5},{12,14},{13,9},{14,10},{15,13... | collective-permute-start | bytes 1622024 | tf_op jit(solution)/shard_map/ppermute | solution.py:199
  52.0 2.7 %collective-permute-start.9 = (bf16[128,4096]{1,0:T(8,128)(2,1)S(1)}, bf16[128,4096]{1,0:T(8,128)(2,1)S(1)}, u32[]{:S(2)}, u32[]{:S(2)}) collective-permute-start(bf16[128,4096]{1,0:T(8,128)(2,1)S(1)} %get-tuple-element.47), channel_id=1, source_target_pairs={{0,1},{1,0},{2,3},{3,2},{4,5},{5,4},{6,7},{7,6},{8,9},{9,8},{10,11... | collective-permute-start | bytes 3145736 | tf_op jit(solution)/shard_map/ppermute | solution.py:202
  54.1 1.9 %collective-permute-start.10 = (bf16[64,4224]{1,0:T(8,128)(2,1)S(1)}, bf16[64,4224]{1,0:T(8,128)(2,1)S(1)}, u32[]{:S(2)}, u32[]{:S(2)}) collective-permute-start(bf16[64,4224]{1,0:T(8,128)(2,1)S(1)} %collective-permute-done.6.refs_0_), channel_id=1, source_target_pairs={{0,1},{1,0},{2,3},{3,2},{4,5},{5,4},{6,7},{7,6},{8,9},{9,8},{10,11... | collective-permute-start | bytes 1622024 | tf_op jit(solution)/shard_map/ppermute | solution.py:202
  54.1 7.8 %collective-permute-start.14 = (bf16[64,4224]{1,0:T(8,128)(2,1)S(1)}, bf16[64,4224]{1,0:T(8,128)(2,1)S(1)}, u32[]{:S(2)}, u32[]{:S(2)}) collective-permute-start(bf16[64,4224]{1,0:T(8,128)(2,1)S(1)} %collective-permute-done.1.refs_0_), channel_id=1, source_target_pairs={{0,1},{1,0},{2,3},{3,2},{4,5},{5,4},{6,7},{7,6},{8,9},{9,8},{10,11... | collective-permute-start | bytes 1622024 | tf_op jit(solution)/shard_map/ppermute | solution.py:202
  54.6 7.3 %collective-permute-start.15 = (bf16[64,4224]{1,0:T(8,128)(2,1)}, bf16[64,4224]{1,0:T(8,128)(2,1)S(1)}, u32[]{:S(2)}, u32[]{:S(2)}) collective-permute-start(bf16[64,4224]{1,0:T(8,128)(2,1)} %collective-permute-done.4.refs_1_), channel_id=1, source_target_pairs={{0,1},{1,0},{2,3},{3,2},{4,5},{5,4},{6,7},{7,6},{8,9},{9,8},{10,11... | collective-permute-start | bytes 1622024 | tf_op jit(solution)/shard_map/ppermute | solution.py:202
  58.7 2.0 %collective-permute-start.11 = (bf16[64,4096]{1,0:T(8,128)(2,1)S(1)}, bf16[64,4096]{1,0:T(8,128)(2,1)S(1)}, u32[]{:S(2)}, u32[]{:S(2)}) collective-permute-start(bf16[64,4096]{1,0:T(8,128)(2,1)S(1)} %get-tuple-element.50), channel_id=1, source_target_pairs={{0,1},{1,0},{2,3},{3,2},{4,5},{5,4},{6,7},{7,6},{8,9},{9,8},{10,11... | collective-permute-start | bytes 1572872 | tf_op jit(solution)/shard_map/ppermute | solution.py:202
  58.9 13.7 %collective-permute-start.19 = (bf16[64,4224]{1,0:T(8,128)(2,1)S(1)}, bf16[64,4224]{1,0:T(8,128)(2,1)S(1)}, u32[]{:S(2)}, u32[]{:S(2)}) collective-permute-start(bf16[64,4224]{1,0:T(8,128)(2,1)S(1)} %collective-permute-done.refs_0_), channel_id=1, source_target_pairs={{0,1},{1,0},{2,3},{3,2},{4,5},{5,4},{6,7},{7,6},{8,9},{9,8},{10,11... | collective-permute-start | bytes 1622024 | tf_op jit(solution)/shard_map/ppermute | solution.py:202
  59.3 13.3 %collective-permute-start.20 = (bf16[64,4224]{1,0:T(8,128)(2,1)S(1)}, bf16[64,4224]{1,0:T(8,128)(2,1)S(1)}, u32[]{:S(2)}, u32[]{:S(2)}) collective-permute-start(bf16[64,4224]{1,0:T(8,128)(2,1)S(1)} %collective-permute-done.3.refs_1_), channel_id=1, source_target_pairs={{0,1},{1,0},{2,3},{3,2},{4,5},{5,4},{6,7},{7,6},{8,9},{9,8},{10,11... | collective-permute-start | bytes 1622024 | tf_op jit(solution)/shard_map/ppermute | solution.py:202
  60.8 9.4 %collective-permute-start.12 = (bf16[64,4096]{1,0:T(8,128)(2,1)S(1)}, bf16[64,4096]{1,0:T(8,128)(2,1)S(1)}, u32[]{:S(2)}, u32[]{:S(2)}) collective-permute-start(bf16[64,4096]{1,0:T(8,128)(2,1)S(1)} %shard_map.68), channel_id=1, source_target_pairs={{0,2},{1,5},{4,0},{5,9},{8,4},{9,13},{12,8},{13,15},{14,12},{15,11... | collective-permute-start | bytes 1572872 | tf_op jit(solution)/shard_map/ppermute | solution.py:199
  68.1 10.3 %collective-permute-start.16 = (bf16[128,4096]{1,0:T(8,128)(2,1)S(1)}, bf16[128,4096]{1,0:T(8,128)(2,1)S(1)}, u32[]{:S(2)}, u32[]{:S(2)}) collective-permute-start(bf16[128,4096]{1,0:T(8,128)(2,1)S(1)} %get-tuple-element.56), channel_id=1, source_target_pairs={{0,1},{1,0},{2,3},{3,2},{4,5},{5,4},{6,7},{7,6},{8,9},{9,8},{10,11... | collective-permute-start | bytes 3145736 | tf_op jit(solution)/shard_map/ppermute | solution.py:202
  70.6 13.2 %collective-permute-start.13 = (bf16[64,4096]{1,0:T(8,128)(2,1)S(1)}, bf16[64,4096]{1,0:T(8,128)(2,1)S(1)}, u32[]{:S(2)}, u32[]{:S(2)}) collective-permute-start(bf16[64,4096]{1,0:T(8,128)(2,1)S(1)} %get-tuple-element.52), channel_id=1, source_target_pairs={{0,2},{1,3},{4,0},{5,1},{8,4},{9,5},{12,8},{13,9},{14,12},{15,13},... | collective-permute-start | bytes 1572872 | tf_op jit(solution)/shard_map/ppermute | solution.py:199
  71.5 12.8 %collective-permute-start.17 = (bf16[64,4096]{1,0:T(8,128)(2,1)S(1)}, bf16[64,4096]{1,0:T(8,128)(2,1)S(1)}, u32[]{:S(2)}, u32[]{:S(2)}) collective-permute-start(bf16[64,4096]{1,0:T(8,128)(2,1)S(1)} %get-tuple-element.57), channel_id=1, source_target_pairs={{0,4},{1,5},{4,8},{5,9},{8,12},{9,13},{12,14},{13,15},{14,10},{15,... | collective-permute-start | bytes 1572872 | tf_op jit(solution)/shard_map/ppermute | solution.py:199
  77.8 11.8 %collective-permute-start.21 = (bf16[128,4096]{1,0:T(8,128)(2,1)S(1)}, bf16[128,4096]{1,0:T(8,128)(2,1)S(1)}, u32[]{:S(2)}, u32[]{:S(2)}) collective-permute-start(bf16[128,4096]{1,0:T(8,128)(2,1)S(1)} %get-tuple-element.62), channel_id=1, source_target_pairs={{0,1},{1,0},{2,3},{3,2},{4,5},{5,4},{6,7},{7,6},{8,9},{9,8},{10,11... | collective-permute-start | bytes 3145736 | tf_op jit(solution)/shard_map/ppermute | solution.py:202
  77.9 8.9 %collective-permute-start.25 = (bf16[64,4224]{1,0:T(8,128)(2,1)S(1)}, bf16[64,4224]{1,0:T(8,128)(2,1)S(1)}, u32[]{:S(2)}, u32[]{:S(2)}) collective-permute-start(bf16[64,4224]{1,0:T(8,128)(2,1)S(1)} %shard_map.64.refs_0_), channel_id=1, source_target_pairs={{0,1},{1,0},{2,3},{3,2},{4,5},{5,4},{6,7},{7,6},{8,9},{9,8},{10,11... | collective-permute-start | bytes 1622024 | tf_op jit(solution)/shard_map/ppermute | solution.py:202
  84.7 11.9 %collective-permute-start.18 = (bf16[64,4096]{1,0:T(8,128)(2,1)S(1)}, bf16[64,4096]{1,0:T(8,128)(2,1)S(1)}, u32[]{:S(2)}, u32[]{:S(2)}) collective-permute-start(bf16[64,4096]{1,0:T(8,128)(2,1)S(1)} %get-tuple-element.58), channel_id=1, source_target_pairs={{0,2},{1,3},{4,0},{5,1},{8,4},{9,5},{12,8},{13,9},{14,12},{15,13},... | collective-permute-start | bytes 1572872 | tf_op jit(solution)/shard_map/ppermute | solution.py:199
  85.8 11.6 %collective-permute-start.22 = (bf16[64,4096]{1,0:T(8,128)(2,1)S(1)}, bf16[64,4096]{1,0:T(8,128)(2,1)S(1)}, u32[]{:S(2)}, u32[]{:S(2)}) collective-permute-start(bf16[64,4096]{1,0:T(8,128)(2,1)S(1)} %get-tuple-element.63), channel_id=1, source_target_pairs={{0,4},{1,5},{4,8},{5,9},{8,12},{9,13},{12,14},{13,15},{14,10},{15,... | collective-permute-start | bytes 1572872 | tf_op jit(solution)/shard_map/ppermute | solution.py:199
  89.6 10.4 %collective-permute-start.26 = (bf16[64,4096]{1,0:T(8,128)(2,1)S(1)}, bf16[64,4096]{1,0:T(8,128)(2,1)S(1)}, u32[]{:S(2)}, u32[]{:S(2)}) collective-permute-start(bf16[64,4096]{1,0:T(8,128)(2,1)S(1)} %get-tuple-element.68), channel_id=1, source_target_pairs={{0,1},{1,0},{2,3},{3,2},{4,5},{5,4},{6,7},{7,6},{8,9},{9,8},{10,11... | collective-permute-start | bytes 1572872 | tf_op jit(solution)/shard_map/ppermute | solution.py:202
  97.9 10.7 %collective-permute-start.23 = (bf16[64,4096]{1,0:T(8,128)(2,1)S(1)}, bf16[64,4096]{1,0:T(8,128)(2,1)S(1)}, u32[]{:S(2)}, u32[]{:S(2)}) collective-permute-start(bf16[64,4096]{1,0:T(8,128)(2,1)S(1)} %get-tuple-element.64), channel_id=1, source_target_pairs={{0,2},{1,3},{4,0},{5,1},{8,4},{9,5},{12,8},{13,9},{14,12},{15,13},... | collective-permute-start | bytes 1572872 | tf_op jit(solution)/shard_map/ppermute | solution.py:199
  99.5 10.4 %collective-permute-start.24 = (bf16[64,4096]{1,0:T(8,128)(2,1)S(1)}, bf16[64,4096]{1,0:T(8,128)(2,1)S(1)}, u32[]{:S(2)}, u32[]{:S(2)}) collective-permute-start(bf16[64,4096]{1,0:T(8,128)(2,1)S(1)} %get-tuple-element.65), channel_id=1, source_target_pairs={{0,4},{1,5},{4,8},{5,9},{8,12},{9,13},{12,14},{13,15},{14,10},{15,... | collective-permute-start | bytes 1572872 | tf_op jit(solution)/shard_map/ppermute | solution.py:199
